TPU v7x, 32 devices: a whole 2x2x4 slice. The times are simulated.
32 devices in a mesh: groups: 2 (over y), expert: 4 (over z), dp: 2 (over x), inner: 2 (over core).
Axes of the slice: x: 2, y: 2, z: 4, core: 2. Of those that a mesh axis runs over, the one named last changes fastest.
Arguments:
- tokens: bfloat16 [2048, 2048], P(('groups', 'expert', 'inner'), 'dp'), parts along dimension 0, may hold values from -6 to 6
- out_grad: bfloat16 [2048, 2048], P(('groups', 'expert', 'inner'), 'dp'), parts along dimension 0, may hold values from -2.5 to 2.5
- expert_ids: int32 [2048, 2], P(('groups', 'expert', 'inner')), parts along dimension 0, may hold values from 0 to 7, all different within a row; in each aligned block of 128 rows (0 to 127, 128 to 255, ...) at most 48 rows name the same one
- gate_weights: float32 [2048, 2], P(('groups', 'expert', 'inner')), parts along dimension 0, may hold values from 0.2 to 1
- shadow_expert: int32 [4], replicated, may hold values from 0 to 7, as said below
- w_gate: bfloat16 [8, 2048, 1024], P('expert', 'dp', 'inner'), may hold values from -0.125 to 0.125
- w_up: bfloat16 [8, 2048, 1024], P('expert', 'dp', 'inner'), may hold values from -0.125 to 0.125
- w_down: bfloat16 [8, 1024, 2048], P('expert', 'inner', 'dp'), may hold values from -0.1875 to 0.1875
- copy_gate: bfloat16 [4, 2048, 1024], P('expert', 'dp', 'inner'), may hold values from -0.125 to 0.125
- copy_up: bfloat16 [4, 2048, 1024], P('expert', 'dp', 'inner'), may hold values from -0.125 to 0.125
- copy_down: bfloat16 [4, 1024, 2048], P('expert', 'inner', 'dp'), may hold values from -0.1875 to 0.1875
Outputs:
- grad_tokens: bfloat16 [2048, 2048], P(('groups', 'expert', 'inner'), 'dp'), parts along dimension 0
- grad_w_gate: bfloat16 [16, 2048, 1024], P(('groups', 'expert'), 'dp', 'inner'), parts along dimension 0
- grad_w_up: bfloat16 [16, 2048, 1024], P(('groups', 'expert'), 'dp', 'inner'), parts along dimension 0
- grad_w_down: bfloat16 [16, 1024, 2048], P(('groups', 'expert'), 'inner', 'dp'), parts along dimension 0
There are 2 independent parts, one for each index of `groups`. A program takes and returns all parts, laid end to end along the dimension named above; an argument that names none is the same for every part. Nothing has to cross between parts.
Inputs may be any that keep to these rules, and one draw needn't show every extreme that they name: `expert_ids`: A token's two experts differ; among the 128 tokens of one index of expert+inner no expert is named more than 48 times, a bound that some block reaches. Experts 2 j and 2 j + 1 are owned by index j of expert. `shadow_expert`: entry j names an expert that index j does not own. Exactly half of the indices of expert own the experts of two entries each, the other indices those of none; the two entries that fall on one index may name the same expert or its two experts.
All inputs are finite; a program needn't handle non-finite values.
Results may differ from a plain program's by a relative error of at most 0.02.
Values may be sent and summed in bfloat16 or wider, within the bound.
No kernel may reach another device: no remote copies, remote signals or barrier semaphores. Data moves between devices by JAX's collectives and lax.ppermute only.
A program may use at most 128 MiB of HBM per device.

v0:
```python
import jax
import jax.numpy as jnp
from jax import lax
from jax.sharding import PartitionSpec as P


def serving_copy(expert_ids, shadow_expert, first_token):
    tok_rows = expert_ids.shape[0]
    shadow_count = shadow_expert.shape[0]
    token_index = first_token + jnp.arange(tok_rows, dtype=jnp.int32)
    position = token_index[:, None] + jnp.arange(2, dtype=jnp.int32)[None, :]
    matches = (expert_ids[:, :, None] == shadow_expert[None, None, :]).astype(jnp.int32)
    copies = 1 + jnp.sum(matches, axis=2)
    chosen = position % copies
    slot_order = jnp.arange(shadow_count, dtype=jnp.int32)
    lower_slot = (slot_order[:, None] > slot_order[None, :]).astype(jnp.int32)
    same_expert = (shadow_expert[:, None] == shadow_expert[None, :]).astype(jnp.int32)
    rank_among = jnp.sum(lower_slot * same_expert, axis=1)
    picked = matches * (rank_among[None, None, :] == chosen[:, :, None] - 1).astype(jnp.int32)
    holder = jnp.sum(picked * slot_order[None, None, :], axis=2)
    shadowed = jnp.sum(picked, axis=2)
    return jnp.where(shadowed > 0, 2 * shadow_count + holder, expert_ids)


def activation(block_sums):
    width_half = block_sums.shape[-1] // 3
    pre_gate = block_sums[..., :width_half]
    pre_up = block_sums[..., width_half : 2 * width_half]
    hidden_grad = block_sums[..., 2 * width_half :]
    sigmoid_gate = jax.nn.sigmoid(pre_gate)
    swish_gate = pre_gate * sigmoid_gate
    grad_up = (hidden_grad * swish_gate).astype(jnp.bfloat16)
    grad_gate = (
        hidden_grad * pre_up * sigmoid_gate * (1.0 + pre_gate * (1.0 - sigmoid_gate))
    ).astype(jnp.bfloat16)
    hidden = (swish_gate * pre_up).astype(jnp.bfloat16)
    return (grad_gate, grad_up, hidden)


def on_device(
    tokens,
    out_grad,
    expert_ids,
    gate_weights,
    shadow_expert,
    w_gate,
    w_up,
    w_down,
    copy_gate,
    copy_up,
    copy_down,
):
    tok_rows, feature_piece = tokens.shape
    hidden_piece = w_gate.shape[2]
    expert_count = lax.axis_size("expert")
    inner_count = lax.axis_size("inner")
    capacity = max(2, 3 * tok_rows // (2 * expert_count))
    owned_total = 2 * expert_count
    block_number = lax.axis_index("expert") * inner_count + lax.axis_index("inner")
    copy_ids = serving_copy(expert_ids, shadow_expert, block_number * tok_rows)
    flat_ids = copy_ids.reshape(-1)
    holder_index = jnp.where(flat_ids < owned_total, flat_ids // 2, flat_ids - owned_total)
    slot_kind = jnp.where(flat_ids < owned_total, flat_ids % 2, 2)
    copy_onehot = (
        flat_ids[:, None] == jnp.arange(3 * expert_count, dtype=jnp.int32)[None, :]
    ).astype(jnp.int32)
    route_rank = jnp.sum((jnp.cumsum(copy_onehot, axis=0) - 1) * copy_onehot, axis=1)
    slot_place = ((slot_kind * expert_count + holder_index) * capacity + route_rank).reshape(
        tok_rows, 2
    )
    send_slots = 3 * expert_count * capacity
    slot_range = jnp.arange(send_slots, dtype=jnp.int32)
    route_hit = (slot_range[:, None, None] == slot_place[None, :, :]).astype(jnp.float32)
    place_matrix = jnp.sum(route_hit, axis=2)
    gate_matrix = jnp.sum(route_hit * gate_weights[None, :, :], axis=2)
    rows_in = jnp.dot(
        place_matrix.astype(jnp.bfloat16), tokens, preferred_element_type=jnp.float32
    ).astype(jnp.bfloat16)
    rows_grad = jnp.dot(
        gate_matrix, out_grad.astype(jnp.float32), precision=lax.Precision.HIGHEST
    ).astype(jnp.bfloat16)

    def duplicate(values):
        shaped = values.reshape(3, expert_count, 1, capacity, feature_piece)
        widened = jnp.broadcast_to(shaped, (3, expert_count, inner_count, capacity, feature_piece))
        return widened.reshape(3, expert_count * inner_count, capacity, feature_piece)

    recv_in, recv_grad = (
        lax.all_to_all(
            duplicate(rows_in), ("expert", "inner"), split_axis=1, concat_axis=1, tiled=True
        ),
        lax.all_to_all(
            duplicate(rows_grad), ("expert", "inner"), split_axis=1, concat_axis=1, tiled=True
        ),
    )
    host_rows = expert_count * inner_count * capacity
    inputs = recv_in.reshape(3, host_rows, feature_piece)
    grad_rows = recv_grad.reshape(3, host_rows, feature_piece)
    weight_gate = jnp.concatenate([w_gate, copy_gate], axis=0)
    weight_up = jnp.concatenate([w_up, copy_up], axis=0)
    weight_down = jnp.concatenate([w_down, copy_down], axis=0)
    partial_sums = jnp.concatenate(
        [
            jnp.einsum("srf,sfh->srh", inputs, weight_gate, preferred_element_type=jnp.float32),
            jnp.einsum("srf,sfh->srh", inputs, weight_up, preferred_element_type=jnp.float32),
            jnp.einsum("srf,shf->srh", grad_rows, weight_down, preferred_element_type=jnp.float32),
        ],
        axis=2,
    )
    block_sums = lax.psum(partial_sums.astype(jnp.bfloat16), "dp").astype(jnp.float32)
    grad_gate, grad_up, hidden = activation(block_sums)
    route_part = jnp.einsum(
        "srh,sfh->srf", grad_gate, weight_gate, preferred_element_type=jnp.float32
    )
    route_part = route_part + jnp.einsum(
        "srh,sfh->srf", grad_up, weight_up, preferred_element_type=jnp.float32
    )
    returned = lax.all_to_all(
        route_part.reshape(3, expert_count * inner_count, capacity, feature_piece).astype(
            jnp.bfloat16
        ),
        ("expert", "inner"),
        split_axis=1,
        concat_axis=1,
        tiled=True,
    ).astype(jnp.float32)
    returned = jnp.sum(
        returned.reshape(3, expert_count, inner_count, capacity, feature_piece), axis=2
    ).reshape(send_slots, feature_piece)
    grad_tokens = jnp.dot(place_matrix.T, returned, precision=lax.Precision.HIGHEST).astype(
        jnp.bfloat16
    )
    dw_gate = jnp.einsum("srf,srh->sfh", inputs, grad_gate, preferred_element_type=jnp.float32)
    dw_up = jnp.einsum("srf,srh->sfh", inputs, grad_up, preferred_element_type=jnp.float32)
    dw_down = jnp.einsum("srh,srf->shf", hidden, grad_rows, preferred_element_type=jnp.float32)
    shadow_panel = jnp.concatenate(
        [
            dw_gate[2].astype(jnp.bfloat16).reshape(expert_count, -1),
            dw_up[2].astype(jnp.bfloat16).reshape(expert_count, -1),
            dw_down[2].astype(jnp.bfloat16).reshape(expert_count, -1),
        ],
        axis=1,
    )
    spread_pieces = lax.all_to_all(shadow_panel, "expert", split_axis=0, concat_axis=0, tiled=True)
    piece_width = spread_pieces.shape[1]
    indicator = (
        shadow_expert[:, None] == jnp.arange(owned_total, dtype=jnp.int32)[None, :]
    ).astype(jnp.float32)
    per_expert = jnp.dot(
        indicator.T, spread_pieces.astype(jnp.float32), precision=lax.Precision.HIGHEST
    )
    collected = lax.all_to_all(
        per_expert.reshape(expert_count, 2, piece_width).astype(jnp.bfloat16),
        "expert",
        split_axis=0,
        concat_axis=0,
        tiled=True,
    ).astype(jnp.float32)
    collected = jnp.transpose(collected, (1, 0, 2))
    third = piece_width // 3
    gate_extra = collected[:, :, :third].reshape(2, feature_piece, hidden_piece)
    up_extra = collected[:, :, third : 2 * third].reshape(2, feature_piece, hidden_piece)
    down_extra = collected[:, :, 2 * third :].reshape(2, hidden_piece, feature_piece)
    grad_w_gate = (dw_gate[:2] + gate_extra).astype(jnp.bfloat16)
    grad_w_up = (dw_up[:2] + up_extra).astype(jnp.bfloat16)
    grad_w_down = (dw_down[:2] + down_extra).astype(jnp.bfloat16)
    return (grad_tokens, grad_w_gate, grad_w_up, grad_w_down)


def solution(mesh):
    return jax.shard_map(
        on_device,
        mesh=mesh,
        in_specs=(
            P(("groups", "expert", "inner"), "dp"),
            P(("groups", "expert", "inner"), "dp"),
            P(("groups", "expert", "inner"), None),
            P(("groups", "expert", "inner"), None),
            P(),
            P("expert", "dp", "inner"),
            P("expert", "dp", "inner"),
            P("expert", "inner", "dp"),
            P("expert", "dp", "inner"),
            P("expert", "dp", "inner"),
            P("expert", "inner", "dp"),
        ),
        out_specs=(
            P(("groups", "expert", "inner"), "dp"),
            P(("groups", "expert"), "dp", "inner"),
            P(("groups", "expert"), "dp", "inner"),
            P(("groups", "expert"), "inner", "dp"),
        ),
        check_vma=False,
    )
```

profile of v0, /device:TPU:0, one launch (start us, length us, event | category | flops | bytes accessed | tf_op | source)
XLA Modules:
  0.0 639.2 jit_solution(14092023790676570305)
XLA Ops:
  15.4 6.5 %all-to-all-start = ((bf16[3,8,48,1024]{3,2,0,1:T(8,128)(2,1)}), bf16[3,8,48,1024]{3,2,0,1:T(8,128)(2,1)S(1)}, u32[]{:S(2)}, u32[]{:S(2)}) async-start(bf16[3,8,48,1024]{3,2,0,1:T(8,128)(2,1)} %bitcast.49), calls=%async_computation | async-start | bytes 4718592 | tf_op jit(solution)/shard_map/all_to_all | solution.py:89
  24.1 52.5 %all-to-all-done = bf16[3,8,48,1024]{3,2,0,1:T(8,128)(2,1)S(1)} async-done(((bf16[3,8,48,1024]{3,2,0,1:T(8,128)(2,1)}), bf16[3,8,48,1024]{3,2,0,1:T(8,128)(2,1)S(1)}, u32[]{:S(2)}, u32[]{:S(2)}) %all-to-all-start) | async-done | bytes 2359328 | tf_op jit(solution)/shard_map/all_to_all | solution.py:89
  76.6 3.9 broadcast_in_dim.15
  80.4 4.4 all-to-all-start.1
  84.9 1.9 constant_dynamic-update-slice_fusion.1
  87.5 1.8 copy-done.22
  90.8 2.4 convolution_convert_fusion.3
  93.2 2.4 convolution_convert_fusion.2
  95.6 43.9 %all-to-all-done.1 = bf16[3,8,48,1024]{3,2,0,1:T(8,128)(2,1)} async-done(((bf16[3,8,48,1024]{3,2,0,1:T(8,128)(2,1)}), bf16[3,8,48,1024]{3,2,0,1:T(8,128)(2,1)}, u32[]{:S(2)}, u32[]{:S(2)}) %all-to-all-start.1) | async-done | bytes 2359328 | tf_op jit(solution)/shard_map/all_to_all | solution.py:92
  139.5 2.1 copy.104
  144.1 2.1 pad_maximum_fusion
  146.2 93.4 %all-reduce.2.cloned.1.call-done = bf16[3,384,1536]{2,1,0:T(8,128)(2,1)} async-done(((bf16[3,384,1536]{2,1,0:T(8,128)(2,1)}), bf16[3,384,1536]{2,1,0:T(8,128)(2,1)}) %all-reduce.2.cloned.1.call-update) | async-done | bytes 3538960 | tf_op jit(solution)/shard_map/psum | solution.py:110
  239.6 3.0 convert_element_type.86
  242.6 2.8 multiply_convert_fusion.1
  245.4 1.9 fusion.13
  247.3 2.6 copy-done.13
  251.1 3.0 convert_element_type.95
  254.1 3.1 fusion.32
  257.2 2.6 copy-done.3
  260.9 3.0 convert_element_type.93
  263.9 3.1 fusion.31
  267.0 2.6 copy-done.2
  271.5 8.8 %maximum_bitcast_fusion = bf16[4,1,393216]{2,0,1:T(4,128)(2,1)S(1)} fusion(bf16[4,131072]{1,0:T(4,128)(2,1)} %convert_element_type.95, bf16[4,131072]{1,0:T(4,128)(2,1)} %convert_element_type.93, bf16[4,131072]{1,0:T(4,128)(2,1)} %convert_element_type.92), kind=kLoop, calls=%fused_computation.15 | loop fusion | flops 9437184 | bytes 6291456 | tf_op jit(solution)/shard_map/all_to_all | solution.py:144
  280.8 6.3 reduce.2
  287.2 6.8 %reshape.192 = bf16[4,2,196608]{2,1,0:T(2,128)(2,1)} reshape(bf16[4,393216]{1,0:T(4,128)(2,1)} %reduce.2) | data formatting | bytes 6291456
  293.9 4.8 all-to-all-start.3
  298.8 3.5 fusion.30
  305.3 64.5 %all-to-all-done.3 = bf16[4,2,196608]{2,1,0:T(2,128)(2,1)} async-done(((bf16[4,2,196608]{2,1,0:T(2,128)(2,1)}), bf16[4,2,196608]{2,1,0:T(2,128)(2,1)}, u32[]{:S(2)}, u32[]{:S(2)}) %all-to-all-start.3) | async-done | bytes 3145760 | tf_op jit(solution)/shard_map/all_to_all | solution.py:144
  369.8 4.8 all-to-all-start.2
  374.6 6.2 reshape.193
  380.8 7.9 %convolution_convert_fusion = bf16[4,2,393216]{2,0,1:T(4,128)(2,1)S(1)} fusion(bf16[4,1,393216]{2,1,0:T(2,128)(2,1)} %reshape.193, s32[4,2]{0,1:T(2,128)S(1)} %multiply_add_fusion, s32[4]{0:T(128)S(1)} %copy-done.24), kind=kOutput, calls=%fused_computation | convolution fusion | flops 28311584 | bytes 9437232 | tf_op jit(solution)/shard_map/dot_general | solution.py:149
  388.7 20.6 %copy.111 = bf16[4,2,393216]{2,1,0:T(2,128)(2,1)} copy(bf16[4,2,393216]{2,0,1:T(4,128)(2,1)S(1)} %convolution_convert_fusion) | data formatting | bytes 12582912 | tf_op jit(solution)/shard_map/convert_element_type | solution.py:153
  409.3 20.0 %all-to-all-done.2 = bf16[3,8,48,1024]{3,2,0,1:T(8,128)(2,1)} async-done(((bf16[3,8,48,1024]{3,2,0,1:T(8,128)(2,1)}), bf16[3,8,48,1024]{3,2,0,1:T(8,128)(2,1)}, u32[]{:S(2)}, u32[]{:S(2)}) %all-to-all-start.2) | async-done | bytes 2359328 | tf_op jit(solution)/shard_map/all_to_all | solution.py:118
  429.3 5.5 all-to-all-start.4
  434.8 2.6 convert_reduce_fusion
  438.3 2.3 convolution_convert_fusion.5
  440.6 132.4 %all-to-all-done.4 = bf16[4,2,393216]{2,1,0:T(2,128)(2,1)} async-done(((bf16[4,2,393216]{2,1,0:T(2,128)(2,1)}), bf16[4,2,393216]{2,1,0:T(2,128)(2,1)}, u32[]{:S(2)}, u32[]{:S(2)}) %all-to-all-start.4) | async-done | bytes 6291488 | tf_op jit(solution)/shard_map/all_to_all | solution.py:152
  573.0 6.7 %convert_bitcast_fusion = f32[2,4,393216]{2,0,1:T(2,128)S(1)} fusion(bf16[4,2,393216]{2,1,0:T(2,128)(2,1)} %all-to-all-done.4), kind=kLoop, calls=%fused_computation.1 | loop fusion | flops 3145728 | bytes 18874368 | tf_op jit(solution)/shard_map/transpose | solution.py:159
  579.7 3.8 fusion.29
  583.5 4.7 copy.114
  588.1 5.8 reshape.186
  594.0 5.7 fusion
  599.6 4.7 copy.113
  604.4 6.0 reshape.185
  610.3 5.7 fusion.1
  616.0 4.8 copy.112
  620.8 5.8 reshape.184
  626.6 5.5 fusion.2
  (94 shorter events, 23.6 us)
Async XLA Ops:
  7.2 5.8 copy-start
  12.9 0.7 copy-start.14
  15.4 6.5 %copy-start.23 = (bf16[128,1024]{1,0:T(8,128)(2,1)S(1)}, bf16[128,1024]{1,0:T(8,128)(2,1)}, u32[]{:S(2)}) copy-start(bf16[128,1024]{1,0:T(8,128)(2,1)} %param.12) | copy-start | bytes 786436
  15.4 61.1 %all-to-all-start = ((bf16[3,8,48,1024]{3,2,0,1:T(8,128)(2,1)}), bf16[3,8,48,1024]{3,2,0,1:T(8,128)(2,1)S(1)}, u32[]{:S(2)}, u32[]{:S(2)}) async-start(bf16[3,8,48,1024]{3,2,0,1:T(8,128)(2,1)} %bitcast.49), calls=%async_computation | async-start | bytes 4718592 | tf_op jit(solution)/shard_map/all_to_all | solution.py:89
  76.6 3.9 copy-start.9
  80.4 59.1 %all-to-all-start.1 = ((bf16[3,8,48,1024]{3,2,0,1:T(8,128)(2,1)}), bf16[3,8,48,1024]{3,2,0,1:T(8,128)(2,1)}, u32[]{:S(2)}, u32[]{:S(2)}) async-start(bf16[3,8,48,1024]{3,2,0,1:T(8,128)(2,1)} %bitcast.48), calls=%async_computation.1 | async-start | bytes 4718592 | tf_op jit(solution)/shard_map/all_to_all | solution.py:92
  84.8 2.0 copy-start.21
  84.8 2.5 copy-start.18
  84.8 154.8 %all-reduce.2.cloned.1.call-start = ((), (), s32[]{:S(2)}) async-start(), calls=%async_computation.5 | async-start | bytes 7077888 | tf_op jit(solution)/shard_map/psum | solution.py:110
  87.4 3.4 copy-start.8
  87.4 2.0 copy-start.22
  87.4 3.1 copy-start.10
  90.5 2.7 copy-start.11
  139.5 2.3 copy-start.25
  139.5 2.6 copy-start.26
  141.6 1.9 copy-start.16
  142.1 1.7 copy-start.19
  142.1 2.0 copy-start.20
  242.6 2.8 copy-start.17
  247.3 2.6 copy-start.13
  257.2 2.6 copy-start.3
  267.0 2.6 copy-start.2
  293.9 4.8 copy-start.6
  293.9 75.8 %all-to-all-start.3 = ((bf16[4,2,196608]{2,1,0:T(2,128)(2,1)}), bf16[4,2,196608]{2,1,0:T(2,128)(2,1)}, u32[]{:S(2)}, u32[]{:S(2)}) async-start(bf16[4,2,196608]{2,1,0:T(2,128)(2,1)} %reshape.192), calls=%async_computation.3 | async-start | bytes 6291456 | tf_op jit(solution)/shard_map/all_to_all | solution.py:144
  298.8 3.5 copy-start.7
  298.8 3.5 copy-start.12
  369.8 59.5 %all-to-all-start.2 = ((bf16[3,8,48,1024]{3,2,0,1:T(8,128)(2,1)}), bf16[3,8,48,1024]{3,2,0,1:T(8,128)(2,1)}, u32[]{:S(2)}, u32[]{:S(2)}) async-start(bf16[3,8,48,1024]{3,2,0,1:T(8,128)(2,1)} %copy.105), calls=%async_computation.2 | async-start | bytes 4718592 | tf_op jit(solution)/shard_map/all_to_all | solution.py:118
  374.6 6.2 copy-start.24
  429.3 143.7 %all-to-all-start.4 = ((bf16[4,2,393216]{2,1,0:T(2,128)(2,1)}), bf16[4,2,393216]{2,1,0:T(2,128)(2,1)}, u32[]{:S(2)}, u32[]{:S(2)}) async-start(bf16[4,2,393216]{2,1,0:T(2,128)(2,1)} %copy.111), calls=%async_computation.4 | async-start | bytes 12582912 | tf_op jit(solution)/shard_map/all_to_all | solution.py:152
  437.3 1.0 copy-start.15
  594.0 5.7 copy-start.5
  610.3 5.7 copy-start.4
  626.6 5.5 copy-start.1
Sparse Core Ops, SparseCore 0:
  146.3 93.2 all-reduce.1
where the time goes:
time: 646 us; the launch traced here: 639 us
  waiting for transfers between devices  407 us (63%)
  local copies, waits for them, and re-layouts  107 us (17%)
  other arithmetic  53.9 us (8%)
  matrix products  31.1 us (5%)
  starting transfers between devices  26 us (4%)
  between operations  14.7 us (2%)
    all_to_all x1, waiting for transfers between devices, on_device(): lax.all_to_all(per_expert.reshape(expert_count, 2, piece_width).astype(jn...  132 us
    psum x1, waiting for transfers between devices, on_device(): lax.psum(partial_sums.astype(jnp.bfloat16), 'dp').astype(jnp.float32)  93.4 us
    all_to_all x1, waiting for transfers between devices, on_device(): lax.all_to_all(shadow_panel, 'expert', split_axis=0, concat_axis=0, tiled...  64.5 us
    all_to_all x1, waiting for transfers between devices, on_device(): lax.all_to_all(duplicate(rows_in), ('expert', 'inner'), split_axis=1, con...  52.5 us
    all_to_all x1, waiting for transfers between devices, on_device(): lax.all_to_all(duplicate(rows_grad), ('expert', 'inner'), split_axis=1, c...  43.9 us
    unnamed x60, local copies, waits for them, and re-layouts  28.3 us
    convert_element_type x1, local copies, waits for them, and re-layouts, on_device(): per_expert.reshape(expert_count, 2, piece_width).astype(jnp.bfloat16)  20.6 us
    all_to_all x1, waiting for transfers between devices, on_device(): lax.all_to_all(route_part.reshape(3, expert_count * inner_count, capacity...  20 us
  transfers between devices with their start and end apart: 6, of which 6 were waited for; matrix products, arithmetic and copies ran while one was open for 9% of the time, Pallas kernels for 0%

commit v1 on v0

v1 whole, which is shorter than its diff:
```python
import functools

import jax
import jax.numpy as jnp
from jax import lax
from jax.experimental import pallas as pl
from jax.experimental.pallas import tpu as pltpu
from jax.sharding import PartitionSpec as P

META = 16
VMEM_BYTES = 56 * 1024 * 1024


def call(body, out_shape, in_specs, out_specs, scratch, flops, moved, **kw):
    return pl.pallas_call(
        body,
        out_shape=out_shape,
        in_specs=in_specs,
        out_specs=out_specs,
        scratch_shapes=scratch,
        compiler_params=pltpu.CompilerParams(vmem_limit_bytes=VMEM_BYTES),
        cost_estimate=pl.CostEstimate(flops=flops, bytes_accessed=moved, transcendentals=0),
        **kw,
    )


WHOLE = pl.BlockSpec(memory_space=pltpu.VMEM)
SCALARS = pl.BlockSpec(memory_space=pltpu.SMEM)
REMAIN = pl.BlockSpec(memory_space=pl.ANY)


def pack_kernel(shadow_count, info, shadow, tok_ref, grad_ref, meta_ref, out_ref):
    rows = tok_ref.shape[0]
    out_ref[0:rows, :] = tok_ref[...]
    out_ref[rows : 2 * rows, :] = grad_ref[...]
    meta = meta_ref[...]
    ids, gates = meta[0:2], meta[2:4]
    choice = lax.broadcasted_iota(jnp.int32, ids.shape, 0)
    position = info[2] * rows + lax.broadcasted_iota(jnp.int32, ids.shape, 1) + choice
    position = position.astype(jnp.float32)
    entry = [shadow[j] for j in range(shadow_count)]
    named = [ids == e.astype(jnp.float32) for e in entry]
    copies = jnp.ones(ids.shape, jnp.float32)
    for hit in named:
        copies = copies + jnp.where(hit, 1.0, 0.0)
    halves = position - 2.0 * jnp.floor((position + 0.5) * 0.5)
    thirds = position - 3.0 * jnp.floor((position + 0.5) * (1.0 / 3.0))
    chosen = jnp.where(copies == 2.0, halves, jnp.where(copies == 3.0, thirds, 0.0))
    serving = ids
    for j in range(shadow_count):
        before = jnp.int32(0)
        for i in range(j):
            before = before + jnp.where(entry[i] == entry[j], 1, 0)
        take = named[j] & (chosen == (before + 1).astype(jnp.float32))
        serving = jnp.where(take, float(2 * shadow_count + j), serving)
    high = gates.astype(jnp.bfloat16)
    rest = gates - high.astype(jnp.float32)
    middle = rest.astype(jnp.bfloat16)
    low = (rest - middle.astype(jnp.float32)).astype(jnp.bfloat16)
    block = jnp.concatenate(
        [
            serving,
            high.astype(jnp.float32),
            middle.astype(jnp.float32),
            low.astype(jnp.float32),
            jnp.zeros((META - 8, rows), jnp.float32),
        ],
        axis=0,
    )
    out_ref[2 * rows : 2 * rows + META, :] = jnp.zeros((META, tok_ref.shape[1]), jnp.bfloat16)
    out_ref[2 * rows : 2 * rows + META, 0:rows] = block.astype(jnp.bfloat16)


def routing(own_ref, sib_ref, rows):
    meta = jnp.concatenate(
        [
            own_ref[2 * rows : 2 * rows + META, 0:rows].astype(jnp.float32),
            sib_ref[2 * rows : 2 * rows + META, 0:rows].astype(jnp.float32),
        ],
        axis=1,
    )
    return meta[0:1], meta[1:2], meta[2:3] + meta[4:5] + meta[6:7], meta[3:4] + meta[5:6] + meta[7:8]


def row_codes(meta, numbers):
    first, second, gate_a, gate_b = meta
    tokens = first.shape[1]
    hit_a, hit_b = first == numbers, second == numbers
    hit = jnp.where(hit_a | hit_b, 1.0, 0.0)
    gate = jnp.where(hit_a, gate_a, 0.0) + jnp.where(hit_b, gate_b, 0.0)
    earlier = lax.broadcasted_iota(jnp.int32, (tokens, tokens), 0) < lax.broadcasted_iota(
        jnp.int32, (tokens, tokens), 1
    )
    rank = jnp.dot(
        hit.astype(jnp.bfloat16),
        jnp.where(earlier, 1.0, 0.0).astype(jnp.bfloat16),
        preferred_element_type=jnp.float32,
    )
    return jnp.where(hit > 0.0, rank, -1.0), gate


def gather_rows(codes, gate, index, cap, tok, grad):
    tokens = codes.shape[1]
    place = lax.broadcasted_iota(jnp.int32, (cap, tokens), 0).astype(jnp.float32) == codes[
        index : index + 1, :
    ]
    row_gate = jnp.sum(jnp.where(place, gate[index : index + 1, :], 0.0), axis=1, keepdims=True)
    place = jnp.where(place, 1.0, 0.0).astype(jnp.bfloat16)
    inputs = jnp.dot(place, tok, preferred_element_type=jnp.float32).astype(jnp.bfloat16)
    grads = jnp.dot(place, grad, preferred_element_type=jnp.float32)
    return place, inputs, (grads * row_gate).astype(jnp.bfloat16)


def copy_numbers(z, shadow_count):
    slot = lax.broadcasted_iota(jnp.int32, (8, 1), 0)
    number = jnp.where(slot < 2, 2 * z + slot, jnp.where(slot == 2, 2 * shadow_count + z, -1))
    return number.astype(jnp.float32)


NT = (((1,), (1,)), ((), ()))
TN = (((0,), (0,)), ((), ()))


def fetch(pairs, sems):
    copies = []
    for i, (src, dst) in enumerate(pairs):
        copies.append(pltpu.make_async_copy(src, dst, sems.at[i]))
        copies[-1].start()
    return copies


def forward_kernel(shadow_count, cap, chunks, *refs):
    info = refs[0]
    packed = refs[1 : 1 + 2 * chunks]
    wg, wu, wd, cg, cu, cd = refs[1 + 2 * chunks : 7 + 2 * chunks]
    x_ref, g_ref, p_ref, place_ref, vg, vu, vd, sems = refs[7 + 2 * chunks :]
    rows = (packed[0].shape[0] - META) // 2
    hidden = wg.shape[2]
    copies = []
    for s in range(3):
        for src, extra, dst in ((wg, cg, vg), (wu, cu, vu), (wd, cd, vd)):
            copies.append((src.at[s] if s < 2 else extra.at[0], dst.at[s]))
    copies = fetch(copies, sems)
    numbers = copy_numbers(info[0], shadow_count)
    width = cap * chunks
    for k in range(chunks):
        own, sib = packed[2 * k], packed[2 * k + 1]
        codes, gate = row_codes(routing(own, sib, rows), numbers)
        tok = jnp.concatenate([own[0:rows, :], sib[0:rows, :]], axis=0)
        grad = jnp.concatenate([own[rows : 2 * rows, :], sib[rows : 2 * rows, :]], axis=0)
        for s in range(3):
            place, inputs, grads = gather_rows(codes, gate, s, cap, tok, grad)
            at = s * width + k * cap
            place_ref[at : at + cap, :] = place
            x_ref[at : at + cap, :] = inputs
            g_ref[at : at + cap, :] = grads
    for s in range(3):
        at = s * width
        inputs, grads = x_ref[at : at + width, :], g_ref[at : at + width, :]
        copies[3 * s].wait()
        p_ref[at : at + width, 0:hidden] = jnp.dot(
            inputs, vg[s], preferred_element_type=jnp.float32
        ).astype(jnp.bfloat16)
        copies[3 * s + 1].wait()
        p_ref[at : at + width, hidden : 2 * hidden] = jnp.dot(
            inputs, vu[s], preferred_element_type=jnp.float32
        ).astype(jnp.bfloat16)
        copies[3 * s + 2].wait()
        p_ref[at : at + width, 2 * hidden : 3 * hidden] = lax.dot_general(
            grads, vd[s], NT, preferred_element_type=jnp.float32
        ).astype(jnp.bfloat16)


def backward_kernel(parts, cap, chunks, *refs):
    partial = refs[0:parts]
    place_ref, wg, wu, cg, cu = refs[parts : parts + 5]
    a_ref, s_ref, own_ref, sib_ref, vg, vu, total, sems = refs[parts + 5 :]
    hidden = wg.shape[2]
    rows = own_ref.shape[0] // chunks
    width = cap * chunks
    copies = []
    for s in range(3):
        for src, extra, dst in ((wg, cg, vg), (wu, cu, vu)):
            copies.append((src.at[s] if s < 2 else extra.at[0], dst.at[s]))
    copies = fetch(copies, sems)
    for s in range(3):
        at = s * width
        full = partial[0][at : at + width, :].astype(jnp.float32)
        for other in partial[1:]:
            full = full + other[at : at + width, :].astype(jnp.float32)
        gate, up, down = full[:, 0:hidden], full[:, hidden : 2 * hidden], full[:, 2 * hidden :]
        sig = 1.0 / (1.0 + jnp.exp(-gate))
        swish = gate * sig
        grad_up = (down * swish).astype(jnp.bfloat16)
        grad_gate = (down * up * sig * (1.0 + gate * (1.0 - sig))).astype(jnp.bfloat16)
        inner = (swish * up).astype(jnp.bfloat16)
        to, base = (a_ref, at) if s < 2 else (s_ref, 0)
        to[base : base + width, 0:hidden] = grad_gate
        to[base : base + width, hidden : 2 * hidden] = grad_up
        to[base : base + width, 2 * hidden : 3 * hidden] = inner
        copies[2 * s].wait()
        route = lax.dot_general(grad_gate, vg[s], NT, preferred_element_type=jnp.float32)
        copies[2 * s + 1].wait()
        route = route + lax.dot_general(grad_up, vu[s], NT, preferred_element_type=jnp.float32)
        route = route.astype(jnp.bfloat16)
        for k in range(chunks):
            part = lax.dot_general(
                place_ref[at + k * cap : at + (k + 1) * cap, :],
                route[k * cap : (k + 1) * cap],
                TN,
                preferred_element_type=jnp.float32,
            )
            if s == 0:
                total[k] = part
            elif s == 1:
                total[k] += part
            else:
                part = (total[k] + part).astype(jnp.bfloat16)
                own_ref[k * rows : (k + 1) * rows, :] = part[0:rows]
                sib_ref[k * rows : (k + 1) * rows, :] = part[rows : 2 * rows]


def weights_kernel(shadow_count, cap, sizes, *refs):
    count, groups = shadow_count, len(sizes)
    info = refs[0]
    refs = refs[1:]
    xs, gs, acts = refs[0:groups], refs[groups : 2 * groups], refs[2 * groups : 3 * groups]
    shadow_acts = refs[3 * groups : 3 * groups + 2]
    packed = refs[3 * groups + 2 : 3 * groups + 2 + 2 * count]
    og, ou, od, x_all, g_all, a_all, tg, tu, td = refs[3 * groups + 2 + 2 * count :]
    rows = (packed[0].shape[0] - META) // 2
    hidden = og.shape[2]
    mine = pl.program_id(0)
    at = 0
    for i, size in enumerate(sizes):
        x_all[at : at + size, :] = xs[i][...]
        g_all[at : at + size, :] = gs[i][...]
        a_all[at : at + size, :] = acts[i][...]
        at += size

    def products():
        x, g = x_all[...], g_all[...]
        return (
            lax.dot_general(x, a_all[:, 0:hidden], TN, preferred_element_type=jnp.float32),
            lax.dot_general(x, a_all[:, hidden : 2 * hidden], TN, preferred_element_type=jnp.float32),
            lax.dot_general(a_all[:, 2 * hidden :], g, TN, preferred_element_type=jnp.float32),
        )

    tg[...], tu[...], td[...] = products()
    for slot in range(2):

        @pl.when(info[4 + 2 * slot] == mine)
        def _(slot=slot):
            holder = info[5 + 2 * slot]
            numbers = jnp.full((8, 1), 2 * count + holder, jnp.int32).astype(jnp.float32)
            for k in range(count):
                own, sib = packed[2 * k], packed[2 * k + 1]
                codes, gate = row_codes(routing(own, sib, rows), numbers)
                tok = jnp.concatenate([own[0:rows, :], sib[0:rows, :]], axis=0)
                grad = jnp.concatenate([own[rows : 2 * rows, :], sib[rows : 2 * rows, :]], axis=0)
                _, inputs, grads = gather_rows(codes, gate, 0, cap, tok, grad)
                x_all[k * cap : (k + 1) * cap, :] = inputs
                g_all[k * cap : (k + 1) * cap, :] = grads
                start = pl.multiple_of((holder ^ info[0] ^ k) * cap, 16)
                a_all[k * cap : (k + 1) * cap, :] = shadow_acts[slot][pl.ds(start, cap), :]
            more_g, more_u, more_d = products()
            tg[...] += more_g
            tu[...] += more_u
            td[...] += more_d

    og[0] = tg[...].astype(jnp.bfloat16)
    ou[0] = tu[...].astype(jnp.bfloat16)
    od[0] = td[...].astype(jnp.bfloat16)


def shadow_patterns():
    found = []
    for code in range(256):
        owners = [(code >> (2 * j)) & 3 for j in range(4)]
        if any(owners[j] == j for j in range(4)):
            continue
        if sorted(owners.count(i) for i in range(4)) == [0, 0, 2, 2]:
            found.append(owners)
    return found


def shadow_moves(acts, owners, count):
    z = lax.axis_index("expert")
    if count != 4:
        whole = lax.all_gather(acts, "expert")
        slots = jnp.arange(count, dtype=jnp.int32)
        low = jnp.min(jnp.where(owners == z, slots, count - 1))
        high = jnp.max(jnp.where(owners == z, slots, 0))
        return (
            lax.dynamic_index_in_dim(whole, low, 0, keepdims=False),
            lax.dynamic_index_in_dim(whole, high, 0, keepdims=False),
        )
    branches, which = [], jnp.int32(0)
    for i, pattern in enumerate(shadow_patterns()):
        lows = [(pattern.index(o), o) for o in sorted(set(pattern))]
        highs = [(3 - pattern[::-1].index(o), o) for o in sorted(set(pattern))]

        def branch(x, lows=lows, highs=highs):
            return lax.ppermute(x, "expert", lows), lax.ppermute(x, "expert", highs)

        branches.append(branch)
        same = jnp.all(owners == jnp.array(pattern, jnp.int32))
        which = jnp.where(same, i, which)
    return lax.switch(which, branches, acts)


def chunk_groups(count):
    groups, at, size = [[0]], 1, 1
    while at < count:
        groups.append(list(range(at, min(count, at + size))))
        at += size
        size = max(size, at)
    return groups


def on_device(
    tokens,
    out_grad,
    expert_ids,
    gate_weights,
    shadow_expert,
    w_gate,
    w_up,
    w_down,
    copy_gate,
    copy_up,
    copy_down,
):
    bf16 = jnp.bfloat16
    rows, width = tokens.shape
    hidden = w_gate.shape[2]
    count, dp_count = lax.axis_size("expert"), lax.axis_size("dp")
    cap = -(-2 * max(2, 3 * rows // (2 * count)) // 16) * 16
    z, core = lax.axis_index("expert"), lax.axis_index("inner")
    owners = shadow_expert // 2
    slots = jnp.arange(count, dtype=jnp.int32)
    low = jnp.min(jnp.where(owners == z, slots, count - 1))
    high = jnp.max(jnp.where(owners == z, slots, 0))
    is_owner = jnp.any(owners == z)
    of_low = jnp.where(is_owner, jnp.sum(jnp.where(slots == low, shadow_expert, 0)) % 2, -1)
    of_high = jnp.where(is_owner, jnp.sum(jnp.where(slots == high, shadow_expert, 0)) % 2, -1)
    info = jnp.stack(
        [z, core, 2 * z + core, jnp.int32(0), of_low, low, of_high, high]
    ).astype(jnp.int32)
    meta = jnp.concatenate([expert_ids.astype(jnp.float32), gate_weights], axis=1).T

    shape = jax.ShapeDtypeStruct
    pack = call(
        functools.partial(pack_kernel, count),
        shape((2 * rows + META, width), bf16),
        [SCALARS, SCALARS, WHOLE, WHOLE, WHOLE],
        WHOLE,
        [],
        0,
        8 * rows * width,
    )
    own = [pack(info, shadow_expert, tokens, out_grad, meta)]
    for k in range(1, count):
        own.append(lax.ppermute(own[0], "expert", [(i, i ^ k) for i in range(count)]))
    swap = [(0, 1), (1, 0)]
    sib = [lax.ppermute(x, "inner", swap) for x in own]

    groups = chunk_groups(count)
    kept, returned = [], [None] * count
    for group in groups:
        chunks = len(group)
        size = cap * chunks
        forward = call(
            functools.partial(forward_kernel, count, cap, chunks),
            (
                shape((3 * size, width), bf16),
                shape((3 * size, width), bf16),
                shape((3 * size, 3 * hidden), bf16),
                shape((3 * size, 2 * rows), bf16),
            ),
            [SCALARS] + [WHOLE] * (2 * chunks) + [REMAIN] * 6,
            (WHOLE,) * 4,
            [
                pltpu.VMEM((3, width, hidden), bf16),
                pltpu.VMEM((3, width, hidden), bf16),
                pltpu.VMEM((3, hidden, width), bf16),
                pltpu.SemaphoreType.DMA((9,)),
            ],
            18 * size * width * hidden,
            18 * width * hidden + 20 * size * width,
        )
        packed = [a for k in group for a in (own[k], sib[k])]
        inputs, grads, partial, place = forward(
            info, *packed, w_gate, w_up, w_down, copy_gate, copy_up, copy_down
        )
        if dp_count == 2:
            partials = [partial, lax.ppermute(partial, "dp", swap)]
        else:
            partials = [lax.psum(partial, "dp")]
        backward = call(
            functools.partial(backward_kernel, len(partials), cap, chunks),
            (
                shape((2 * size, 3 * hidden), bf16),
                shape((size, 3 * hidden), bf16),
                shape((chunks * rows, width), bf16),
                shape((chunks * rows, width), bf16),
            ),
            [WHOLE] * (len(partials) + 1) + [REMAIN] * 4,
            (WHOLE,) * 4,
            [
                pltpu.VMEM((3, width, hidden), bf16),
                pltpu.VMEM((3, width, hidden), bf16),
                pltpu.VMEM((chunks, 2 * rows, width), jnp.float32),
                pltpu.SemaphoreType.DMA((6,)),
            ],
            12 * size * width * hidden,
            12 * width * hidden + 20 * size * width,
        )
        acts, shadow_acts, dx_own, dx_sib = backward(
            *partials, place, w_gate, w_up, copy_gate, copy_up
        )
        dx_other = lax.ppermute(dx_sib, "inner", swap)
        for i, k in enumerate(group):
            both = dx_own[i * rows : (i + 1) * rows].astype(jnp.float32) + dx_other[
                i * rows : (i + 1) * rows
            ].astype(jnp.float32)
            if k > 0:
                both = lax.ppermute(both.astype(bf16), "expert", [(i, i ^ k) for i in range(count)])
            returned[k] = both
        kept.append((inputs, grads, acts, shadow_acts))

    total = returned[0]
    for x in returned[1:]:
        total = total + x.astype(jnp.float32)
    grad_tokens = total.astype(bf16)

    shadow_rows = jnp.concatenate([k[3] for k in kept], axis=0)
    moved = shadow_moves(shadow_rows, owners, count)
    sizes = [cap * len(g) for g in groups]

    def part(size, columns):
        return pl.BlockSpec((size, columns), lambda e: (e, 0))

    every = cap * count
    weights = call(
        functools.partial(weights_kernel, count, cap, sizes),
        (
            shape((2, width, hidden), bf16),
            shape((2, width, hidden), bf16),
            shape((2, hidden, width), bf16),
        ),
        [SCALARS]
        + [part(s, width) for s in sizes] * 2
        + [part(s, 3 * hidden) for s in sizes]
        + [WHOLE] * (2 + 2 * count),
        (
            pl.BlockSpec((1, width, hidden), lambda e: (e, 0, 0)),
            pl.BlockSpec((1, width, hidden), lambda e: (e, 0, 0)),
            pl.BlockSpec((1, hidden, width), lambda e: (e, 0, 0)),
        ),
        [
            pltpu.VMEM((every, width), bf16),
            pltpu.VMEM((every, width), bf16),
            pltpu.VMEM((every, 3 * hidden), bf16),
            pltpu.VMEM((width, hidden), jnp.float32),
            pltpu.VMEM((width, hidden), jnp.float32),
            pltpu.VMEM((hidden, width), jnp.float32),
        ],
        24 * every * width * hidden,
        24 * width * hidden,
        grid=(2,),
    )
    grad_gate, grad_up, grad_down = weights(
        info,
        *[k[0] for k in kept],
        *[k[1] for k in kept],
        *[k[2] for k in kept],
        *moved,
        *[a for k in range(count) for a in (own[k], sib[k])],
    )
    return grad_tokens, grad_gate, grad_up, grad_down


def solution(mesh):
    return jax.shard_map(
        on_device,
        mesh=mesh,
        in_specs=(
            P(("groups", "expert", "inner"), "dp"),
            P(("groups", "expert", "inner"), "dp"),
            P(("groups", "expert", "inner"), None),
            P(("groups", "expert", "inner"), None),
            P(),
            P("expert", "dp", "inner"),
            P("expert", "dp", "inner"),
            P("expert", "inner", "dp"),
            P("expert", "dp", "inner"),
            P("expert", "dp", "inner"),
            P("expert", "inner", "dp"),
        ),
        out_specs=(
            P(("groups", "expert", "inner"), "dp"),
            P(("groups", "expert"), "dp", "inner"),
            P(("groups", "expert"), "dp", "inner"),
            P(("groups", "expert"), "inner", "dp"),
        ),
        check_vma=False,
    )
```

time: 646 us -> 260 us (0.40)
  waiting for transfers between devices: 407 us -> 122 us
  local copies, waits for them, and re-layouts: 107 us -> 7.41 us
  Pallas kernels: 0 us -> 56.9 us
  other arithmetic: 53.9 us -> 9.77 us
  matrix products: 31.1 us -> 0 us
  starting transfers between devices: 26 us -> 47 us
    all_to_all x5 -> x0, waiting for transfers between devices: 313 us -> none  [the longest x1 132 us: on_device(): lax.all_to_all(per_expert.reshape(expert_count, 2, piece_width).astype(jn...]
    ppermute x0 -> x18, waiting for transfers between devices: none -> 122 us  [the longest x3 50.2 us: on_device(): lax.ppermute(own[0], 'expert', [(i, i ^ k) for i in range(count)])]
    psum x1 -> x0, waiting for transfers between devices: 93.4 us -> none  [on_device(): lax.psum(partial_sums.astype(jnp.bfloat16), 'dp').astype(jnp.float32)]
    pallas_call x0 -> x8, Pallas kernels: none -> 56.9 us  [the longest x3 22.8 us: on_device(): backward(*partials, place, w_gate, w_up, copy_gate, copy_up)]
    ppermute x0 -> x18, starting transfers between devices: none -> 47 us  [the longest x3 28.5 us: on_device(): lax.ppermute(both.astype(bf16), 'expert', [(i, i ^ k) for i in range(coun...]
    dot_general x12 -> x0, matrix products: 31.1 us -> none  [the longest x1 7.91 us: on_device(): jnp.dot(indicator.T, spread_pieces.astype(jnp.float32), precision=lax.Pre...]
    convert_element_type x5 -> x0, local copies, waits for them, and re-layouts: 29.9 us -> none  [the longest x1 20.6 us: on_device(): per_expert.reshape(expert_count, 2, piece_width).astype(jnp.bfloat16)]
    all_to_all x5 -> x0, starting transfers between devices: 25.9 us -> none  [the longest x1 6.46 us: on_device(): lax.all_to_all(duplicate(rows_in), ('expert', 'inner'), split_axis=1, con...]
  transfers between devices with their start and end apart: 6 -> 18, of which waited for: 6 -> 8; matrix products, arithmetic and copies ran while one was open for 9% -> 1% of each run, Pallas kernels for 0% -> 21%
where the time goes in v1:
time: 260 us; the launch traced here: 256 us
  waiting for transfers between devices  122 us (47%)
  Pallas kernels  56.9 us (22%)
  starting transfers between devices  47 us (18%)
  between operations  13 us (5%)
  other arithmetic  9.77 us (4%)
  local copies, waits for them, and re-layouts  7.41 us (3%)
    ppermute x3, waiting for transfers between devices, on_device(): lax.ppermute(own[0], 'expert', [(i, i ^ k) for i in range(count)])  50.2 us
    ppermute x3, waiting for transfers between devices, on_device(): partials = [partial, lax.ppermute(partial, 'dp', swap)]  37.5 us
    ppermute x3, starting transfers between devices, on_device(): lax.ppermute(both.astype(bf16), 'expert', [(i, i ^ k) for i in range(coun...  28.5 us
    ppermute x2, waiting for transfers between devices, branch(): return (lax.ppermute(x, 'expert', lows), lax.ppermute(x, 'expert', highs))  24.3 us
    pallas_call x3, Pallas kernels, on_device(): backward(*partials, place, w_gate, w_up, copy_gate, copy_up)  22.8 us
    pallas_call x3, Pallas kernels, on_device(): forward(info, *packed, w_gate, w_up, w_down, copy_gate, copy_up, copy_down)  22 us
    pallas_call x1, Pallas kernels, on_device(): weights(info, *[k[0] for k in kept], *[k[1] for k in kept], *[k[2] for k...  10.1 us
    ppermute x2, starting transfers between devices, branch(): return (lax.ppermute(x, 'expert', lows), lax.ppermute(x, 'expert', highs))  8.49 us
  transfers between devices with their start and end apart: 18, of which 8 were waited for; matrix products, arithmetic and copies ran while one was open for 1% of the time, Pallas kernels for 21%

profile of v1, /device:TPU:0, one launch (start us, length us, event | category | flops | bytes accessed | tf_op | source)
XLA Modules:
  0.0 256.4 jit_solution(17479366601023014183)
XLA Ops:
  0.6 1.4 select_reduce_fusion
  2.0 2.5 fusion.1
  8.4 0.7 convert_element_type.48
  9.1 1.7 compare_reduce_fusion
  12.1 1.3 maximum_bitcast_fusion.meta_ref
  13.3 1.9 stack.31.info.refs_0_
  15.2 1.9 shard_map.242.refs_1_.refs_12_
  17.1 5.0 %collective-permute-start.34 = (bf16[272,1024]{1,0:T(8,128)(2,1)}, bf16[272,1024]{1,0:T(8,128)(2,1)S(1)}, u32[]{:S(2)}, u32[]{:S(2)}) collective-permute-start(bf16[272,1024]{1,0:T(8,128)(2,1)} %shard_map.242.refs_1_.refs_12_), channel_id=1, source_target_pairs={{0,12},{4,8},{8,4},{12,0},{1,13},{5,9},{9,5},{13,1},{2,14},{6,10},... | collective-permute-start | bytes 1671176 | tf_op jit(solution)/shard_map/ppermute | solution.py:364
  22.2 13.8 %collective-permute-done.34.refs_3_.refs_18_ = bf16[272,1024]{1,0:T(8,128)(2,1)S(1)} collective-permute-done((bf16[272,1024]{1,0:T(8,128)(2,1)}, bf16[272,1024]{1,0:T(8,128)(2,1)S(1)}, u32[]{:S(2)}, u32[]{:S(2)}) %collective-permute-start.34) | collective-permute-done | bytes 557088 | tf_op jit(solution)/shard_map/ppermute | solution.py:364
  36.0 34.0 %collective-permute-done.32.refs_1_.refs_16_ = bf16[272,1024]{1,0:T(8,128)(2,1)S(1)} collective-permute-done((bf16[272,1024]{1,0:T(8,128)(2,1)}, bf16[272,1024]{1,0:T(8,128)(2,1)S(1)}, u32[]{:S(2)}, u32[]{:S(2)}) %collective-permute-start.32) | collective-permute-done | bytes 557088 | tf_op jit(solution)/shard_map/ppermute | solution.py:364
  70.0 1.9 collective-permute-done.33.refs_2_.refs_17_
  72.0 0.8 copy-done.8
  72.8 8.5 %shard_map.247 = (bf16[576,1024]{1,0:T(8,128)(2,1)}, bf16[576,1024]{1,0:T(8,128)(2,1)}, bf16[576,1536]{1,0:T(8,128)(2,1)}, bf16[576,256]{1,0:T(8,128)(2,1)}) custom-call(s32[8]{0:T(128)} %stack.31.info.refs_0_, bf16[272,1024]{1,0:T(8,128)(2,1)} %copy-done.6, bf16[272,1024]{1,0:T(8,128)(2,1)} %copy-done.8, bf16[272,1024]{1,0:T(8,128)(2,1)} %copy-done.5, ...), custom_call_target="tpu_custom_call" | custom-call | flops 1811939328 | bytes 13369344 | tf_op jit(solution)/shard_map/pallas_call | solution.py:393
  81.3 1.6 collective-permute-start.36
  82.9 2.4 collective-permute-done.27.refs_1_.refs_14_
  85.2 0.5 collective-permute-start.24
  85.7 1.4 collective-permute-done.28.refs_2_.refs_15_
  87.2 0.8 copy-done.10
  88.0 6.7 %shard_map.245 = (bf16[288,1024]{1,0:T(8,128)(2,1)}, bf16[288,1024]{1,0:T(8,128)(2,1)}, bf16[288,1536]{1,0:T(8,128)(2,1)}, bf16[288,256]{1,0:T(8,128)(2,1)}) custom-call(s32[8]{0:T(128)} %stack.31.info.refs_0_, bf16[272,1024]{1,0:T(8,128)(2,1)} %copy-done.9, bf16[272,1024]{1,0:T(8,128)(2,1)} %copy-done.10, bf16[2,1024,512]{2,1,0:T(8,128)(2,1)} %refs_3_.9, ...), custom_call_target="tpu_custom_call" | custom-call | flops 905969664 | bytes 11403264 | tf_op jit(solution)/shard_map/pallas_call | solution.py:393
  94.8 1.6 collective-permute-start.29
  96.3 0.8 copy-done.11
  97.1 6.7 %shard_map.243 = (bf16[288,1024]{1,0:T(8,128)(2,1)}, bf16[288,1024]{1,0:T(8,128)(2,1)}, bf16[288,1536]{1,0:T(8,128)(2,1)}, bf16[288,256]{1,0:T(8,128)(2,1)}) custom-call(s32[8]{0:T(128)} %stack.31.info.refs_0_, bf16[272,1024]{1,0:T(8,128)(2,1)} %shard_map.242.refs_1_.refs_12_, bf16[272,1024]{1,0:T(8,128)(2,1)} %copy-done.11, bf16[2,1024,512]{2,1,0:T(8,128)(2,1)} %refs_3_.9, ...), custom_call_target="tpu_custom_call" | custom-call | flops 905969664 | bytes 11403264 | tf_op jit(solution)/shard_map/pallas_call | solution.py:393
  103.9 0.6 collective-permute-start.25
  104.5 37.5 %collective-permute-done.29.refs_1_ = bf16[288,1536]{1,0:T(8,128)(2,1)S(1)} collective-permute-done((bf16[288,1536]{1,0:T(8,128)(2,1)}, bf16[288,1536]{1,0:T(8,128)(2,1)S(1)}, u32[]{:S(2)}, u32[]{:S(2)}) %collective-permute-start.29) | collective-permute-done | bytes 884768 | tf_op jit(solution)/shard_map/ppermute | solution.py:397
  142.0 0.9 copy-done.3
  142.9 6.9 %shard_map.246 = (bf16[192,1536]{1,0:T(8,128)(2,1)}, bf16[96,1536]{1,0:T(8,128)(2,1)}, bf16[128,1024]{1,0:T(8,128)(2,1)}, bf16[128,1024]{1,0:T(8,128)(2,1)}) custom-call(bf16[288,1536]{1,0:T(8,128)(2,1)} %get-tuple-element.49.refs_0_, bf16[288,1536]{1,0:T(8,128)(2,1)} %copy-done.3, bf16[288,256]{1,0:T(8,128)(2,1)} %get-tuple-element.50.refs_2_, ...), custom_call_target="tpu_custom_call" | custom-call | flops 603979776 | bytes 8257536 | tf_op jit(solution)/shard_map/pallas_call | solution.py:419
  149.8 0.1 collective-permute-start.30
  156.9 0.0 copy-start.1
  156.9 1.2 copy-done.1
  158.1 9.1 %shard_map.248 = (bf16[384,1536]{1,0:T(8,128)(2,1)}, bf16[192,1536]{1,0:T(8,128)(2,1)}, bf16[256,1024]{1,0:T(8,128)(2,1)}, bf16[256,1024]{1,0:T(8,128)(2,1)}) custom-call(bf16[576,1536]{1,0:T(8,128)(2,1)} %get-tuple-element.53.refs_0_, bf16[576,1536]{1,0:T(8,128)(2,1)} %copy-done.1, bf16[576,256]{1,0:T(8,128)(2,1)} %get-tuple-element.54.refs_2_, ...), custom_call_target="tpu_custom_call" | custom-call | flops 1207959552 | bytes 10223616 | tf_op jit(solution)/shard_map/pallas_call | solution.py:419
  167.2 0.6 collective-permute-start.37
  167.7 0.9 copy-done.2
  168.7 6.9 %shard_map.244 = (bf16[192,1536]{1,0:T(8,128)(2,1)}, bf16[96,1536]{1,0:T(8,128)(2,1)}, bf16[128,1024]{1,0:T(8,128)(2,1)}, bf16[128,1024]{1,0:T(8,128)(2,1)}) custom-call(bf16[288,1536]{1,0:T(8,128)(2,1)} %get-tuple-element.45.refs_0_, bf16[288,1536]{1,0:T(8,128)(2,1)} %copy-done.2, bf16[288,256]{1,0:T(8,128)(2,1)} %get-tuple-element.46.refs_2_, ...), custom_call_target="tpu_custom_call" | custom-call | flops 603979776 | bytes 8257536 | tf_op jit(solution)/shard_map/pallas_call | solution.py:419
  175.6 0.0 copy-start.4
  175.6 0.1 collective-permute-start.26
  175.7 0.1 add_convert_fusion.3
  175.8 0.9 collective-permute-start.31
  176.7 1.1 pad_maximum_fusion
  177.8 32.8 %conditional.1 = (bf16[384,1536]{1,0:T(8,128)(2,1)}, bf16[384,1536]{1,0:T(8,128)(2,1)}) conditional(s32[]{:T(128)} %clamp.3, bf16[384,1536]{1,0:T(8,128)(2,1)S(1)} %pad_maximum_fusion, bf16[384,1536]{1,0:T(8,128)(2,1)S(1)} %pad_maximum_fusion, bf16[384,1536]{1,0:T(8,128)(2,1)S(1)} %pad_maximum_fusion, ...), branch_computations={%region_16.17_spmd, %region_17.18_spmd, %region_18.19_spmd, %regio... | conditional | bytes 9437280 | solution.py:309
  177.8 1.7 collective-permute-start.21
  179.5 6.8 %collective-permute-start.20 = (bf16[384,1536]{1,0:T(8,128)(2,1)S(1)}, bf16[384,1536]{1,0:T(8,128)(2,1)}, u32[]{:S(2)}, u32[]{:S(2)}) collective-permute-start(bf16[384,1536]{1,0:T(8,128)(2,1)S(1)} %param.10), channel_id=1, source_target_pairs={{4,8},{0,12},{5,9},{1,13},{6,10},{2,14},{7,11},{3,15},{20,24},{16,... | collective-permute-start | bytes 3538952 | tf_op jit(solution)/shard_map/cond/branch_10_fun/ppermute | solution.py:304
  186.3 24.3 %collective-permute-done.20 = bf16[384,1536]{1,0:T(8,128)(2,1)} collective-permute-done((bf16[384,1536]{1,0:T(8,128)(2,1)S(1)}, bf16[384,1536]{1,0:T(8,128)(2,1)}, u32[]{:S(2)}, u32[]{:S(2)}) %collective-permute-start.20) | collective-permute-done | bytes 1179680 | tf_op jit(solution)/shard_map/cond/branch_10_fun/ppermute | solution.py:304
  210.6 0.2 add_convert_fusion.2
  210.8 27.3 %collective-permute-start.38 = (bf16[128,1024]{1,0:T(8,128)(2,1)S(1)}, bf16[128,1024]{1,0:T(8,128)(2,1)S(1)}, u32[]{:S(2)}, u32[]{:S(2)}) collective-permute-start(bf16[128,1024]{1,0:T(8,128)(2,1)S(1)} %get-tuple-element.91), channel_id=1, source_target_pairs={{0,8},{4,12},{8,0},{12,4},{1,9},{5,13},{9,1},{13,5},{2,10},{6,14},... | collective-permute-start | bytes 786440 | tf_op jit(solution)/shard_map/ppermute | solution.py:428
  238.1 0.3 collective-permute-start.39
  238.5 10.1 %shard_map.249 = (bf16[2,1024,512]{2,1,0:T(8,128)(2,1)}, bf16[2,1024,512]{2,1,0:T(8,128)(2,1)}, bf16[2,512,1024]{2,1,0:T(8,128)(2,1)}) custom-call(s32[8]{0:T(128)} %stack.31.info.refs_0_, bf16[288,1024]{1,0:T(8,128)(2,1)} %get-tuple-element.57.refs_1_, bf16[288,1024]{1,0:T(8,128)(2,1)} %get-tuple-element.58.refs_2_, ...), custom_call_target="tpu_custom_call" | custom-call | flops 4831838208 | bytes 12582912 | tf_op jit(solution)/shard_map/pallas_call | solution.py:473
  248.6 6.8 %collective-permute-done.38 = bf16[128,1024]{1,0:T(8,128)(2,1)S(1)} collective-permute-done((bf16[128,1024]{1,0:T(8,128)(2,1)S(1)}, bf16[128,1024]{1,0:T(8,128)(2,1)S(1)}, u32[]{:S(2)}, u32[]{:S(2)}) %collective-permute-start.38) | collective-permute-done | bytes 262176 | tf_op jit(solution)/shard_map/ppermute | solution.py:428
  255.5 0.9 add_convert_fusion
  (39 shorter events, 0.1 us)
Async XLA Ops:
  17.1 68.1 %copy-start = (bf16[272,1024]{1,0:T(8,128)(2,1)S(1)}, bf16[272,1024]{1,0:T(8,128)(2,1)}, u32[]{:S(2)}) copy-start(bf16[272,1024]{1,0:T(8,128)(2,1)} %shard_map.242.refs_1_.refs_12_) | copy-start | bytes 1671172
  17.1 18.9 %collective-permute-start.34 = (bf16[272,1024]{1,0:T(8,128)(2,1)}, bf16[272,1024]{1,0:T(8,128)(2,1)S(1)}, u32[]{:S(2)}, u32[]{:S(2)}) collective-permute-start(bf16[272,1024]{1,0:T(8,128)(2,1)} %shard_map.242.refs_1_.refs_12_), channel_id=1, source_target_pairs={{0,12},{4,8},{8,4},{12,0},{1,13},{5,9},{9,5},{13,1},{2,14},{6,10},... | collective-permute-start | bytes 1671176 | tf_op jit(solution)/shard_map/ppermute | solution.py:364
  22.2 47.8 %collective-permute-start.32 = (bf16[272,1024]{1,0:T(8,128)(2,1)}, bf16[272,1024]{1,0:T(8,128)(2,1)S(1)}, u32[]{:S(2)}, u32[]{:S(2)}) collective-permute-start(bf16[272,1024]{1,0:T(8,128)(2,1)} %shard_map.242.refs_1_.refs_12_), channel_id=1, source_target_pairs={{0,8},{4,12},{8,0},{12,4},{1,9},{5,13},{9,1},{13,5},{2,10},{6,14},... | collective-permute-start | bytes 1671176 | tf_op jit(solution)/shard_map/ppermute | solution.py:364
  36.0 35.9 %copy-start.5 = (bf16[272,1024]{1,0:T(8,128)(2,1)}, bf16[272,1024]{1,0:T(8,128)(2,1)S(1)}, u32[]{:S(2)}) copy-start(bf16[272,1024]{1,0:T(8,128)(2,1)S(1)} %collective-permute-done.34.refs_3_.refs_18_) | copy-start | bytes 1671172
  36.0 34.0 %collective-permute-start.35 = (bf16[272,1024]{1,0:T(8,128)(2,1)S(1)}, bf16[272,1024]{1,0:T(8,128)(2,1)S(1)}, u32[]{:S(2)}, u32[]{:S(2)}) collective-permute-start(bf16[272,1024]{1,0:T(8,128)(2,1)S(1)} %collective-permute-done.34.refs_3_.refs_18_), channel_id=1, source_target_pairs={{0,1},{1,0},{2,3},{3,2},{4,5},{5,4},{6,7},{7,6},{8,9},{9,8},{10,11... | collective-permute-start | bytes 1671176 | tf_op jit(solution)/shard_map/ppermute | solution.py:366
  70.0 2.0 copy-start.6
  70.0 2.0 collective-permute-start.33
  70.0 15.2 %collective-permute-start.27 = (bf16[272,1024]{1,0:T(8,128)(2,1)}, bf16[272,1024]{1,0:T(8,128)(2,1)S(1)}, u32[]{:S(2)}, u32[]{:S(2)}) collective-permute-start(bf16[272,1024]{1,0:T(8,128)(2,1)} %shard_map.242.refs_1_.refs_12_), channel_id=1, source_target_pairs={{0,4},{4,0},{8,12},{12,8},{1,5},{5,1},{9,13},{13,9},{2,6},{6,2},{1... | collective-permute-start | bytes 1671176 | tf_op jit(solution)/shard_map/ppermute | solution.py:364
  70.0 1.9 copy-start.7
  71.9 0.8 copy-start.8
  81.3 75.5 %collective-permute-start.36 = (bf16[576,1536]{1,0:T(8,128)(2,1)}, bf16[576,1536]{1,0:T(8,128)(2,1)S(1)}, u32[]{:S(2)}, u32[]{:S(2)}) collective-permute-start(bf16[576,1536]{1,0:T(8,128)(2,1)} %get-tuple-element.53.refs_0_), channel_id=1, source_target_pairs={{0,2},{2,0},{1,3},{3,1},{4,6},{6,4},{5,7},{7,5},{8,10},{10,8},{9,1... | collective-permute-start | bytes 5308424 | tf_op jit(solution)/shard_map/ppermute | solution.py:397
  85.2 2.0 copy-start.9
  85.2 2.0 collective-permute-start.28
  85.2 11.1 %collective-permute-start.24 = (bf16[272,1024]{1,0:T(8,128)(2,1)S(1)}, bf16[272,1024]{1,0:T(8,128)(2,1)S(1)}, u32[]{:S(2)}, u32[]{:S(2)}) collective-permute-start(bf16[272,1024]{1,0:T(8,128)(2,1)S(1)} %copy-done), channel_id=1, source_target_pairs={{0,1},{1,0},{2,3},{3,2},{4,5},{5,4},{6,7},{7,6},{8,9},{9,8},{10,11... | collective-permute-start | bytes 1671176 | tf_op jit(solution)/shard_map/ppermute | solution.py:366
  87.2 0.8 copy-start.10
  94.8 47.2 %collective-permute-start.29 = (bf16[288,1536]{1,0:T(8,128)(2,1)}, bf16[288,1536]{1,0:T(8,128)(2,1)S(1)}, u32[]{:S(2)}, u32[]{:S(2)}) collective-permute-start(bf16[288,1536]{1,0:T(8,128)(2,1)} %get-tuple-element.49.refs_0_), channel_id=1, source_target_pairs={{0,2},{2,0},{1,3},{3,1},{4,6},{6,4},{5,7},{7,5},{8,10},{10,8},{9,1... | collective-permute-start | bytes 2654216 | tf_op jit(solution)/shard_map/ppermute | solution.py:397
  96.3 0.8 copy-start.11
  103.9 63.9 %collective-permute-start.25 = (bf16[288,1536]{1,0:T(8,128)(2,1)}, bf16[288,1536]{1,0:T(8,128)(2,1)S(1)}, u32[]{:S(2)}, u32[]{:S(2)}) collective-permute-start(bf16[288,1536]{1,0:T(8,128)(2,1)} %get-tuple-element.45.refs_0_), channel_id=1, source_target_pairs={{0,2},{2,0},{1,3},{3,1},{4,6},{6,4},{5,7},{7,5},{8,10},{10,8},{9,1... | collective-permute-start | bytes 2654216 | tf_op jit(solution)/shard_map/ppermute | solution.py:397
  142.0 0.9 copy-start.3
  149.8 25.9 %collective-permute-start.30 = (bf16[128,1024]{1,0:T(8,128)(2,1)}, bf16[128,1024]{1,0:T(8,128)(2,1)S(1)}, u32[]{:S(2)}, u32[]{:S(2)}) collective-permute-start(bf16[128,1024]{1,0:T(8,128)(2,1)} %get-tuple-element.52), channel_id=1, source_target_pairs={{0,1},{1,0},{2,3},{3,2},{4,5},{5,4},{6,7},{7,6},{8,9},{9,8},{10,11... | collective-permute-start | bytes 786440 | tf_op jit(solution)/shard_map/ppermute | solution.py:422
  156.9 1.2 copy-start.1
  167.2 43.5 %collective-permute-start.37 = (bf16[256,1024]{1,0:T(8,128)(2,1)}, bf16[256,1024]{1,0:T(8,128)(2,1)S(1)}, u32[]{:S(2)}, u32[]{:S(2)}) collective-permute-start(bf16[256,1024]{1,0:T(8,128)(2,1)} %get-tuple-element.56), channel_id=1, source_target_pairs={{0,1},{1,0},{2,3},{3,2},{4,5},{5,4},{6,7},{7,6},{8,9},{9,8},{10,11... | collective-permute-start | bytes 1572872 | tf_op jit(solution)/shard_map/ppermute | solution.py:422
  167.7 0.9 copy-start.2
  168.7 7.0 %copy-start.14 = (bf16[128,1024]{1,0:T(8,128)(2,1)S(1)}, bf16[128,1024]{1,0:T(8,128)(2,1)}, u32[]{:S(2)}) copy-start(bf16[128,1024]{1,0:T(8,128)(2,1)} %get-tuple-element.51) | copy-start | bytes 786436
  168.7 8.0 %copy-start.13 = (bf16[96,1536]{1,0:T(8,128)(2,1)S(1)}, bf16[96,1536]{1,0:T(8,128)(2,1)}, u32[]{:S(2)}) copy-start(bf16[96,1536]{1,0:T(8,128)(2,1)} %get-tuple-element.67) | copy-start | bytes 884740
  175.6 1.1 copy-start.4
  175.6 73.0 %collective-permute-start.26 = (bf16[128,1024]{1,0:T(8,128)(2,1)}, bf16[128,1024]{1,0:T(8,128)(2,1)S(1)}, u32[]{:S(2)}, u32[]{:S(2)}) collective-permute-start(bf16[128,1024]{1,0:T(8,128)(2,1)} %get-tuple-element.48), channel_id=1, source_target_pairs={{0,1},{1,0},{2,3},{3,2},{4,5},{5,4},{6,7},{7,6},{8,9},{9,8},{10,11... | collective-permute-start | bytes 786440 | tf_op jit(solution)/shard_map/ppermute | solution.py:422
  175.8 72.9 %collective-permute-start.31 = (bf16[128,1024]{1,0:T(8,128)(2,1)S(1)}, bf16[128,1024]{1,0:T(8,128)(2,1)S(1)}, u32[]{:S(2)}, u32[]{:S(2)}) collective-permute-start(bf16[128,1024]{1,0:T(8,128)(2,1)S(1)} %add_convert_fusion.3), channel_id=1, source_target_pairs={{0,4},{4,0},{8,12},{12,8},{1,5},{5,1},{9,13},{13,9},{2,6},{6,2},{1... | collective-permute-start | bytes 786440 | tf_op jit(solution)/shard_map/ppermute | solution.py:428
  176.7 34.0 %copy-start.12 = (bf16[256,1024]{1,0:T(8,128)(2,1)S(1)}, bf16[256,1024]{1,0:T(8,128)(2,1)}, u32[]{:S(2)}) copy-start(bf16[256,1024]{1,0:T(8,128)(2,1)} %get-tuple-element.55) | copy-start | bytes 1572868
  177.8 8.5 %collective-permute-start.21 = (bf16[384,1536]{1,0:T(8,128)(2,1)S(1)}, bf16[384,1536]{1,0:T(8,128)(2,1)}, u32[]{:S(2)}, u32[]{:S(2)}) collective-permute-start(bf16[384,1536]{1,0:T(8,128)(2,1)S(1)} %param.10), channel_id=1, source_target_pairs={{12,8},{8,12},{13,9},{9,13},{14,10},{10,14},{15,11},{11,15},{28,24... | collective-permute-start | bytes 3538952 | tf_op jit(solution)/shard_map/cond/branch_10_fun/ppermute | solution.py:304
  179.5 31.1 %collective-permute-start.20 = (bf16[384,1536]{1,0:T(8,128)(2,1)S(1)}, bf16[384,1536]{1,0:T(8,128)(2,1)}, u32[]{:S(2)}, u32[]{:S(2)}) collective-permute-start(bf16[384,1536]{1,0:T(8,128)(2,1)S(1)} %param.10), channel_id=1, source_target_pairs={{4,8},{0,12},{5,9},{1,13},{6,10},{2,14},{7,11},{3,15},{20,24},{16,... | collective-permute-start | bytes 3538952 | tf_op jit(solution)/shard_map/cond/branch_10_fun/ppermute | solution.py:304
  210.8 44.6 %collective-permute-start.38 = (bf16[128,1024]{1,0:T(8,128)(2,1)S(1)}, bf16[128,1024]{1,0:T(8,128)(2,1)S(1)}, u32[]{:S(2)}, u32[]{:S(2)}) collective-permute-start(bf16[128,1024]{1,0:T(8,128)(2,1)S(1)} %get-tuple-element.91), channel_id=1, source_target_pairs={{0,8},{4,12},{8,0},{12,4},{1,9},{5,13},{9,1},{13,5},{2,10},{6,14},... | collective-permute-start | bytes 786440 | tf_op jit(solution)/shard_map/ppermute | solution.py:428
  238.1 17.4 %collective-permute-start.39 = (bf16[128,1024]{1,0:T(8,128)(2,1)S(1)}, bf16[128,1024]{1,0:T(8,128)(2,1)S(1)}, u32[]{:S(2)}, u32[]{:S(2)}) collective-permute-start(bf16[128,1024]{1,0:T(8,128)(2,1)S(1)} %get-tuple-element.92), channel_id=1, source_target_pairs={{0,12},{4,8},{8,4},{12,0},{1,13},{5,9},{9,5},{13,1},{2,14},{6,10},... | collective-permute-start | bytes 786440 | tf_op jit(solution)/shard_map/ppermute | solution.py:428
  238.5 17.0 %copy-start.15 = (bf16[128,1024]{1,0:T(8,128)(2,1)S(1)}, bf16[128,1024]{1,0:T(8,128)(2,1)}, u32[]{:S(2)}) copy-start(bf16[128,1024]{1,0:T(8,128)(2,1)} %get-tuple-element.47) | copy-start | bytes 786436

commit v2 on v0

v2 whole, which is shorter than its diff:
```python
import functools

import jax
import jax.numpy as jnp
from jax import lax
from jax.experimental import pallas as pl
from jax.experimental.pallas import tpu as pltpu
from jax.sharding import PartitionSpec as P

META = 16


def call(body, out_shape, in_specs, out_specs, scratch, **kw):
    return pl.pallas_call(
        body,
        out_shape=out_shape,
        in_specs=in_specs,
        out_specs=out_specs,
        scratch_shapes=scratch,
        compiler_params=pltpu.CompilerParams(vmem_limit_bytes=60 * 1024 * 1024),
        **kw,
    )


WHOLE = pl.BlockSpec(memory_space=pltpu.VMEM)
SCALARS = pl.BlockSpec(memory_space=pltpu.SMEM)
REMAIN = pl.BlockSpec(memory_space=pl.ANY)


def position():
    return lax.axis_index("expert"), lax.axis_index("inner")


def pack_kernel(shadow_count, shadow, tok_ref, grad_ref, ids_ref, gate_ref, out_ref, which_ref):
    rows = tok_ref.shape[0]
    out_ref[0:rows, :] = tok_ref[...]
    out_ref[rows : 2 * rows, :] = grad_ref[...]
    z, core = position()
    ids, gates = ids_ref[...].astype(jnp.float32), gate_ref[...]
    choice = lax.broadcasted_iota(jnp.int32, ids.shape, 0)
    place = (2 * z + core) * rows + lax.broadcasted_iota(jnp.int32, ids.shape, 1) + choice
    place = place.astype(jnp.float32)
    entry = [shadow[j] for j in range(shadow_count)]
    named = [ids == e.astype(jnp.float32) for e in entry]
    copies = jnp.ones(ids.shape, jnp.float32)
    for hit in named:
        copies = copies + jnp.where(hit, 1.0, 0.0)
    halves = place - 2.0 * jnp.floor((place + 0.5) * 0.5)
    thirds = place - 3.0 * jnp.floor((place + 0.5) * (1.0 / 3.0))
    chosen = jnp.where(copies == 2.0, halves, jnp.where(copies == 3.0, thirds, 0.0))
    serving = ids
    for j in range(shadow_count):
        before = jnp.int32(0)
        for i in range(j):
            before = before + jnp.where(entry[i] == entry[j], 1, 0)
        take = named[j] & (chosen == (before + 1).astype(jnp.float32))
        serving = jnp.where(take, float(2 * shadow_count + j), serving)
    high = gates.astype(jnp.bfloat16)
    rest = gates - high.astype(jnp.float32)
    middle = rest.astype(jnp.bfloat16)
    low = (rest - middle.astype(jnp.float32)).astype(jnp.bfloat16)
    block = jnp.concatenate(
        [
            serving,
            high.astype(jnp.float32),
            middle.astype(jnp.float32),
            low.astype(jnp.float32),
            jnp.zeros((META - 8, rows), jnp.float32),
        ],
        axis=0,
    )
    out_ref[2 * rows : 2 * rows + META, :] = jnp.zeros((META, tok_ref.shape[1]), jnp.bfloat16)
    out_ref[2 * rows : 2 * rows + META, 0:rows] = block.astype(jnp.bfloat16)
    which = jnp.int32(0)
    if shadow_count == 4:
        for i, (_, placements) in enumerate(shadow_moves()):
            for owners in placements:
                same = jnp.bool_(True)
                for j in range(4):
                    same = same & (entry[j] // 2 == owners[j])
                which = jnp.where(same, i, which)
    which_ref[0] = which


def routing(meta):
    meta = meta.astype(jnp.float32)
    return meta[0:1], meta[1:2], meta[2:3] + meta[4:5] + meta[6:7], meta[3:4] + meta[5:6] + meta[7:8]


def row_codes(meta, numbers):
    first, second, gate_a, gate_b = meta
    tokens = first.shape[1]
    hit_a, hit_b = first == numbers, second == numbers
    hit = jnp.where(hit_a | hit_b, 1.0, 0.0)
    gate = jnp.where(hit_a, gate_a, 0.0) + jnp.where(hit_b, gate_b, 0.0)
    earlier = lax.broadcasted_iota(jnp.int32, (tokens, tokens), 0) < lax.broadcasted_iota(
        jnp.int32, (tokens, tokens), 1
    )
    rank = jnp.dot(
        hit.astype(jnp.bfloat16),
        jnp.where(earlier, 1.0, 0.0).astype(jnp.bfloat16),
        preferred_element_type=jnp.float32,
    )
    return jnp.where(hit > 0.0, rank, -1.0), gate


def gather_rows(codes, gate, wanted, cap, tok, grad):
    tokens = codes.shape[1]
    row = lax.broadcasted_iota(jnp.int32, (cap, tokens), 0).astype(jnp.float32)
    places, gates = [], []
    for s in wanted:
        place = row == codes[s : s + 1, :]
        gates.append(
            jnp.sum(jnp.where(place, gate[s : s + 1, :], 0.0), axis=1, keepdims=True)
        )
        places.append(jnp.where(place, 1.0, 0.0).astype(jnp.bfloat16))
    place = places[0] if len(places) == 1 else jnp.concatenate(places, axis=0)
    row_gate = gates[0] if len(gates) == 1 else jnp.concatenate(gates, axis=0)
    inputs = jnp.dot(place, tok, preferred_element_type=jnp.float32).astype(jnp.bfloat16)
    grads = jnp.dot(place, grad, preferred_element_type=jnp.float32)
    return place, inputs, (grads * row_gate).astype(jnp.bfloat16)


def held_for(shadow, count):
    z = position()[0]
    near, far = jnp.int32(0), jnp.int32(0)
    for k in range(1, count):
        mine = shadow[z ^ k] // 2 == z
        near = jnp.where(mine & (near == 0), k, near)
        far = jnp.where(mine, k, far)
    found = near > 0
    return tuple(
        (z ^ k, jnp.where(found, shadow[z ^ k] - 2 * z, -1)) for k in (near, far)
    )


def copy_numbers(shadow, count):
    z = position()[0]
    slot = lax.broadcasted_iota(jnp.int32, (8, 1), 0)
    number = jnp.where(slot < 2, 2 * z + slot, jnp.where(slot == 2, 2 * count + z, -1))
    for i, (holder, of) in enumerate(held_for(shadow, count)):
        number = jnp.where(slot == 3 + i, jnp.where(of >= 0, 2 * count + holder, -1), number)
    return number.astype(jnp.float32)


def heavy_loads(meta, count, light):
    holder = lax.broadcasted_iota(jnp.int32, (-(-count // 8) * 8, 1), 0)
    number = jnp.where(holder < count, 2 * count + holder, -1).astype(jnp.float32)
    mine = jnp.where(meta[0] == number, 1.0, 0.0) + jnp.where(meta[1] == number, 1.0, 0.0)
    load = jnp.sum(mine, axis=1, keepdims=True)
    return jnp.sum(jnp.where(load > float(light), 1.0, 0.0), axis=0, keepdims=True)


NT = (((1,), (1,)), ((), ()))
TN = (((0,), (0,)), ((), ()))


class Copies:
    def __init__(self, sems):
        self.sems, self.started = sems, []

    def start(self, src, dst):
        copy = pltpu.make_async_copy(src, dst, self.sems.at[len(self.started)])
        copy.start()
        self.started.append(copy)
        return copy


def blocks_of(size):
    block = min(256, size)
    return block, size // block


def forward_kernel(count, cap, light, split, shadow, load_in, own, sib, *refs):
    weights, load_out, outs, scratch = refs[0:6], refs[6], refs[7 : 11 + split], refs[11 + split :]
    vg, vu, vd, rows_in, rows_out, meta, x_s, g_s, p_s, place_s, sems = scratch
    rows, hidden = rows_in.shape[0] // 2, vg.shape[2]
    copies = Copies(sems)
    loads = []
    for core, src in enumerate((own, sib)):
        at = pl.ds(core * rows, rows)
        loads.append(copies.start(src.at[pl.ds(2 * rows, META), pl.ds(0, rows)], meta.at[:, at]))
        loads.append(copies.start(src.at[pl.ds(0, rows)], rows_in.at[at]))
        loads.append(copies.start(src.at[pl.ds(rows, rows)], rows_out.at[at]))
    for load in loads:
        load.wait()
    ready = {}
    for s in range(3):
        for i, (src, extra, dst) in enumerate(zip(weights[0:3], weights[3:6], (vg, vu, vd))):
            ready[3 * s + i] = copies.start(src.at[s] if s < 2 else extra.at[0], dst.at[s])
    routes = routing(meta[...])
    load_out[...] = load_in[...] + heavy_loads(routes, count, light)
    codes, gate = row_codes(routes, copy_numbers(shadow, count))
    place, x_s[...], g_s[...] = gather_rows(
        codes, gate, range(5), cap, rows_in[...], rows_out[...]
    )
    place_s[...] = place[0 : 3 * cap]
    stores = [copies.start(a, b) for a, b in zip((x_s, g_s, place_s), (outs[0], outs[1], outs[2]))]
    for s in range(3):
        at = slice(s * cap, (s + 1) * cap)
        inputs, grads = x_s[at, :], g_s[at, :]
        ready[3 * s].wait()
        p_s[at, 0:hidden] = jnp.dot(
            inputs, vg[s], preferred_element_type=jnp.float32
        ).astype(jnp.bfloat16)
        ready[3 * s + 1].wait()
        p_s[at, hidden : 2 * hidden] = jnp.dot(
            inputs, vu[s], preferred_element_type=jnp.float32
        ).astype(jnp.bfloat16)
        ready[3 * s + 2].wait()
        p_s[at, 2 * hidden :] = lax.dot_general(
            grads, vd[s], NT, preferred_element_type=jnp.float32
        ).astype(jnp.bfloat16)
        of = pl.ds(s * cap, cap)
        stores.append(copies.start(p_s.at[of], outs[4] if split and s == 2 else outs[3].at[of]))
    for store in stores:
        store.wait()


def choose_kernel(moves, which, load, other, last):
    heavy = jnp.max(load[...] + other[...]) > 0.0
    last[0] = which[0] + jnp.where(heavy, moves, 0)


def activation(partial, hidden):
    full = partial[0].astype(jnp.float32)
    for other in partial[1:]:
        full = full + other.astype(jnp.float32)
    gate, up, down = full[:, 0:hidden], full[:, hidden : 2 * hidden], full[:, 2 * hidden :]
    sig = 1.0 / (1.0 + jnp.exp(-gate))
    swish = gate * sig
    return (
        (down * up * sig * (1.0 + gate * (1.0 - sig))).astype(jnp.bfloat16),
        (down * swish).astype(jnp.bfloat16),
        (swish * up).astype(jnp.bfloat16),
    )


def token_grads(grad_gate, grad_up, place, gate_weight, up_weight):
    route = lax.dot_general(grad_gate, gate_weight, NT, preferred_element_type=jnp.float32)
    route = route + lax.dot_general(grad_up, up_weight, NT, preferred_element_type=jnp.float32)
    return lax.dot_general(
        place, route.astype(jnp.bfloat16), TN, preferred_element_type=jnp.float32
    )


def backward_kernel(parts, split, cap, light, carried, *refs):
    pieces = 2 if split else 1
    partial = [refs[pieces * i : pieces * (i + 1)] for i in range(parts)]
    refs = refs[pieces * parts :]
    place_in, weights, carry, refs = refs[0], refs[1:5], refs[5 : 5 + carried], refs[5 + carried :]
    kinds = 2 if light < cap else 1
    a_out, shadow_outs, own_out, sib_out = refs[0], refs[1 : 1 + kinds], *refs[1 + kinds : 3 + kinds]
    vg, vu, part_s, place_s, a_s, total, own_s, sib_s, sems = refs[3 + kinds :]
    hidden, rows = vg.shape[2], own_s.shape[0]
    copies = Copies(sems)
    loads, ready, stores, ends = [], [], [], [0, 0]
    for s in range(3):
        of = pl.ds(s * cap, cap)
        loads.append([])
        for i, p in enumerate(partial):
            src = p[1] if split and s == 2 else p[0].at[of]
            loads[s].append(copies.start(src, part_s.at[i, of]))
        loads[s].append(copies.start(place_in.at[of], place_s.at[of]))
        for src, extra, dst in zip(weights[0:2], weights[2:4], (vg, vu)):
            ready.append(copies.start(src.at[s] if s < 2 else extra.at[0], dst.at[s]))
    for kind, held in enumerate(carry):
        kind = kind + kinds - carried
        ends[kind] = held.shape[0]
        stores.append(copies.start(held, shadow_outs[kind].at[pl.ds(0, ends[kind])]))
    for s in range(3):
        at, of = slice(s * cap, (s + 1) * cap), pl.ds(s * cap, cap)
        for load in loads[s]:
            load.wait()
        grads = activation([part_s[i, at, :] for i in range(parts)], hidden)
        for i in range(3):
            a_s[at, i * hidden : (i + 1) * hidden] = grads[i]
        if s < 2:
            stores.append(copies.start(a_s.at[of], a_out.at[of]))
        else:
            first = 2 * cap
            for kind, size in enumerate((light, cap - light)[0:kinds]):
                to = shadow_outs[kind].at[pl.ds(ends[kind], size)]
                stores.append(copies.start(a_s.at[pl.ds(first, size)], to))
                first += size
        ready[2 * s].wait()
        ready[2 * s + 1].wait()
        part = token_grads(grads[0], grads[1], place_s[at, :], vg[s], vu[s])
        if s == 0:
            total[...] = part
        elif s == 1:
            total[...] += part
        else:
            part = total[...] + part
            own_s[...] = part[0:rows].astype(jnp.bfloat16)
            sib_s[...] = part[rows : 2 * rows].astype(jnp.bfloat16)
            stores.append(copies.start(own_s, own_out))
            stores.append(copies.start(sib_s, sib_out))
    for store in stores:
        store.wait()


def weights_kernel(count, cap, light, pieces, heavy_from, shadow, which, *refs):
    arrays = sum(n for _, n in pieces)
    owned, whole, near = cap * count, cap * count, light * count
    xs, gs, acts = refs[0:count], refs[count : 2 * count], refs[2 * count : 3 * count]
    refs = refs[3 * count :]
    shadow_acts = refs[0:arrays]
    og, ou, od, x_all, g_all, a_all, og_s, ou_s, od_s, sems, slot_sems = refs[arrays:]
    width, hidden = og_s.shape[1], og_s.shape[2]

    def owned_copies(e):
        copies = []
        for i in range(count):
            to, of = pl.ds(i * cap, cap), pl.ds(pl.multiple_of(e * cap, 16), cap)
            for j, (srcs, dst) in enumerate(((xs, x_all), (gs, g_all), (acts, a_all))):
                sem = sems.at[e * 3 * count + 3 * i + j]
                copies.append(pltpu.make_async_copy(srcs[i].at[of], dst.at[e, to], sem))
        return copies

    for e in range(2):
        for copy in owned_copies(e):
            copy.start()
    heavy = which[0] >= heavy_from
    held = held_for(shadow, count)
    together = held[0][1] == held[1][1]
    after_first = jnp.where(together, jnp.where(heavy, whole, near), 0)

    def slot_copies(slot, act):
        e = jnp.maximum(held[slot][1], 0)
        start = owned if slot == 0 else owned + after_first
        z, found = position()[0], held[slot][1] >= 0
        rest, first = cap - light, (3 + slot) * cap
        plans = []
        for k in range(count):
            part = held[slot][0] ^ z ^ k
            for src, dst in ((xs[k], x_all), (gs[k], g_all)):
                plans.append((found, src.at[pl.ds(first, light)], dst, part * light, light))
                if rest:
                    src = src.at[pl.ds(first + light, rest)]
                    plans.append((found & heavy, src, dst, near + part * rest, rest))
        at, i = 0, 0
        for size, number in pieces:
            for n in range(number):
                when = found if at < near else found & heavy
                if number == count - 1:
                    when = when & ((held[slot][0] ^ z) == n + 1)
                if number == count - 1 or n == slot:
                    plans.append((when, shadow_acts[i], a_all, at, size))
                i += 1
            at += size
        for number, (when, src, dst, at, size) in enumerate(plans):
            to = pl.ds(pl.multiple_of(start + at, 16), size)
            sem = slot_sems.at[slot, number]

            @pl.when(when)
            def _(src=src, dst=dst, to=to, sem=sem):
                act(pltpu.make_async_copy(src, dst.at[e, to], sem))

    def for_slots(act):
        for slot in range(2):
            slot_copies(slot, act)

    for_slots(lambda copy: copy.start())
    f_block, f_blocks = blocks_of(width)
    h_block, h_blocks = blocks_of(hidden)

    def products(e, k):
        for j in range(f_blocks):
            of = slice(j * f_block, (j + 1) * f_block)
            both = lax.dot_general(
                x_all[e, 0:k, of],
                a_all[e, 0:k, 0 : 2 * hidden],
                TN,
                preferred_element_type=jnp.float32,
            ).astype(jnp.bfloat16)
            og_s[e, of, :] = both[:, 0:hidden]
            ou_s[e, of, :] = both[:, hidden:]
        for j in range(h_blocks):
            of = slice(j * h_block, (j + 1) * h_block)
            from_ = slice(2 * hidden + j * h_block, 2 * hidden + (j + 1) * h_block)
            od_s[e, of, :] = lax.dot_general(
                a_all[e, 0:k, from_], g_all[e, 0:k, :], TN, preferred_element_type=jnp.float32
            ).astype(jnp.bfloat16)

    def results(e):
        return [
            pltpu.make_async_copy(src.at[e], dst.at[e], sems.at[e * 3 * count + i])
            for i, (src, dst) in enumerate(((og_s, og), (ou_s, ou), (od_s, od)))
        ]

    def turn(n, _):
        e = jnp.where(held[0][1] == 0, 1 - n, n)
        for copy in owned_copies(e):
            copy.wait()

        @pl.when(n == jnp.where(together, 1, 0))
        def _():
            for_slots(lambda copy: copy.wait())

        first = jnp.where(held[0][1] == e, 1, 0)
        slots = first + jnp.where(held[1][1] == e, 1, 0)

        @pl.when(slots == 0)
        def _():
            products(e, owned)

        for number in (1, 2):
            if near < whole:

                @pl.when((slots == number) & ~heavy)
                def _(number=number):
                    products(e, owned + number * near)

            @pl.when((slots == number) & heavy)
            def _(number=number):
                products(e, owned + number * whole)

        for copy in results(e):
            copy.start()
        return 0

    lax.fori_loop(0, 2, turn, 0)
    for e in range(2):
        for copy in results(e):
            copy.wait()


def shadow_moves():
    moves = {}
    for code in range(256):
        owners = [(code >> (2 * j)) & 3 for j in range(4)]
        if any(owners[j] == j for j in range(4)):
            continue
        if sorted(owners.count(i) for i in range(4)) != [0, 0, 2, 2]:
            continue
        apart = sorted({j ^ owners[j] for j in range(4)})
        if 1 in apart:
            perms = [[(j, j ^ d) for j in range(4)] for d in apart]
        else:
            perms = [[(j, o) for j, o in enumerate(owners) if j ^ o == d] for d in apart]
        key = tuple(tuple(p) for p in perms)
        moves.setdefault(key, []).append(owners)
    return list(moves.items())


def after(value, *others):
    return lax.optimization_barrier((value, *others))[0]


def on_device(
    tokens,
    out_grad,
    expert_ids,
    gate_weights,
    shadow_expert,
    w_gate,
    w_up,
    w_down,
    copy_gate,
    copy_up,
    copy_down,
):
    bf16 = jnp.bfloat16
    rows, width = tokens.shape
    hidden = w_gate.shape[2]
    count, dp_count = lax.axis_size("expert"), lax.axis_size("dp")
    cap = -(-2 * max(2, 3 * rows // (2 * count)) // 16) * 16
    light = -(-2 * cap // 3 // 16) * 16
    swap = [(0, 1), (1, 0)]
    shape = jax.ShapeDtypeStruct

    def to_index(x, k):
        return lax.ppermute(x, "expert", [(i, i ^ k) for i in range(count)])

    def swapped(x):
        return lax.ppermute(x, "inner", swap)

    def forward(load, own, sib, split=0):
        outs = (
            shape((8, 128), jnp.float32),
            shape((5 * cap, width), bf16),
            shape((5 * cap, width), bf16),
            shape((3 * cap, 2 * rows), bf16),
            *[shape((n * cap, 3 * hidden), bf16) for n in ((2, 1) if split else (3,))],
        )
        return call(
            functools.partial(forward_kernel, count, cap, light, split),
            outs,
            [SCALARS, WHOLE] + [REMAIN] * 8,
            (WHOLE,) + (REMAIN,) * (len(outs) - 1),
            [
                pltpu.VMEM((3, width, hidden), bf16),
                pltpu.VMEM((3, width, hidden), bf16),
                pltpu.VMEM((3, hidden, width), bf16),
                pltpu.VMEM((2 * rows, width), bf16),
                pltpu.VMEM((2 * rows, width), bf16),
                pltpu.VMEM((META, 2 * rows), bf16),
                pltpu.VMEM((5 * cap, width), bf16),
                pltpu.VMEM((5 * cap, width), bf16),
                pltpu.VMEM((3 * cap, 3 * hidden), bf16),
                pltpu.VMEM((3 * cap, 2 * rows), bf16),
                pltpu.SemaphoreType.DMA((21,)),
            ],
        )(shadow_expert, load, own, sib, w_gate, w_up, w_down, copy_gate, copy_up, copy_down)

    def exchange(partial):
        if dp_count == 2:
            return [partial, lax.ppermute(partial, "dp", swap)]
        return [lax.psum(partial, "dp")]

    def backward(partials, place, carry=(), near=1, far=1):
        parts, split = len(partials), len(partials[0]) - 1
        outs = [shape((2 * cap, 3 * hidden), bf16), shape((near * light, 3 * hidden), bf16)]
        if light < cap:
            outs.append(shape((far * (cap - light), 3 * hidden), bf16))
        outs += [shape((rows, width), bf16)] * 2
        return call(
            functools.partial(backward_kernel, parts, split, cap, light, len(carry)),
            outs,
            [REMAIN] * ((1 + split) * parts + 5 + len(carry)),
            [REMAIN] * len(outs),
            [
                pltpu.VMEM((3, width, hidden), bf16),
                pltpu.VMEM((3, width, hidden), bf16),
                pltpu.VMEM((parts, 3 * cap, 3 * hidden), bf16),
                pltpu.VMEM((3 * cap, 2 * rows), bf16),
                pltpu.VMEM((3 * cap, 3 * hidden), bf16),
                pltpu.VMEM((2 * rows, width), jnp.float32),
                pltpu.VMEM((rows, width), bf16),
                pltpu.VMEM((rows, width), bf16),
                pltpu.SemaphoreType.DMA((17 + 3 * parts,)),
            ],
        )(*[p for x in partials for p in x], place, w_gate, w_up, copy_gate, copy_up, *carry)

    def give_back(dx_own, dx_sib, k):
        both = dx_own.astype(jnp.float32) + swapped(dx_sib).astype(jnp.float32)
        return to_index(both.astype(bf16), k) if k else both

    def add_up(returned):
        total = returned[0]
        for x in returned[1:]:
            total = total + x.astype(jnp.float32)
        return total.astype(bf16)

    def weight_grads(kept, pieces, which, heavy_from):
        layout = [(p[0].shape[0], len(p)) for p in pieces]
        outs = (
            shape((2, width, hidden), bf16),
            shape((2, width, hidden), bf16),
            shape((2, hidden, width), bf16),
        )
        most = cap * count * 3
        arrays = [
            *[k[0] for k in kept],
            *[k[1] for k in kept],
            *[k[2] for k in kept],
            *[x for p in pieces for x in p],
        ]
        return call(
            functools.partial(weights_kernel, count, cap, light, layout, heavy_from),
            outs,
            [SCALARS, SCALARS] + [REMAIN] * len(arrays),
            (REMAIN,) * 3,
            [
                pltpu.VMEM((2, most, width), bf16),
                pltpu.VMEM((2, most, width), bf16),
                pltpu.VMEM((2, most, 3 * hidden), bf16),
                *[pltpu.VMEM(o.shape, bf16) for o in outs],
                pltpu.SemaphoreType.DMA((6 * count,)),
                pltpu.SemaphoreType.DMA((2, 4 * count + sum(n for _, n in layout))),
            ],
        )(shadow_expert, which, *arrays)

    own, which = call(
        functools.partial(pack_kernel, count),
        (shape((2 * rows + META, width), bf16), shape((1,), jnp.int32)),
        [SCALARS] + [WHOLE] * 4,
        (WHOLE, SCALARS),
        [],
    )(shadow_expert, tokens, out_grad, expert_ids.T, gate_weights.T)
    load = jnp.zeros((8, 128), jnp.float32)
    if count != 4:
        kept, returned, shadow_acts = [], [], []
        for k in range(count):
            here = to_index(own, k) if k else own
            sib = swapped(here)
            load, inputs, grads, place, partial = forward(load, here, sib)
            acts, *shadow_part, dx_own, dx_sib = backward([[p] for p in exchange(partial)], place)
            returned.append(give_back(dx_own, dx_sib, k))
            kept.append((inputs, grads, acts))
            shadow_acts += shadow_part
        whole = lax.all_gather(jnp.concatenate(shadow_acts, axis=0), "expert")
        z = lax.axis_index("expert")
        apart = jnp.arange(count, dtype=jnp.int32) ^ z
        held = shadow_expert // 2 == z
        near = jnp.min(jnp.where(held, apart, count - 1))
        far = jnp.max(jnp.where(held, apart, 0))
        near = lax.dynamic_index_in_dim(whole, z ^ near, 0, keepdims=False)
        far = lax.dynamic_index_in_dim(whole, z ^ far, 0, keepdims=False)
        pieces = [[near, far]]
        return (add_up(returned), *weight_grads(kept, pieces, which, 0))

    moves = [perms for perms, _ in shadow_moves()]

    def everywhere(x):
        two = to_index(x, 2)
        return [to_index(x, 1), two, to_index(two, 1)]

    here1 = to_index(own, 1)
    sib0 = swapped(own)
    load, x0, g0, place0, p0, q0 = forward(load, own, sib0, 1)
    t0 = lax.ppermute(q0, "dp", swap)
    r0 = lax.ppermute(p0, "dp", swap)
    here2 = to_index(after(own, q0), 2)
    sib1 = swapped(after(here1, t0))
    load, x1, g1, place1, p1, q1 = forward(load, here1, sib1, 1)
    p1, q1 = after((p1, q1), r0)
    t1 = lax.ppermute(q1, "dp", swap)
    r1 = lax.ppermute(p1, "dp", swap)
    here3 = to_index(here2, 1)
    a0, near0, far0, dx_own0, dx_sib0 = backward([[p0, q0], [after(r0, p1), t0]], place0)
    sib2 = swapped(after(here2, a0, t1))
    moved0 = everywhere(near0)
    ret0 = give_back(dx_own0, dx_sib0, 0)
    load, x2, g2, place2, p2, q2 = forward(load, here2, sib2, 1)
    p2, q2 = after((p2, q2), r1)
    t2 = lax.ppermute(q2, "dp", swap)
    r2 = lax.ppermute(p2, "dp", swap)
    a1, near1, far01, dx_own1, dx_sib1 = backward(
        [[p1, q1], [after(r1, p2), t1]], place1, (far0,), 1, 2
    )
    sib3 = swapped(after(here3, a1, t2, moved0[0], moved0[1]))
    moved1 = everywhere(near1)
    ret1 = give_back(dx_own1, dx_sib1, 1)
    load, x3, g3, place3, p3, q3 = forward(load, here3, sib3, 1)
    p3, q3 = after((p3, q3), r2, moved0[2], moved1[0], moved1[1])
    t3 = lax.ppermute(q3, "dp", swap)
    r3 = lax.ppermute(p3, "dp", swap)
    last = call(
        functools.partial(choose_kernel, len(moves)),
        shape((1,), jnp.int32),
        [SCALARS, WHOLE, WHOLE],
        SCALARS,
        [],
    )(which, load, lax.ppermute(load, "groups", swap))
    a2, near2, far012, dx_own2, dx_sib2 = backward(
        [[p2, q2], [after(r2, p3), t2]], place2, (far01,), 1, 3
    )
    moved2 = lax.switch(
        which[0],
        [functools.partial(lambda m, x: [lax.ppermute(x, "expert", p) for p in m], m) for m in moves],
        after(near2, t3, moved1[2]),
    )
    ret2 = give_back(dx_own2, dx_sib2, 2)
    r3 = after(r3, ret1, moved2)
    a3, near3, rest, dx_own3, dx_sib3 = backward([[p3, q3], [r3, t3]], place3, (far012,), 1, 4)
    near3 = after(near3, ret2)

    def light_branch(perms, x, more):
        return [[lax.ppermute(x, "expert", p), more] for p in perms]

    def heavy_branch(perms, x, more):
        return [[lax.ppermute(y, "expert", p) for y in (x, more)] for p in perms]

    moved3 = lax.switch(
        last[0],
        [functools.partial(f, m) for f in (light_branch, heavy_branch) for m in moves],
        near3,
        rest,
    )
    ret3 = give_back(dx_own3, dx_sib3, 3)
    pieces = [moved0, moved1, moved2, [m[0] for m in moved3], [m[1] for m in moved3]]
    kept = [(x0, g0, a0), (x1, g1, a1), (x2, g2, a2), (x3, g3, a3)]
    grads = weight_grads(kept, pieces, last, len(moves))
    return (add_up([ret0, ret1, ret2, ret3]), *grads)


def solution(mesh):
    return jax.shard_map(
        on_device,
        mesh=mesh,
        in_specs=(
            P(("groups", "expert", "inner"), "dp"),
            P(("groups", "expert", "inner"), "dp"),
            P(("groups", "expert", "inner"), None),
            P(("groups", "expert", "inner"), None),
            P(),
            P("expert", "dp", "inner"),
            P("expert", "dp", "inner"),
            P("expert", "inner", "dp"),
            P("expert", "dp", "inner"),
            P("expert", "dp", "inner"),
            P("expert", "inner", "dp"),
        ),
        out_specs=(
            P(("groups", "expert", "inner"), "dp"),
            P(("groups", "expert"), "dp", "inner"),
            P(("groups", "expert"), "dp", "inner"),
            P(("groups", "expert"), "inner", "dp"),
        ),
        check_vma=False,
    )
```

time: 646 us -> 179 us (0.28)
  waiting for transfers between devices: 407 us -> 53.4 us
  local copies, waits for them, and re-layouts: 107 us -> 7.01 us
  Pallas kernels: 0 us -> 76.6 us
  other arithmetic: 53.9 us -> 2.07 us
  matrix products: 31.1 us -> 0 us
  between operations: 14.7 us -> 2.29 us
  starting transfers between devices: 26 us -> 36.6 us
    all_to_all x5 -> x0, waiting for transfers between devices: 313 us -> none  [the longest x1 132 us: on_device(): lax.all_to_all(per_expert.reshape(expert_count, 2, piece_width).astype(jn...]
    psum x1 -> x0, waiting for transfers between devices: 93.4 us -> none  [on_device(): lax.psum(partial_sums.astype(jnp.bfloat16), 'dp').astype(jnp.float32)]
    pallas_call x0 -> x11, Pallas kernels: none -> 76.6 us  [the longest x4 35 us: forward(): call(functools.partial(forward_kernel, count, cap, light, split), outs, [...]
    ppermute x0 -> x33, waiting for transfers between devices: none -> 53.4 us  [the longest x12 26 us: to_index(): return lax.ppermute(x, 'expert', [(i, i ^ k) for i in range(count)])]
    ppermute x0 -> x33, starting transfers between devices: none -> 36.6 us  [the longest x12 20.8 us: to_index(): return lax.ppermute(x, 'expert', [(i, i ^ k) for i in range(count)])]
    dot_general x12 -> x0, matrix products: 31.1 us -> none  [the longest x1 7.91 us: on_device(): jnp.dot(indicator.T, spread_pieces.astype(jnp.float32), precision=lax.Pre...]
    convert_element_type x5 -> x0, local copies, waits for them, and re-layouts: 29.9 us -> none  [the longest x1 20.6 us: on_device(): per_expert.reshape(expert_count, 2, piece_width).astype(jnp.bfloat16)]
    all_to_all x5 -> x0, starting transfers between devices: 25.9 us -> none  [the longest x1 6.46 us: on_device(): lax.all_to_all(duplicate(rows_in), ('expert', 'inner'), split_axis=1, con...]
  transfers between devices with their start and end apart: 6 -> 33, of which waited for: 6 -> 14; matrix products, arithmetic and copies ran while one was open for 9% -> 2% of each run, Pallas kernels for 0% -> 42%
where the time goes in v2:
time: 179 us; the launch traced here: 178 us
  Pallas kernels  76.6 us (43%)
  waiting for transfers between devices  53.4 us (30%)
  starting transfers between devices  36.6 us (20%)
  local copies, waits for them, and re-layouts  7.01 us (4%)
  between operations  2.29 us (1%)
  other arithmetic  2.07 us (1%)
    pallas_call x4, Pallas kernels, forward(): call(functools.partial(forward_kernel, count, cap, light, split), outs, [...  35 us
    ppermute x12, waiting for transfers between devices, to_index(): return lax.ppermute(x, 'expert', [(i, i ^ k) for i in range(count)])  26 us
    pallas_call x4, Pallas kernels, backward(): call(functools.partial(backward_kernel, parts, split, cap, light, len(car...  24.9 us
    ppermute x12, starting transfers between devices, to_index(): return lax.ppermute(x, 'expert', [(i, i ^ k) for i in range(count)])  20.8 us
    pallas_call x1, Pallas kernels, weight_grads(): call(functools.partial(weights_kernel, count, cap, light, layout, heavy_f...  12.8 us
    ppermute x2, waiting for transfers between devices, on_device(): lax.ppermute(x, 'expert', p)  9.28 us
    ppermute x2, waiting for transfers between devices, light_branch(): return [[lax.ppermute(x, 'expert', p), more] for p in perms]  8.61 us
    ppermute x1, waiting for transfers between devices, on_device(): t0 = lax.ppermute(q0, 'dp', swap)  6.29 us
  transfers between devices with their start and end apart: 33, of which 14 were waited for; matrix products, arithmetic and copies ran while one was open for 2% of the time, Pallas kernels for 42%

profile of v2, /device:TPU:0, one launch (start us, length us, event | category | flops | bytes accessed | tf_op | source)
XLA Modules:
  0.0 177.9 jit_solution(15029813492628811441)
XLA Ops:
  0.6 1.9 %shard_map.138 = (bf16[272,1024]{1,0:T(8,128)(2,1)}, s32[1]{0:T(128)}) custom-call(s32[4]{0:T(128)} %shadow.11, bf16[128,1024]{1,0:T(8,128)(2,1)} %tok_ref.1, bf16[128,1024]{1,0:T(8,128)(2,1)} %grad_ref.1, s32[2,128]{1,0:T(2,128)} %bitcast.4, f32[2,128]{1,0:T(2,128)} %bitcast.5), custom_call_target="tpu_custom_call" | custom-call | tf_op jit(solution)/shard_map/pallas_call | solution.py:575
  3.1 2.6 %collective-permute-start.50 = (bf16[272,1024]{1,0:T(8,128)(2,1)}, bf16[272,1024]{1,0:T(8,128)(2,1)S(1)}, u32[]{:S(2)}, u32[]{:S(2)}) collective-permute-start(bf16[272,1024]{1,0:T(8,128)(2,1)} %get-tuple-element.167.own), channel_id=1, source_target_pairs={{0,4},{4,0},{8,12},{12,8},{1,5},{5,1},{9,13},{13,9},{2,6},{6,2},{1... | collective-permute-start | bytes 1671176 | tf_op jit(solution)/shard_map/ppermute | solution.py:474
  6.5 8.8 %shard_map.139 = (f32[8,128]{1,0:T(8,128)}, bf16[480,1024]{1,0:T(8,128)(2,1)}, bf16[480,1024]{1,0:T(8,128)(2,1)}, bf16[288,256]{1,0:T(8,128)(2,1)}, bf16[192,1536]{1,0:T(8,128)(2,1)}, /*index=5*/bf16[96,1536]{1,0:T(8,128)(2,1)}) custom-call(s32[4]{0:T(128)} %shadow.11, f32[8,128]{1,0:T(8,128)} %broadcast_in_dim.3.load_in, ...), custom_call_target="tpu_custom_call" | custom-call | tf_op jit(solution)/shard_map/pallas_call | solution.py:487
  15.3 2.1 %collective-permute-start.51 = (bf16[96,1536]{1,0:T(8,128)(2,1)}, bf16[96,1536]{1,0:T(8,128)(2,1)S(1)}, u32[]{:S(2)}, u32[]{:S(2)}) collective-permute-start(bf16[96,1536]{1,0:T(8,128)(2,1)} %get-tuple-element.155.refs_1_), channel_id=1, source_target_pairs={{0,2},{2,0},{1,3},{3,1},{4,6},{6,4},{5,7},{7,5},{8,10},{10,8},{9,1... | collective-permute-start | bytes 884744 | tf_op jit(solution)/shard_map/ppermute | solution.py:613
  17.5 1.7 collective-permute-done.50.own
  19.1 6.3 %collective-permute-done.51.refs_3_ = bf16[96,1536]{1,0:T(8,128)(2,1)S(1)} collective-permute-done((bf16[96,1536]{1,0:T(8,128)(2,1)}, bf16[96,1536]{1,0:T(8,128)(2,1)S(1)}, u32[]{:S(2)}, u32[]{:S(2)}) %collective-permute-start.51) | collective-permute-done | bytes 294944 | tf_op jit(solution)/shard_map/ppermute | solution.py:613
  25.4 3.2 %collective-permute-start.55 = (bf16[272,1024]{1,0:T(8,128)(2,1)S(1)}, bf16[272,1024]{1,0:T(8,128)(2,1)S(1)}, u32[]{:S(2)}, u32[]{:S(2)}) collective-permute-start(bf16[272,1024]{1,0:T(8,128)(2,1)S(1)} %copy-done.7), channel_id=1, source_target_pairs={{0,8},{4,12},{8,0},{12,4},{1,9},{5,13},{9,1},{13,5},{2,10},{6,14},... | collective-permute-start | bytes 1671176 | tf_op jit(solution)/shard_map/ppermute | solution.py:474
  28.6 0.9 copy-done.11
  29.5 8.7 %shard_map.140 = (f32[8,128]{1,0:T(8,128)}, bf16[480,1024]{1,0:T(8,128)(2,1)}, bf16[480,1024]{1,0:T(8,128)(2,1)}, bf16[288,256]{1,0:T(8,128)(2,1)}, bf16[192,1536]{1,0:T(8,128)(2,1)}, /*index=5*/bf16[96,1536]{1,0:T(8,128)(2,1)}) custom-call(s32[4]{0:T(128)} %shadow.11, f32[8,128]{1,0:T(8,128)} %get-tuple-element.156.load_in, bf16[272,1024]{1,0:T(8,128)(2,1)} %copy-done.8, ...), custom_call_target="tpu_custom_call" | custom-call | tf_op jit(solution)/shard_map/pallas_call | solution.py:487
  38.2 1.6 collective-permute-start.56
  40.3 5.7 %shard_map.141 = (bf16[192,1536]{1,0:T(8,128)(2,1)}, bf16[64,1536]{1,0:T(8,128)(2,1)}, bf16[32,1536]{1,0:T(8,128)(2,1)}, bf16[128,1024]{1,0:T(8,128)(2,1)}, bf16[128,1024]{1,0:T(8,128)(2,1)}) custom-call(bf16[192,1536]{1,0:T(8,128)(2,1)} %get-tuple-element.154.refs_0_, bf16[96,1536]{1,0:T(8,128)(2,1)} %get-tuple-element.155.refs_1_, ...), custom_call_target="tpu_custom_call" | custom-call | tf_op jit(solution)/shard_map/pallas_call | solution.py:518
  46.0 7.8 %collective-permute-done.55.own = bf16[272,1024]{1,0:T(8,128)(2,1)S(1)} collective-permute-done((bf16[272,1024]{1,0:T(8,128)(2,1)S(1)}, bf16[272,1024]{1,0:T(8,128)(2,1)S(1)}, u32[]{:S(2)}, u32[]{:S(2)}) %collective-permute-start.55) | collective-permute-done | bytes 557088 | tf_op jit(solution)/shard_map/ppermute | solution.py:474
  54.6 1.2 collective-permute-done.57.sib
  55.8 0.9 copy-done.12
  56.7 8.8 %shard_map.142 = (f32[8,128]{1,0:T(8,128)}, bf16[480,1024]{1,0:T(8,128)(2,1)}, bf16[480,1024]{1,0:T(8,128)(2,1)}, bf16[288,256]{1,0:T(8,128)(2,1)}, bf16[192,1536]{1,0:T(8,128)(2,1)}, /*index=5*/bf16[96,1536]{1,0:T(8,128)(2,1)}) custom-call(s32[4]{0:T(128)} %shadow.11, f32[8,128]{1,0:T(8,128)} %get-tuple-element.166.load_in, bf16[272,1024]{1,0:T(8,128)(2,1)} %copy-done.5, ...), custom_call_target="tpu_custom_call" | custom-call | tf_op jit(solution)/shard_map/pallas_call | solution.py:487
  65.5 1.6 collective-permute-start.62
  67.1 2.2 %collective-permute-start.64 = (bf16[64,1536]{1,0:T(8,128)(2,1)S(1)}, bf16[64,1536]{1,0:T(8,128)(2,1)S(1)}, u32[]{:S(2)}, u32[]{:S(2)}) collective-permute-start(bf16[64,1536]{1,0:T(8,128)(2,1)S(1)} %copy-done.30), channel_id=1, source_target_pairs={{0,8},{4,12},{8,0},{12,4},{1,9},{5,13},{9,1},{13,5},{2,10},{6,14},... | collective-permute-start | bytes 589832 | tf_op jit(solution)/shard_map/ppermute | solution.py:474
  69.4 1.9 %collective-permute-start.63 = (bf16[64,1536]{1,0:T(8,128)(2,1)S(1)}, bf16[64,1536]{1,0:T(8,128)(2,1)S(1)}, u32[]{:S(2)}, u32[]{:S(2)}) collective-permute-start(bf16[64,1536]{1,0:T(8,128)(2,1)S(1)} %copy-done.30), channel_id=1, source_target_pairs={{0,4},{4,0},{8,12},{12,8},{1,5},{5,1},{9,13},{13,9},{2,6},{6,2},{1... | collective-permute-start | bytes 589832 | tf_op jit(solution)/shard_map/ppermute | solution.py:474
  71.2 5.8 %shard_map.143 = (bf16[192,1536]{1,0:T(8,128)(2,1)}, bf16[64,1536]{1,0:T(8,128)(2,1)}, bf16[64,1536]{1,0:T(8,128)(2,1)}, bf16[128,1024]{1,0:T(8,128)(2,1)}, bf16[128,1024]{1,0:T(8,128)(2,1)}) custom-call(bf16[192,1536]{1,0:T(8,128)(2,1)} %get-tuple-element.160.refs_0_, bf16[96,1536]{1,0:T(8,128)(2,1)} %get-tuple-element.165.refs_1_, ...), custom_call_target="tpu_custom_call" | custom-call | tf_op jit(solution)/shard_map/pallas_call | solution.py:518
  77.0 2.0 %collective-permute-done.64.refs_13_ = bf16[64,1536]{1,0:T(8,128)(2,1)S(1)} collective-permute-done((bf16[64,1536]{1,0:T(8,128)(2,1)S(1)}, bf16[64,1536]{1,0:T(8,128)(2,1)S(1)}, u32[]{:S(2)}, u32[]{:S(2)}) %collective-permute-start.64) | collective-permute-done | bytes 196640 | tf_op jit(solution)/shard_map/ppermute | solution.py:474
  79.7 1.3 collective-permute-start.66
  81.0 2.3 %collective-permute-start.68 = (bf16[64,1536]{1,0:T(8,128)(2,1)}, bf16[64,1536]{1,0:T(8,128)(2,1)S(1)}, u32[]{:S(2)}, u32[]{:S(2)}) collective-permute-start(bf16[64,1536]{1,0:T(8,128)(2,1)} %get-tuple-element.185), channel_id=1, source_target_pairs={{0,8},{4,12},{8,0},{12,4},{1,9},{5,13},{9,1},{13,5},{2,10},{6,14},... | collective-permute-start | bytes 589832 | tf_op jit(solution)/shard_map/ppermute | solution.py:474
  83.5 0.8 copy-done.9
  84.3 8.7 %shard_map.144 = (f32[8,128]{1,0:T(8,128)}, bf16[480,1024]{1,0:T(8,128)(2,1)}, bf16[480,1024]{1,0:T(8,128)(2,1)}, bf16[288,256]{1,0:T(8,128)(2,1)}, bf16[192,1536]{1,0:T(8,128)(2,1)}, /*index=5*/bf16[96,1536]{1,0:T(8,128)(2,1)}) custom-call(s32[4]{0:T(128)} %shadow.11, f32[8,128]{1,0:T(8,128)} %get-tuple-element.179.load_in, bf16[272,1024]{1,0:T(8,128)(2,1)} %copy-done.6, ...), custom_call_target="tpu_custom_call" | custom-call | tf_op jit(solution)/shard_map/pallas_call | solution.py:487
  93.1 1.9 %collective-permute-done.67.refs_15_ = bf16[64,1536]{1,0:T(8,128)(2,1)S(1)} collective-permute-done((bf16[64,1536]{1,0:T(8,128)(2,1)}, bf16[64,1536]{1,0:T(8,128)(2,1)S(1)}, u32[]{:S(2)}, u32[]{:S(2)}) %collective-permute-start.67) | collective-permute-done | bytes 196640 | tf_op jit(solution)/shard_map/ppermute | solution.py:474
  95.8 1.6 collective-permute-start.71
  97.4 7.3 %shard_map.145 = (bf16[192,1536]{1,0:T(8,128)(2,1)}, bf16[64,1536]{1,0:T(8,128)(2,1)S(1)}, bf16[96,1536]{1,0:T(8,128)(2,1)}, bf16[128,1024]{1,0:T(8,128)(2,1)}, bf16[128,1024]{1,0:T(8,128)(2,1)}) custom-call(bf16[192,1536]{1,0:T(8,128)(2,1)} %get-tuple-element.172.refs_0_, bf16[96,1536]{1,0:T(8,128)(2,1)} %get-tuple-element.178.refs_1_, ...), custom_call_target="tpu_custom_call" | custom-call | tf_op jit(solution)/shard_map/pallas_call | solution.py:518
  105.3 1.4 collective-permute-start.59
  108.2 1.0 add_convert_fusion.2
  109.2 2.0 %collective-permute-start.70 = (bf16[128,1024]{1,0:T(8,128)(2,1)S(1)}, bf16[128,1024]{1,0:T(8,128)(2,1)S(1)}, u32[]{:S(2)}, u32[]{:S(2)}) collective-permute-start(bf16[128,1024]{1,0:T(8,128)(2,1)S(1)} %add_convert_fusion.2), channel_id=1, source_target_pairs={{0,8},{4,12},{8,0},{12,4},{1,9},{5,13},{9,1},{13,5},{2,10},{6,14},... | collective-permute-start | bytes 786440 | tf_op jit(solution)/shard_map/ppermute | solution.py:474
  111.2 12.4 %collective-permute-done.73.refs_17_ = bf16[64,1536]{1,0:T(8,128)(2,1)S(1)} collective-permute-done((bf16[64,1536]{1,0:T(8,128)(2,1)S(1)}, bf16[64,1536]{1,0:T(8,128)(2,1)S(1)}, u32[]{:S(2)}, u32[]{:S(2)}) %collective-permute-start.73) | collective-permute-done | bytes 196640 | tf_op jit(solution)/shard_map/ppermute | solution.py:474
  123.6 12.4 %conditional.2 = (bf16[64,1536]{1,0:T(8,128)(2,1)}, bf16[64,1536]{1,0:T(8,128)(2,1)}) conditional(s32[]{:T(128)} %bitcast.2, bf16[64,1536]{1,0:T(8,128)(2,1)S(1)} %get-tuple-element.195, bf16[64,1536]{1,0:T(8,128)(2,1)S(1)} %get-tuple-element.195, bf16[64,1536]{1,0:T(8,128)(2,1)S(1)} %get-tuple-element.195, ...), branch_computations={%region_0.0_spmd, %region_1.0_spmd, %region_2.0_spmd, %region_3.0_... | conditional | bytes 1572960 | solution.py:650
  123.6 3.1 %collective-permute-start.5 = (bf16[64,1536]{1,0:T(8,128)(2,1)S(1)}, bf16[64,1536]{1,0:T(8,128)(2,1)}, u32[]{:S(2)}, u32[]{:S(2)}) collective-permute-start(bf16[64,1536]{1,0:T(8,128)(2,1)S(1)} %param.2), channel_id=1, source_target_pairs={{0,12},{4,8},{8,4},{12,0},{1,13},{5,9},{9,5},{13,1},{2,14},{6,10},... | collective-permute-start | bytes 589832 | tf_op jit(solution)/shard_map/cond/branch_2_fun/ppermute | solution.py:652
  126.8 6.7 %collective-permute-done.5 = bf16[64,1536]{1,0:T(8,128)(2,1)} collective-permute-done((bf16[64,1536]{1,0:T(8,128)(2,1)S(1)}, bf16[64,1536]{1,0:T(8,128)(2,1)}, u32[]{:S(2)}, u32[]{:S(2)}) %collective-permute-start.5) | collective-permute-done | bytes 196640 | tf_op jit(solution)/shard_map/cond/branch_2_fun/ppermute | solution.py:652
  133.4 2.6 %collective-permute-done.4 = bf16[64,1536]{1,0:T(8,128)(2,1)} collective-permute-done((bf16[64,1536]{1,0:T(8,128)(2,1)S(1)}, bf16[64,1536]{1,0:T(8,128)(2,1)}, u32[]{:S(2)}, u32[]{:S(2)}) %collective-permute-start.4) | collective-permute-done | bytes 196640 | tf_op jit(solution)/shard_map/cond/branch_2_fun/ppermute | solution.py:652
  136.1 0.8 copy-done
  136.9 6.1 %shard_map.146 = (bf16[192,1536]{1,0:T(8,128)(2,1)}, bf16[64,1536]{1,0:T(8,128)(2,1)S(1)}, bf16[128,1536]{1,0:T(8,128)(2,1)S(1)}, bf16[128,1024]{1,0:T(8,128)(2,1)}, bf16[128,1024]{1,0:T(8,128)(2,1)}) custom-call(bf16[192,1536]{1,0:T(8,128)(2,1)} %get-tuple-element.186.refs_0_, bf16[96,1536]{1,0:T(8,128)(2,1)} %get-tuple-element.192.refs_1_, ...), custom_call_target="tpu_custom_call" | custom-call | tf_op jit(solution)/shard_map/pallas_call | solution.py:518
  143.1 1.7 collective-permute-start.76
  144.8 2.0 %collective-permute-done.76.other = f32[8,128]{1,0:T(8,128)S(1)} collective-permute-done((f32[8,128]{1,0:T(8,128)S(1)}, f32[8,128]{1,0:T(8,128)S(1)}, u32[]{:S(2)}, u32[]{:S(2)}) %collective-permute-start.76) | collective-permute-done | bytes 4128 | tf_op jit(solution)/shard_map/ppermute | solution.py:646
  147.4 2.0 %shard_map.147.which = s32[1]{0:T(128)} custom-call(s32[1]{0:T(128)} %get-tuple-element.193.which, f32[8,128]{1,0:T(8,128)} %get-tuple-element.203.load, f32[8,128]{1,0:T(8,128)} %copy-done.28), custom_call_target="tpu_custom_call" | custom-call | tf_op jit(solution)/shard_map/pallas_call | solution.py:640
  150.0 11.9 %conditional.3 = (bf16[64,1536]{1,0:T(8,128)(2,1)}, bf16[128,1536]{1,0:T(8,128)(2,1)}, bf16[64,1536]{1,0:T(8,128)(2,1)}, bf16[128,1536]{1,0:T(8,128)(2,1)}) conditional(s32[]{:T(128)} %bitcast.3, (bf16[64,1536]{1,0:T(8,128)(2,1)S(1)}, bf16[128,1536]{1,0:T(8,128)(2,1)S(1)}) %tuple.106, ...), branch_computations={%region_6.0_spmd, %region_7.0_spmd, %region_8.0_spmd, %region_9.0_... | conditional | bytes 4718784 | solution.py:666
  150.1 1.7 collective-permute-start.17
  151.8 0.8 copy.36
  153.3 6.6 %collective-permute-done.17 = bf16[64,1536]{1,0:T(8,128)(2,1)} collective-permute-done((bf16[64,1536]{1,0:T(8,128)(2,1)S(1)}, bf16[64,1536]{1,0:T(8,128)(2,1)}, u32[]{:S(2)}, u32[]{:S(2)}) %collective-permute-start.17) | collective-permute-done | bytes 196640 | tf_op jit(solution)/shard_map/cond/branch_2_fun/ppermute | solution.py:661
  159.9 2.0 %collective-permute-done.16 = bf16[64,1536]{1,0:T(8,128)(2,1)} collective-permute-done((bf16[64,1536]{1,0:T(8,128)(2,1)S(1)}, bf16[64,1536]{1,0:T(8,128)(2,1)}, u32[]{:S(2)}, u32[]{:S(2)}) %collective-permute-start.16) | collective-permute-done | bytes 196640 | tf_op jit(solution)/shard_map/cond/branch_2_fun/ppermute | solution.py:661
  162.0 2.2 %collective-permute-start.75 = (bf16[128,1024]{1,0:T(8,128)(2,1)S(1)}, bf16[128,1024]{1,0:T(8,128)(2,1)S(1)}, u32[]{:S(2)}, u32[]{:S(2)}) collective-permute-start(bf16[128,1024]{1,0:T(8,128)(2,1)S(1)} %add_convert_fusion.1), channel_id=1, source_target_pairs={{0,12},{4,8},{8,4},{12,0},{1,13},{5,9},{9,5},{13,1},{2,14},{6,10},... | collective-permute-start | bytes 786440 | tf_op jit(solution)/shard_map/ppermute | solution.py:474
  164.2 12.8 %shard_map.148 = (bf16[2,1024,512]{2,1,0:T(8,128)(2,1)}, bf16[2,1024,512]{2,1,0:T(8,128)(2,1)}, bf16[2,512,1024]{2,1,0:T(8,128)(2,1)}) custom-call(s32[4]{0:T(128)} %shadow.11, s32[1]{0:T(128)} %shard_map.147.which, bf16[480,1024]{1,0:T(8,128)(2,1)} %get-tuple-element.204.refs_0_, bf16[480,1024]{1,0:T(8,128)(2,1)} %get-tuple-element.205.refs_1_, ...), custom_call_target="tpu_custom_call" | custom-call | tf_op jit(solution)/shard_map/pallas_call | solution.py:560
  177.0 0.9 add_convert_fusion
  (100 shorter events, 7.3 us)
Async XLA Ops:
  2.5 3.2 %collective-permute-start.48 = (bf16[272,1024]{1,0:T(8,128)(2,1)}, bf16[272,1024]{1,0:T(8,128)(2,1)S(1)}, u32[]{:S(2)}, u32[]{:S(2)}) collective-permute-start(bf16[272,1024]{1,0:T(8,128)(2,1)} %get-tuple-element.167.own), channel_id=1, source_target_pairs={{0,1},{1,0},{2,3},{3,2},{4,5},{5,4},{6,7},{7,6},{8,9},{9,8},{10,11... | collective-permute-start | bytes 1671176 | tf_op jit(solution)/shard_map/ppermute | solution.py:477
  3.1 16.1 %collective-permute-start.50 = (bf16[272,1024]{1,0:T(8,128)(2,1)}, bf16[272,1024]{1,0:T(8,128)(2,1)S(1)}, u32[]{:S(2)}, u32[]{:S(2)}) collective-permute-start(bf16[272,1024]{1,0:T(8,128)(2,1)} %get-tuple-element.167.own), channel_id=1, source_target_pairs={{0,4},{4,0},{8,12},{12,8},{1,5},{5,1},{9,13},{13,9},{2,6},{6,2},{1... | collective-permute-start | bytes 1671176 | tf_op jit(solution)/shard_map/ppermute | solution.py:474
  6.5 18.9 %copy-start.7 = (bf16[272,1024]{1,0:T(8,128)(2,1)S(1)}, bf16[272,1024]{1,0:T(8,128)(2,1)}, u32[]{:S(2)}) copy-start(bf16[272,1024]{1,0:T(8,128)(2,1)} %get-tuple-element.167.own) | copy-start | bytes 1671172
  15.3 10.1 %collective-permute-start.51 = (bf16[96,1536]{1,0:T(8,128)(2,1)}, bf16[96,1536]{1,0:T(8,128)(2,1)S(1)}, u32[]{:S(2)}, u32[]{:S(2)}) collective-permute-start(bf16[96,1536]{1,0:T(8,128)(2,1)} %get-tuple-element.155.refs_1_), channel_id=1, source_target_pairs={{0,2},{2,0},{1,3},{3,1},{4,6},{6,4},{5,7},{7,5},{8,10},{10,8},{9,1... | collective-permute-start | bytes 884744 | tf_op jit(solution)/shard_map/ppermute | solution.py:613
  17.4 20.8 %collective-permute-start.49 = (bf16[192,1536]{1,0:T(8,128)(2,1)}, bf16[192,1536]{1,0:T(8,128)(2,1)S(1)}, u32[]{:S(2)}, u32[]{:S(2)}) collective-permute-start(bf16[192,1536]{1,0:T(8,128)(2,1)} %get-tuple-element.154.refs_0_), channel_id=1, source_target_pairs={{0,2},{2,0},{1,3},{3,1},{4,6},{6,4},{5,7},{7,5},{8,10},{10,8},{9,1... | collective-permute-start | bytes 1769480 | tf_op jit(solution)/shard_map/ppermute | solution.py:614
  19.1 9.5 %copy-start.8 = (bf16[272,1024]{1,0:T(8,128)(2,1)}, bf16[272,1024]{1,0:T(8,128)(2,1)S(1)}, u32[]{:S(2)}) copy-start(bf16[272,1024]{1,0:T(8,128)(2,1)S(1)} %collective-permute-done.50.own) | copy-start | bytes 1671172
  25.4 14.9 %copy-start.17 = (bf16[96,1536]{1,0:T(8,128)(2,1)}, bf16[96,1536]{1,0:T(8,128)(2,1)S(1)}, u32[]{:S(2)}) copy-start(bf16[96,1536]{1,0:T(8,128)(2,1)S(1)} %collective-permute-done.51.refs_3_) | copy-start | bytes 884740
  25.4 3.2 %collective-permute-start.52 = (bf16[272,1024]{1,0:T(8,128)(2,1)S(1)}, bf16[272,1024]{1,0:T(8,128)(2,1)S(1)}, u32[]{:S(2)}, u32[]{:S(2)}) collective-permute-start(bf16[272,1024]{1,0:T(8,128)(2,1)S(1)} %collective-permute-done.50.own), channel_id=1, source_target_pairs={{0,1},{1,0},{2,3},{3,2},{4,5},{5,4},{6,7},{7,6},{8,9},{9,8},{10,11... | collective-permute-start | bytes 1671176 | tf_op jit(solution)/shard_map/ppermute | solution.py:477
  25.4 28.4 %collective-permute-start.55 = (bf16[272,1024]{1,0:T(8,128)(2,1)S(1)}, bf16[272,1024]{1,0:T(8,128)(2,1)S(1)}, u32[]{:S(2)}, u32[]{:S(2)}) collective-permute-start(bf16[272,1024]{1,0:T(8,128)(2,1)S(1)} %copy-done.7), channel_id=1, source_target_pairs={{0,8},{4,12},{8,0},{12,4},{1,9},{5,13},{9,1},{13,5},{2,10},{6,14},... | collective-permute-start | bytes 1671176 | tf_op jit(solution)/shard_map/ppermute | solution.py:474
  38.2 15.6 %collective-permute-start.56 = (bf16[96,1536]{1,0:T(8,128)(2,1)}, bf16[96,1536]{1,0:T(8,128)(2,1)S(1)}, u32[]{:S(2)}, u32[]{:S(2)}) collective-permute-start(bf16[96,1536]{1,0:T(8,128)(2,1)} %get-tuple-element.165.refs_1_), channel_id=1, source_target_pairs={{0,2},{2,0},{1,3},{3,1},{4,6},{6,4},{5,7},{7,5},{8,10},{10,8},{9,1... | collective-permute-start | bytes 884744 | tf_op jit(solution)/shard_map/ppermute | solution.py:619
  39.8 25.7 %collective-permute-start.54 = (bf16[192,1536]{1,0:T(8,128)(2,1)}, bf16[192,1536]{1,0:T(8,128)(2,1)S(1)}, u32[]{:S(2)}, u32[]{:S(2)}) collective-permute-start(bf16[192,1536]{1,0:T(8,128)(2,1)} %get-tuple-element.160.refs_0_), channel_id=1, source_target_pairs={{0,2},{2,0},{1,3},{3,1},{4,6},{6,4},{5,7},{7,5},{8,10},{10,8},{9,1... | collective-permute-start | bytes 1769480 | tf_op jit(solution)/shard_map/ppermute | solution.py:620
  53.8 17.4 %copy-start.16 = (bf16[96,1536]{1,0:T(8,128)(2,1)}, bf16[96,1536]{1,0:T(8,128)(2,1)S(1)}, u32[]{:S(2)}) copy-start(bf16[96,1536]{1,0:T(8,128)(2,1)S(1)} %collective-permute-done.56.refs_3_) | copy-start | bytes 884740
  53.8 2.0 %collective-permute-start.57 = (bf16[272,1024]{1,0:T(8,128)(2,1)S(1)}, bf16[272,1024]{1,0:T(8,128)(2,1)S(1)}, u32[]{:S(2)}, u32[]{:S(2)}) collective-permute-start(bf16[272,1024]{1,0:T(8,128)(2,1)S(1)} %collective-permute-done.55.own), channel_id=1, source_target_pairs={{0,1},{1,0},{2,3},{3,2},{4,5},{5,4},{6,7},{7,6},{8,9},{9,8},{10,11... | collective-permute-start | bytes 1671176 | tf_op jit(solution)/shard_map/ppermute | solution.py:477
  53.9 25.2 %collective-permute-start.61 = (bf16[272,1024]{1,0:T(8,128)(2,1)S(1)}, bf16[272,1024]{1,0:T(8,128)(2,1)S(1)}, u32[]{:S(2)}, u32[]{:S(2)}) collective-permute-start(bf16[272,1024]{1,0:T(8,128)(2,1)S(1)} %collective-permute-done.55.own), channel_id=1, source_target_pairs={{0,4},{4,0},{8,12},{12,8},{1,5},{5,1},{9,13},{13,9},{2,6},{6,2},{1... | collective-permute-start | bytes 1671176 | tf_op jit(solution)/shard_map/ppermute | solution.py:474
  56.7 10.4 %copy-start.30 = (bf16[64,1536]{1,0:T(8,128)(2,1)S(1)}, bf16[64,1536]{1,0:T(8,128)(2,1)}, u32[]{:S(2)}) copy-start(bf16[64,1536]{1,0:T(8,128)(2,1)} %get-tuple-element.181) | copy-start | bytes 589828
  65.5 13.6 %collective-permute-start.62 = (bf16[96,1536]{1,0:T(8,128)(2,1)}, bf16[96,1536]{1,0:T(8,128)(2,1)S(1)}, u32[]{:S(2)}, u32[]{:S(2)}) collective-permute-start(bf16[96,1536]{1,0:T(8,128)(2,1)} %get-tuple-element.178.refs_1_), channel_id=1, source_target_pairs={{0,2},{2,0},{1,3},{3,1},{4,6},{6,4},{5,7},{7,5},{8,10},{10,8},{9,1... | collective-permute-start | bytes 884744 | tf_op jit(solution)/shard_map/ppermute | solution.py:628
  67.1 11.9 %collective-permute-start.64 = (bf16[64,1536]{1,0:T(8,128)(2,1)S(1)}, bf16[64,1536]{1,0:T(8,128)(2,1)S(1)}, u32[]{:S(2)}, u32[]{:S(2)}) collective-permute-start(bf16[64,1536]{1,0:T(8,128)(2,1)S(1)} %copy-done.30), channel_id=1, source_target_pairs={{0,8},{4,12},{8,0},{12,4},{1,9},{5,13},{9,1},{13,5},{2,10},{6,14},... | collective-permute-start | bytes 589832 | tf_op jit(solution)/shard_map/ppermute | solution.py:474
  69.4 9.7 %collective-permute-start.63 = (bf16[64,1536]{1,0:T(8,128)(2,1)S(1)}, bf16[64,1536]{1,0:T(8,128)(2,1)S(1)}, u32[]{:S(2)}, u32[]{:S(2)}) collective-permute-start(bf16[64,1536]{1,0:T(8,128)(2,1)S(1)} %copy-done.30), channel_id=1, source_target_pairs={{0,4},{4,0},{8,12},{12,8},{1,5},{5,1},{9,13},{13,9},{2,6},{6,2},{1... | collective-permute-start | bytes 589832 | tf_op jit(solution)/shard_map/ppermute | solution.py:474
  79.0 25.7 %copy-start.21 = (bf16[64,1536]{1,0:T(8,128)(2,1)}, bf16[64,1536]{1,0:T(8,128)(2,1)S(1)}, u32[]{:S(2)}) copy-start(bf16[64,1536]{1,0:T(8,128)(2,1)S(1)} %collective-permute-done.64.refs_13_) | copy-start | bytes 589828
  79.1 25.6 %copy-start.22 = (bf16[64,1536]{1,0:T(8,128)(2,1)}, bf16[64,1536]{1,0:T(8,128)(2,1)S(1)}, u32[]{:S(2)}) copy-start(bf16[64,1536]{1,0:T(8,128)(2,1)S(1)} %collective-permute-done.63.refs_12_) | copy-start | bytes 589828
  79.1 18.3 %copy-start.15 = (bf16[96,1536]{1,0:T(8,128)(2,1)}, bf16[96,1536]{1,0:T(8,128)(2,1)S(1)}, u32[]{:S(2)}) copy-start(bf16[96,1536]{1,0:T(8,128)(2,1)S(1)} %collective-permute-done.62.refs_3_) | copy-start | bytes 884740
  79.1 4.4 %collective-permute-start.65 = (bf16[272,1024]{1,0:T(8,128)(2,1)S(1)}, bf16[272,1024]{1,0:T(8,128)(2,1)S(1)}, u32[]{:S(2)}, u32[]{:S(2)}) collective-permute-start(bf16[272,1024]{1,0:T(8,128)(2,1)S(1)} %collective-permute-done.61.own), channel_id=1, source_target_pairs={{0,1},{1,0},{2,3},{3,2},{4,5},{5,4},{6,7},{7,6},{8,9},{9,8},{10,11... | collective-permute-start | bytes 1671176 | tf_op jit(solution)/shard_map/ppermute | solution.py:477
  79.2 15.9 %collective-permute-start.60 = (bf16[192,1536]{1,0:T(8,128)(2,1)S(1)}, bf16[192,1536]{1,0:T(8,128)(2,1)S(1)}, u32[]{:S(2)}, u32[]{:S(2)}) collective-permute-start(bf16[192,1536]{1,0:T(8,128)(2,1)S(1)} %copy-done.1), channel_id=1, source_target_pairs={{0,2},{2,0},{1,3},{3,1},{4,6},{6,4},{5,7},{7,5},{8,10},{10,8},{9,1... | collective-permute-start | bytes 1769480 | tf_op jit(solution)/shard_map/ppermute | solution.py:629
  79.7 13.3 %collective-permute-start.66 = (bf16[64,1536]{1,0:T(8,128)(2,1)S(1)}, bf16[64,1536]{1,0:T(8,128)(2,1)S(1)}, u32[]{:S(2)}, u32[]{:S(2)}) collective-permute-start(bf16[64,1536]{1,0:T(8,128)(2,1)S(1)} %collective-permute-done.64.refs_13_), channel_id=1, source_target_pairs={{0,4},{4,0},{8,12},{12,8},{1,5},{5,1},{9,13},{13,9},{2,6},{6,2},{1... | collective-permute-start | bytes 589832 | tf_op jit(solution)/shard_map/ppermute | solution.py:474
  81.0 12.2 %collective-permute-start.68 = (bf16[64,1536]{1,0:T(8,128)(2,1)}, bf16[64,1536]{1,0:T(8,128)(2,1)S(1)}, u32[]{:S(2)}, u32[]{:S(2)}) collective-permute-start(bf16[64,1536]{1,0:T(8,128)(2,1)} %get-tuple-element.185), channel_id=1, source_target_pairs={{0,8},{4,12},{8,0},{12,4},{1,9},{5,13},{9,1},{13,5},{2,10},{6,14},... | collective-permute-start | bytes 589832 | tf_op jit(solution)/shard_map/ppermute | solution.py:474
  83.3 11.8 %collective-permute-start.67 = (bf16[64,1536]{1,0:T(8,128)(2,1)}, bf16[64,1536]{1,0:T(8,128)(2,1)S(1)}, u32[]{:S(2)}, u32[]{:S(2)}) collective-permute-start(bf16[64,1536]{1,0:T(8,128)(2,1)} %get-tuple-element.185), channel_id=1, source_target_pairs={{0,4},{4,0},{8,12},{12,8},{1,5},{5,1},{9,13},{13,9},{2,6},{6,2},{1... | collective-permute-start | bytes 589832 | tf_op jit(solution)/shard_map/ppermute | solution.py:474
  83.5 21.8 %collective-permute-start.58 = (bf16[128,1024]{1,0:T(8,128)(2,1)}, bf16[128,1024]{1,0:T(8,128)(2,1)S(1)}, u32[]{:S(2)}, u32[]{:S(2)}) collective-permute-start(bf16[128,1024]{1,0:T(8,128)(2,1)} %get-tuple-element.177), channel_id=1, source_target_pairs={{0,1},{1,0},{2,3},{3,2},{4,5},{5,4},{6,7},{7,6},{8,9},{9,8},{10,11... | collective-permute-start | bytes 786440 | tf_op jit(solution)/shard_map/ppermute | solution.py:477
  93.0 50.0 %copy-start.23 = (bf16[64,1536]{1,0:T(8,128)(2,1)}, bf16[64,1536]{1,0:T(8,128)(2,1)S(1)}, u32[]{:S(2)}) copy-start(bf16[64,1536]{1,0:T(8,128)(2,1)S(1)} %collective-permute-done.66.refs_14_) | copy-start | bytes 589828
  93.1 49.9 %copy-start.24 = (bf16[64,1536]{1,0:T(8,128)(2,1)}, bf16[64,1536]{1,0:T(8,128)(2,1)S(1)}, u32[]{:S(2)}) copy-start(bf16[64,1536]{1,0:T(8,128)(2,1)S(1)} %collective-permute-done.68.refs_16_) | copy-start | bytes 589828
  95.8 40.3 %collective-permute-start.71 = (bf16[192,1536]{1,0:T(8,128)(2,1)}, bf16[192,1536]{1,0:T(8,128)(2,1)S(1)}, u32[]{:S(2)}, u32[]{:S(2)}) collective-permute-start(bf16[192,1536]{1,0:T(8,128)(2,1)} %get-tuple-element.186.refs_0_), channel_id=1, source_target_pairs={{0,2},{2,0},{1,3},{3,1},{4,6},{6,4},{5,7},{7,5},{8,10},{10,8},{9,1... | collective-permute-start | bytes 1769480 | tf_op jit(solution)/shard_map/ppermute | solution.py:639
  104.7 3.5 %collective-permute-start.69 = (bf16[128,1024]{1,0:T(8,128)(2,1)}, bf16[128,1024]{1,0:T(8,128)(2,1)S(1)}, u32[]{:S(2)}, u32[]{:S(2)}) collective-permute-start(bf16[128,1024]{1,0:T(8,128)(2,1)} %get-tuple-element.191), channel_id=1, source_target_pairs={{0,1},{1,0},{2,3},{3,2},{4,5},{5,4},{6,7},{7,6},{8,9},{9,8},{10,11... | collective-permute-start | bytes 786440 | tf_op jit(solution)/shard_map/ppermute | solution.py:477
  104.8 18.8 %collective-permute-start.72 = (bf16[96,1536]{1,0:T(8,128)(2,1)S(1)}, bf16[96,1536]{1,0:T(8,128)(2,1)S(1)}, u32[]{:S(2)}, u32[]{:S(2)}) collective-permute-start(bf16[96,1536]{1,0:T(8,128)(2,1)S(1)} %copy-done.13), channel_id=1, source_target_pairs={{0,2},{2,0},{1,3},{3,1},{4,6},{6,4},{5,7},{7,5},{8,10},{10,8},{9,1... | collective-permute-start | bytes 884744 | tf_op jit(solution)/shard_map/ppermute | solution.py:638
  105.3 30.7 %collective-permute-start.59 = (bf16[128,1024]{1,0:T(8,128)(2,1)S(1)}, bf16[128,1024]{1,0:T(8,128)(2,1)S(1)}, u32[]{:S(2)}, u32[]{:S(2)}) collective-permute-start(bf16[128,1024]{1,0:T(8,128)(2,1)S(1)} %add_convert_fusion.3), channel_id=1, source_target_pairs={{0,4},{4,0},{8,12},{12,8},{1,5},{5,1},{9,13},{13,9},{2,6},{6,2},{1... | collective-permute-start | bytes 786440 | tf_op jit(solution)/shard_map/ppermute | solution.py:474
  107.4 16.2 %collective-permute-start.73 = (bf16[64,1536]{1,0:T(8,128)(2,1)S(1)}, bf16[64,1536]{1,0:T(8,128)(2,1)S(1)}, u32[]{:S(2)}, u32[]{:S(2)}) collective-permute-start(bf16[64,1536]{1,0:T(8,128)(2,1)S(1)} %collective-permute-done.68.refs_16_), channel_id=1, source_target_pairs={{0,4},{4,0},{8,12},{12,8},{1,5},{5,1},{9,13},{13,9},{2,6},{6,2},{1... | collective-permute-start | bytes 589832 | tf_op jit(solution)/shard_map/ppermute | solution.py:474
  109.2 40.7 %collective-permute-start.70 = (bf16[128,1024]{1,0:T(8,128)(2,1)S(1)}, bf16[128,1024]{1,0:T(8,128)(2,1)S(1)}, u32[]{:S(2)}, u32[]{:S(2)}) collective-permute-start(bf16[128,1024]{1,0:T(8,128)(2,1)S(1)} %add_convert_fusion.2), channel_id=1, source_target_pairs={{0,8},{4,12},{8,0},{12,4},{1,9},{5,13},{9,1},{13,5},{2,10},{6,14},... | collective-permute-start | bytes 786440 | tf_op jit(solution)/shard_map/ppermute | solution.py:474
  123.6 26.4 %copy-start.26 = (bf16[64,1536]{1,0:T(8,128)(2,1)}, bf16[64,1536]{1,0:T(8,128)(2,1)S(1)}, u32[]{:S(2)}) copy-start(bf16[64,1536]{1,0:T(8,128)(2,1)S(1)} %collective-permute-done.73.refs_17_) | copy-start | bytes 589828
  123.6 12.5 %copy-start.14 = (bf16[96,1536]{1,0:T(8,128)(2,1)}, bf16[96,1536]{1,0:T(8,128)(2,1)S(1)}, u32[]{:S(2)}) copy-start(bf16[96,1536]{1,0:T(8,128)(2,1)S(1)} %collective-permute-done.72.refs_3_) | copy-start | bytes 884740
  123.6 9.8 %collective-permute-start.5 = (bf16[64,1536]{1,0:T(8,128)(2,1)S(1)}, bf16[64,1536]{1,0:T(8,128)(2,1)}, u32[]{:S(2)}, u32[]{:S(2)}) collective-permute-start(bf16[64,1536]{1,0:T(8,128)(2,1)S(1)} %param.2), channel_id=1, source_target_pairs={{0,12},{4,8},{8,4},{12,0},{1,13},{5,9},{9,5},{13,1},{2,14},{6,10},... | collective-permute-start | bytes 589832 | tf_op jit(solution)/shard_map/cond/branch_2_fun/ppermute | solution.py:652
  126.8 9.3 %collective-permute-start.4 = (bf16[64,1536]{1,0:T(8,128)(2,1)S(1)}, bf16[64,1536]{1,0:T(8,128)(2,1)}, u32[]{:S(2)}, u32[]{:S(2)}) collective-permute-start(bf16[64,1536]{1,0:T(8,128)(2,1)S(1)} %param.2), channel_id=1, source_target_pairs={{0,4},{4,0},{8,12},{12,8},{1,5},{5,1},{9,13},{13,9},{2,6},{6,2},{1... | collective-permute-start | bytes 589832 | tf_op jit(solution)/shard_map/cond/branch_2_fun/ppermute | solution.py:652
  143.0 18.9 %collective-permute-start.74 = (bf16[128,1024]{1,0:T(8,128)(2,1)}, bf16[128,1024]{1,0:T(8,128)(2,1)S(1)}, u32[]{:S(2)}, u32[]{:S(2)}) collective-permute-start(bf16[128,1024]{1,0:T(8,128)(2,1)} %get-tuple-element.202), channel_id=1, source_target_pairs={{0,1},{1,0},{2,3},{3,2},{4,5},{5,4},{6,7},{7,6},{8,9},{9,8},{10,11... | collective-permute-start | bytes 786440 | tf_op jit(solution)/shard_map/ppermute | solution.py:477
  143.1 3.7 %collective-permute-start.76 = (f32[8,128]{1,0:T(8,128)S(1)}, f32[8,128]{1,0:T(8,128)S(1)}, u32[]{:S(2)}, u32[]{:S(2)}) collective-permute-start(f32[8,128]{1,0:T(8,128)S(1)} %copy-done.27), channel_id=1, source_target_pairs={{0,16},{16,0},{1,17},{17,1},{2,18},{18,2},{3,19},{19,3},{4,20},{20... | collective-permute-start | bytes 12296 | tf_op jit(solution)/shard_map/ppermute | solution.py:646
  150.0 11.9 %copy-start.29 = (bf16[128,1024]{1,0:T(8,128)(2,1)S(1)}, bf16[128,1024]{1,0:T(8,128)(2,1)}, u32[]{:S(2)}) copy-start(bf16[128,1024]{1,0:T(8,128)(2,1)} %get-tuple-element.164) | copy-start | bytes 786436
  150.0 11.9 %copy-start.18 = (bf16[128,1024]{1,0:T(8,128)(2,1)S(1)}, bf16[128,1024]{1,0:T(8,128)(2,1)}, u32[]{:S(2)}) copy-start(bf16[128,1024]{1,0:T(8,128)(2,1)} %get-tuple-element.201) | copy-start | bytes 786436
  150.1 9.8 %collective-permute-start.17 = (bf16[64,1536]{1,0:T(8,128)(2,1)S(1)}, bf16[64,1536]{1,0:T(8,128)(2,1)}, u32[]{:S(2)}, u32[]{:S(2)}) collective-permute-start(bf16[64,1536]{1,0:T(8,128)(2,1)S(1)} %get-tuple-element.58), channel_id=1, source_target_pairs={{0,12},{4,8},{8,4},{12,0},{1,13},{5,9},{9,5},{13,1},{2,14},{6,10},... | collective-permute-start | bytes 589832 | tf_op jit(solution)/shard_map/cond/branch_2_fun/ppermute | solution.py:661
  151.8 10.1 %collective-permute-start.16 = (bf16[64,1536]{1,0:T(8,128)(2,1)S(1)}, bf16[64,1536]{1,0:T(8,128)(2,1)}, u32[]{:S(2)}, u32[]{:S(2)}) collective-permute-start(bf16[64,1536]{1,0:T(8,128)(2,1)S(1)} %get-tuple-element.58), channel_id=1, source_target_pairs={{0,4},{4,0},{8,12},{12,8},{1,5},{5,1},{9,13},{13,9},{2,6},{6,2},{1... | collective-permute-start | bytes 589832 | tf_op jit(solution)/shard_map/cond/branch_2_fun/ppermute | solution.py:661
  161.9 15.1 %collective-permute-start.53 = (bf16[128,1024]{1,0:T(8,128)(2,1)S(1)}, bf16[128,1024]{1,0:T(8,128)(2,1)S(1)}, u32[]{:S(2)}, u32[]{:S(2)}) collective-permute-start(bf16[128,1024]{1,0:T(8,128)(2,1)S(1)} %copy-done.29), channel_id=1, source_target_pairs={{0,1},{1,0},{2,3},{3,2},{4,5},{5,4},{6,7},{7,6},{8,9},{9,8},{10,11... | collective-permute-start | bytes 786440 | tf_op jit(solution)/shard_map/ppermute | solution.py:477
  162.0 15.0 %collective-permute-start.75 = (bf16[128,1024]{1,0:T(8,128)(2,1)S(1)}, bf16[128,1024]{1,0:T(8,128)(2,1)S(1)}, u32[]{:S(2)}, u32[]{:S(2)}) collective-permute-start(bf16[128,1024]{1,0:T(8,128)(2,1)S(1)} %add_convert_fusion.1), channel_id=1, source_target_pairs={{0,12},{4,8},{8,4},{12,0},{1,13},{5,9},{9,5},{13,1},{2,14},{6,10},... | collective-permute-start | bytes 786440 | tf_op jit(solution)/shard_map/ppermute | solution.py:474
  164.2 12.8 %copy-start.20 = (bf16[128,1024]{1,0:T(8,128)(2,1)S(1)}, bf16[128,1024]{1,0:T(8,128)(2,1)}, u32[]{:S(2)}) copy-start(bf16[128,1024]{1,0:T(8,128)(2,1)} %get-tuple-element.163) | copy-start | bytes 786436
  (16 other events, 51.5 us)

commit v3 on v2

--- a/solution.py
+++ b/solution.py
@@ -182,10 +182,11 @@
         loads.append(copies.start(src.at[pl.ds(2 * rows, META), pl.ds(0, rows)], meta.at[:, at]))
         loads.append(copies.start(src.at[pl.ds(0, rows)], rows_in.at[at]))
         loads.append(copies.start(src.at[pl.ds(rows, rows)], rows_out.at[at]))
-    for load in loads:
-        load.wait()
     ready = {}
     for s in range(3):
+        if s == 1:
+            for load in loads:
+                load.wait()
         for i, (src, extra, dst) in enumerate(zip(weights[0:3], weights[3:6], (vg, vu, vd))):
             ready[3 * s + i] = copies.start(src.at[s] if s < 2 else extra.at[0], dst.at[s])
     routes = routing(meta[...])
@@ -244,17 +245,17 @@
     )
 
 
-def backward_kernel(parts, split, cap, light, carried, *refs):
+def backward_kernel(parts, split, cap, light, *refs):
     pieces = 2 if split else 1
     partial = [refs[pieces * i : pieces * (i + 1)] for i in range(parts)]
     refs = refs[pieces * parts :]
-    place_in, weights, carry, refs = refs[0], refs[1:5], refs[5 : 5 + carried], refs[5 + carried :]
+    place_in, weights, refs = refs[0], refs[1:5], refs[5:]
     kinds = 2 if light < cap else 1
     a_out, shadow_outs, own_out, sib_out = refs[0], refs[1 : 1 + kinds], *refs[1 + kinds : 3 + kinds]
     vg, vu, part_s, place_s, a_s, total, own_s, sib_s, sems = refs[3 + kinds :]
     hidden, rows = vg.shape[2], own_s.shape[0]
     copies = Copies(sems)
-    loads, ready, stores, ends = [], [], [], [0, 0]
+    loads, ready, stores = [], [], []
     for s in range(3):
         of = pl.ds(s * cap, cap)
         loads.append([])
@@ -264,10 +265,6 @@
         loads[s].append(copies.start(place_in.at[of], place_s.at[of]))
         for src, extra, dst in zip(weights[0:2], weights[2:4], (vg, vu)):
             ready.append(copies.start(src.at[s] if s < 2 else extra.at[0], dst.at[s]))
-    for kind, held in enumerate(carry):
-        kind = kind + kinds - carried
-        ends[kind] = held.shape[0]
-        stores.append(copies.start(held, shadow_outs[kind].at[pl.ds(0, ends[kind])]))
     for s in range(3):
         at, of = slice(s * cap, (s + 1) * cap), pl.ds(s * cap, cap)
         for load in loads[s]:
@@ -280,8 +277,7 @@
         else:
             first = 2 * cap
             for kind, size in enumerate((light, cap - light)[0:kinds]):
-                to = shadow_outs[kind].at[pl.ds(ends[kind], size)]
-                stores.append(copies.start(a_s.at[pl.ds(first, size)], to))
+                stores.append(copies.start(a_s.at[pl.ds(first, size)], shadow_outs[kind]))
                 first += size
         ready[2 * s].wait()
         ready[2 * s + 1].wait()
@@ -318,11 +314,12 @@
                 copies.append(pltpu.make_async_copy(srcs[i].at[of], dst.at[e, to], sem))
         return copies
 
-    for e in range(2):
+    heavy = which[0] >= heavy_from
+    held = held_for(shadow, count)
+    last = jnp.where(held[0][1] == 0, 0, 1)
+    for e in (1 - last, last):
         for copy in owned_copies(e):
             copy.start()
-    heavy = which[0] >= heavy_from
-    held = held_for(shadow, count)
     together = held[0][1] == held[1][1]
     after_first = jnp.where(together, jnp.where(heavy, whole, near), 0)
 
@@ -365,6 +362,12 @@
     f_block, f_blocks = blocks_of(width)
     h_block, h_blocks = blocks_of(hidden)
 
+    def results(e):
+        return [
+            pltpu.make_async_copy(src.at[e], dst.at[e], sems.at[e * 3 * count + i])
+            for i, (src, dst) in enumerate(((og_s, og), (ou_s, ou), (od_s, od)))
+        ]
+
     def products(e, k):
         for j in range(f_blocks):
             of = slice(j * f_block, (j + 1) * f_block)
@@ -376,6 +379,8 @@
             ).astype(jnp.bfloat16)
             og_s[e, of, :] = both[:, 0:hidden]
             ou_s[e, of, :] = both[:, hidden:]
+        for copy in results(e)[0:2]:
+            copy.start()
         for j in range(h_blocks):
             of = slice(j * h_block, (j + 1) * h_block)
             from_ = slice(2 * hidden + j * h_block, 2 * hidden + (j + 1) * h_block)
@@ -383,14 +388,8 @@
                 a_all[e, 0:k, from_], g_all[e, 0:k, :], TN, preferred_element_type=jnp.float32
             ).astype(jnp.bfloat16)
 
-    def results(e):
-        return [
-            pltpu.make_async_copy(src.at[e], dst.at[e], sems.at[e * 3 * count + i])
-            for i, (src, dst) in enumerate(((og_s, og), (ou_s, ou), (od_s, od)))
-        ]
-
     def turn(n, _):
-        e = jnp.where(held[0][1] == 0, 1 - n, n)
+        e = jnp.where(n == 0, 1 - last, last)
         for copy in owned_copies(e):
             copy.wait()
 
@@ -416,8 +415,7 @@
             def _(number=number):
                 products(e, owned + number * whole)
 
-        for copy in results(e):
-            copy.start()
+        results(e)[2].start()
         return 0
 
     lax.fori_loop(0, 2, turn, 0)
@@ -509,16 +507,16 @@
             return [partial, lax.ppermute(partial, "dp", swap)]
         return [lax.psum(partial, "dp")]
 
-    def backward(partials, place, carry=(), near=1, far=1):
+    def backward(partials, place):
         parts, split = len(partials), len(partials[0]) - 1
-        outs = [shape((2 * cap, 3 * hidden), bf16), shape((near * light, 3 * hidden), bf16)]
+        outs = [shape((2 * cap, 3 * hidden), bf16), shape((light, 3 * hidden), bf16)]
         if light < cap:
-            outs.append(shape((far * (cap - light), 3 * hidden), bf16))
+            outs.append(shape((cap - light, 3 * hidden), bf16))
         outs += [shape((rows, width), bf16)] * 2
         return call(
-            functools.partial(backward_kernel, parts, split, cap, light, len(carry)),
+            functools.partial(backward_kernel, parts, split, cap, light),
             outs,
-            [REMAIN] * ((1 + split) * parts + 5 + len(carry)),
+            [REMAIN] * ((1 + split) * parts + 5),
             [REMAIN] * len(outs),
             [
                 pltpu.VMEM((3, width, hidden), bf16),
@@ -531,7 +529,7 @@
                 pltpu.VMEM((rows, width), bf16),
                 pltpu.SemaphoreType.DMA((17 + 3 * parts,)),
             ],
-        )(*[p for x in partials for p in x], place, w_gate, w_up, copy_gate, copy_up, *carry)
+        )(*[p for x in partials for p in x], place, w_gate, w_up, copy_gate, copy_up)
 
     def give_back(dx_own, dx_sib, k):
         both = dx_own.astype(jnp.float32) + swapped(dx_sib).astype(jnp.float32)
@@ -627,15 +625,14 @@
     p2, q2 = after((p2, q2), r1)
     t2 = lax.ppermute(q2, "dp", swap)
     r2 = lax.ppermute(p2, "dp", swap)
-    a1, near1, far01, dx_own1, dx_sib1 = backward(
-        [[p1, q1], [after(r1, p2), t1]], place1, (far0,), 1, 2
+    a1, near1, far1, dx_own1, dx_sib1 = backward(
+        [[p1, q1], [after(r1, p2), t1]], place1
     )
     sib3 = swapped(after(here3, a1, t2, moved0[0], moved0[1]))
     moved1 = everywhere(near1)
     ret1 = give_back(dx_own1, dx_sib1, 1)
-    load, x3, g3, place3, p3, q3 = forward(load, here3, sib3, 1)
-    p3, q3 = after((p3, q3), r2, moved0[2], moved1[0], moved1[1])
-    t3 = lax.ppermute(q3, "dp", swap)
+    load, x3, g3, place3, p3 = forward(load, here3, sib3)
+    p3 = after(p3, r2)
     r3 = lax.ppermute(p3, "dp", swap)
     last = call(
         functools.partial(choose_kernel, len(moves)),
@@ -644,33 +641,35 @@
         SCALARS,
         [],
     )(which, load, lax.ppermute(load, "groups", swap))
-    a2, near2, far012, dx_own2, dx_sib2 = backward(
-        [[p2, q2], [after(r2, p3), t2]], place2, (far01,), 1, 3
-    )
-    moved2 = lax.switch(
-        which[0],
-        [functools.partial(lambda m, x: [lax.ppermute(x, "expert", p) for p in m], m) for m in moves],
-        after(near2, t3, moved1[2]),
+    a2, near2, far2, dx_own2, dx_sib2 = backward(
+        [[p2, q2], [after(r2, p3, moved0[2], moved1[0], moved1[1]), t2]], place2
     )
     ret2 = give_back(dx_own2, dx_sib2, 2)
-    r3 = after(r3, ret1, moved2)
-    a3, near3, rest, dx_own3, dx_sib3 = backward([[p3, q3], [r3, t3]], place3, (far012,), 1, 4)
-    near3 = after(near3, ret2)
-
-    def light_branch(perms, x, more):
-        return [[lax.ppermute(x, "expert", p), more] for p in perms]
-
-    def heavy_branch(perms, x, more):
+    r3 = after(r3, last, ret1, ret2, moved1[2])
+    a3, near3, far3, dx_own3, dx_sib3 = backward([[p3], [r3]], place3)
+    near23 = jnp.concatenate([near2, near3], axis=0)
+
+    rest = shape((count * (cap - light), 3 * hidden), bf16)
+
+    def light_branch(perms, x, *more):
+        unused = call(lambda *refs: None, (rest, rest), [], (REMAIN, REMAIN), [])()
+        return [[lax.ppermute(x, "expert", p), u] for p, u in zip(perms, unused)]
+
+    def heavy_branch(perms, x, *more):
+        more = jnp.concatenate(more, axis=0)
         return [[lax.ppermute(y, "expert", p) for y in (x, more)] for p in perms]
 
-    moved3 = lax.switch(
+    moved23 = lax.switch(
         last[0],
         [functools.partial(f, m) for f in (light_branch, heavy_branch) for m in moves],
-        near3,
-        rest,
+        near23,
+        far0,
+        far1,
+        far2,
+        far3,
     )
     ret3 = give_back(dx_own3, dx_sib3, 3)
-    pieces = [moved0, moved1, moved2, [m[0] for m in moved3], [m[1] for m in moved3]]
+    pieces = [moved0, moved1, [m[0] for m in moved23], [m[1] for m in moved23]]
     kept = [(x0, g0, a0), (x1, g1, a1), (x2, g2, a2), (x3, g3, a3)]
     grads = weight_grads(kept, pieces, last, len(moves))
     return (add_up([ret0, ret1, ret2, ret3]), *grads)

time: 179 us -> 167 us (0.933)
  waiting for transfers between devices: 53.4 us -> 37.7 us
  starting transfers between devices: 36.6 us -> 49.7 us
  Pallas kernels: 76.6 us -> 67.8 us
    ppermute x12, starting transfers between devices: 20.8 us -> 32.7 us  [to_index(): return lax.ppermute(x, 'expert', [(i, i ^ k) for i in range(count)])]
    ppermute x5 -> x2, waiting for transfers between devices: 17.9 us -> 6.91 us  [light_branch(): return [[lax.ppermute(x, 'expert', p), u] for p, u in zip(perms, unused)]]
    ppermute x12, waiting for transfers between devices: 26 us -> 19.5 us  [to_index(): return lax.ppermute(x, 'expert', [(i, i ^ k) for i in range(count)])]
    pallas_call x1, Pallas kernels: 12.8 us -> 8.57 us  [weight_grads(): call(functools.partial(weights_kernel, count, cap, light, layout, heavy_f...]
    pallas_call x4, Pallas kernels: 35 us -> 31.5 us  [forward(): call(functools.partial(forward_kernel, count, cap, light, split), outs, [...]
    ppermute x5 -> x2, starting transfers between devices: 5.33 us -> 7.68 us  [light_branch(): return [[lax.ppermute(x, 'expert', p), u] for p, u in zip(perms, unused)]]
    ppermute x1, waiting for transfers between devices: 0.01 us -> 2.24 us  [on_device(): r2 = lax.ppermute(p2, 'dp', swap)]
    pallas_call x4 -> x5, Pallas kernels: 24.9 us -> 23.9 us  [the longest x4 23.9 us: backward(): call(functools.partial(backward_kernel, parts, split, cap, light), outs,...]
  transfers between devices with their start and end apart: 33 -> 30, of which waited for: 14 -> 12; matrix products, arithmetic and copies ran while one was open for 2% -> 2% of each run, Pallas kernels for 42% -> 36%
where the time goes in v3:
time: 167 us
  Pallas kernels  67.8 us (41%)
  starting transfers between devices  49.7 us (30%)
  waiting for transfers between devices  37.7 us (23%)
  local copies, waits for them, and re-layouts  6.8 us (4%)
  other arithmetic  3.02 us (2%)
    ppermute x12, starting transfers between devices, to_index(): return lax.ppermute(x, 'expert', [(i, i ^ k) for i in range(count)])  32.7 us
    pallas_call x4, Pallas kernels, forward(): call(functools.partial(forward_kernel, count, cap, light, split), outs, [...  31.5 us
    pallas_call x4, Pallas kernels, backward(): call(functools.partial(backward_kernel, parts, split, cap, light), outs,...  23.9 us
    ppermute x12, waiting for transfers between devices, to_index(): return lax.ppermute(x, 'expert', [(i, i ^ k) for i in range(count)])  19.5 us
    pallas_call x1, Pallas kernels, weight_grads(): call(functools.partial(weights_kernel, count, cap, light, layout, heavy_f...  8.57 us
    ppermute x2, starting transfers between devices, light_branch(): return [[lax.ppermute(x, 'expert', p), u] for p, u in zip(perms, unused)]  7.68 us
    ppermute x2, waiting for transfers between devices, light_branch(): return [[lax.ppermute(x, 'expert', p), u] for p, u in zip(perms, unused)]  6.91 us
    ppermute x1, waiting for transfers between devices, on_device(): t0 = lax.ppermute(q0, 'dp', swap)  5.47 us
  transfers between devices with their start and end apart: 30, of which 12 were waited for; matrix products, arithmetic and copies ran while one was open for 2% of the time, Pallas kernels for 36%

profile of v3, /device:TPU:0, one launch (start us, length us, event | category | flops | bytes accessed | tf_op | source)
XLA Modules:
  0.0 166.7 jit_solution(12446910596814136981)
XLA Ops:
  0.6 1.9 %shard_map.138 = (bf16[272,1024]{1,0:T(8,128)(2,1)}, s32[1]{0:T(128)}) custom-call(s32[4]{0:T(128)} %shadow.11, bf16[128,1024]{1,0:T(8,128)(2,1)} %tok_ref.1, bf16[128,1024]{1,0:T(8,128)(2,1)} %grad_ref.1, s32[2,128]{1,0:T(2,128)} %bitcast.3, f32[2,128]{1,0:T(2,128)} %bitcast.4), custom_call_target="tpu_custom_call" | custom-call | tf_op jit(solution)/shard_map/pallas_call | solution.py:573
  3.1 2.6 %collective-permute-start.38 = (bf16[272,1024]{1,0:T(8,128)(2,1)}, bf16[272,1024]{1,0:T(8,128)(2,1)S(1)}, u32[]{:S(2)}, u32[]{:S(2)}) collective-permute-start(bf16[272,1024]{1,0:T(8,128)(2,1)} %get-tuple-element.191.own), channel_id=1, source_target_pairs={{0,4},{4,0},{8,12},{12,8},{1,5},{5,1},{9,13},{13,9},{2,6},{6,2},{1... | collective-permute-start | bytes 1671176 | tf_op jit(solution)/shard_map/ppermute | solution.py:472
  5.7 0.6 broadcast_in_dim.3.load_in
  6.5 8.0 %shard_map.139 = (f32[8,128]{1,0:T(8,128)}, bf16[480,1024]{1,0:T(8,128)(2,1)}, bf16[480,1024]{1,0:T(8,128)(2,1)}, bf16[288,256]{1,0:T(8,128)(2,1)}, bf16[192,1536]{1,0:T(8,128)(2,1)}, /*index=5*/bf16[96,1536]{1,0:T(8,128)(2,1)}) custom-call(s32[4]{0:T(128)} %shadow.11, f32[8,128]{1,0:T(8,128)} %broadcast_in_dim.3.load_in, ...), custom_call_target="tpu_custom_call" | custom-call | tf_op jit(solution)/shard_map/pallas_call | solution.py:485
  14.5 2.1 %collective-permute-start.39 = (bf16[96,1536]{1,0:T(8,128)(2,1)}, bf16[96,1536]{1,0:T(8,128)(2,1)S(1)}, u32[]{:S(2)}, u32[]{:S(2)}) collective-permute-start(bf16[96,1536]{1,0:T(8,128)(2,1)} %get-tuple-element.179.refs_1_), channel_id=1, source_target_pairs={{0,2},{2,0},{1,3},{3,1},{4,6},{6,4},{5,7},{7,5},{8,10},{10,8},{9,1... | collective-permute-start | bytes 884744 | tf_op jit(solution)/shard_map/ppermute | solution.py:611
  16.7 2.5 %collective-permute-done.38.own = bf16[272,1024]{1,0:T(8,128)(2,1)S(1)} collective-permute-done((bf16[272,1024]{1,0:T(8,128)(2,1)}, bf16[272,1024]{1,0:T(8,128)(2,1)S(1)}, u32[]{:S(2)}, u32[]{:S(2)}) %collective-permute-start.38) | collective-permute-done | bytes 557088 | tf_op jit(solution)/shard_map/ppermute | solution.py:472
  19.1 5.5 %collective-permute-done.39.refs_3_ = bf16[96,1536]{1,0:T(8,128)(2,1)S(1)} collective-permute-done((bf16[96,1536]{1,0:T(8,128)(2,1)}, bf16[96,1536]{1,0:T(8,128)(2,1)S(1)}, u32[]{:S(2)}, u32[]{:S(2)}) %collective-permute-start.39) | collective-permute-done | bytes 294944 | tf_op jit(solution)/shard_map/ppermute | solution.py:611
  24.6 3.2 %collective-permute-start.43 = (bf16[272,1024]{1,0:T(8,128)(2,1)S(1)}, bf16[272,1024]{1,0:T(8,128)(2,1)S(1)}, u32[]{:S(2)}, u32[]{:S(2)}) collective-permute-start(bf16[272,1024]{1,0:T(8,128)(2,1)S(1)} %copy-done.7), channel_id=1, source_target_pairs={{0,8},{4,12},{8,0},{12,4},{1,9},{5,13},{9,1},{13,5},{2,10},{6,14},... | collective-permute-start | bytes 1671176 | tf_op jit(solution)/shard_map/ppermute | solution.py:472
  27.8 0.8 copy-done.11
  28.6 7.8 %shard_map.140 = (f32[8,128]{1,0:T(8,128)}, bf16[480,1024]{1,0:T(8,128)(2,1)}, bf16[480,1024]{1,0:T(8,128)(2,1)}, bf16[288,256]{1,0:T(8,128)(2,1)}, bf16[192,1536]{1,0:T(8,128)(2,1)}, /*index=5*/bf16[96,1536]{1,0:T(8,128)(2,1)}) custom-call(s32[4]{0:T(128)} %shadow.11, f32[8,128]{1,0:T(8,128)} %get-tuple-element.180.load_in, bf16[272,1024]{1,0:T(8,128)(2,1)} %copy-done.8, ...), custom_call_target="tpu_custom_call" | custom-call | tf_op jit(solution)/shard_map/pallas_call | solution.py:485
  36.7 1.7 %collective-permute-start.44 = (bf16[96,1536]{1,0:T(8,128)(2,1)}, bf16[96,1536]{1,0:T(8,128)(2,1)S(1)}, u32[]{:S(2)}, u32[]{:S(2)}) collective-permute-start(bf16[96,1536]{1,0:T(8,128)(2,1)} %get-tuple-element.189.refs_1_), channel_id=1, source_target_pairs={{0,2},{2,0},{1,3},{3,1},{4,6},{6,4},{5,7},{7,5},{8,10},{10,8},{9,1... | collective-permute-start | bytes 884744 | tf_op jit(solution)/shard_map/ppermute | solution.py:617
  38.8 6.0 %shard_map.141 = (bf16[192,1536]{1,0:T(8,128)(2,1)}, bf16[64,1536]{1,0:T(8,128)(2,1)}, bf16[32,1536]{1,0:T(8,128)(2,1)S(1)}, bf16[128,1024]{1,0:T(8,128)(2,1)}, bf16[128,1024]{1,0:T(8,128)(2,1)}) custom-call(bf16[192,1536]{1,0:T(8,128)(2,1)} %get-tuple-element.178.refs_0_, bf16[96,1536]{1,0:T(8,128)(2,1)} %get-tuple-element.179.refs_1_, ...), custom_call_target="tpu_custom_call" | custom-call | tf_op jit(solution)/shard_map/pallas_call | solution.py:516
  44.8 8.2 %collective-permute-done.43.own = bf16[272,1024]{1,0:T(8,128)(2,1)S(1)} collective-permute-done((bf16[272,1024]{1,0:T(8,128)(2,1)S(1)}, bf16[272,1024]{1,0:T(8,128)(2,1)S(1)}, u32[]{:S(2)}, u32[]{:S(2)}) %collective-permute-start.43) | collective-permute-done | bytes 557088 | tf_op jit(solution)/shard_map/ppermute | solution.py:472
  53.1 0.7 collective-permute-start.49
  53.8 1.2 collective-permute-done.45.sib
  55.0 0.9 copy-done.12
  55.9 7.9 %shard_map.142 = (f32[8,128]{1,0:T(8,128)}, bf16[480,1024]{1,0:T(8,128)(2,1)}, bf16[480,1024]{1,0:T(8,128)(2,1)}, bf16[288,256]{1,0:T(8,128)(2,1)}, bf16[192,1536]{1,0:T(8,128)(2,1)}, /*index=5*/bf16[96,1536]{1,0:T(8,128)(2,1)}) custom-call(s32[4]{0:T(128)} %shadow.11, f32[8,128]{1,0:T(8,128)} %get-tuple-element.190.load_in, bf16[272,1024]{1,0:T(8,128)(2,1)} %copy-done.5, ...), custom_call_target="tpu_custom_call" | custom-call | tf_op jit(solution)/shard_map/pallas_call | solution.py:485
  63.8 1.6 collective-permute-start.50
  65.4 2.2 %collective-permute-start.52 = (bf16[64,1536]{1,0:T(8,128)(2,1)}, bf16[64,1536]{1,0:T(8,128)(2,1)S(1)}, u32[]{:S(2)}, u32[]{:S(2)}) collective-permute-start(bf16[64,1536]{1,0:T(8,128)(2,1)} %get-tuple-element.204), channel_id=1, source_target_pairs={{0,8},{4,12},{8,0},{12,4},{1,9},{5,13},{9,1},{13,5},{2,10},{6,14},... | collective-permute-start | bytes 589832 | tf_op jit(solution)/shard_map/ppermute | solution.py:472
  67.6 1.9 %collective-permute-start.51 = (bf16[64,1536]{1,0:T(8,128)(2,1)}, bf16[64,1536]{1,0:T(8,128)(2,1)S(1)}, u32[]{:S(2)}, u32[]{:S(2)}) collective-permute-start(bf16[64,1536]{1,0:T(8,128)(2,1)} %get-tuple-element.204), channel_id=1, source_target_pairs={{0,4},{4,0},{8,12},{12,8},{1,5},{5,1},{9,13},{13,9},{2,6},{6,2},{1... | collective-permute-start | bytes 589832 | tf_op jit(solution)/shard_map/ppermute | solution.py:472
  69.5 5.9 %shard_map.143 = (bf16[192,1536]{1,0:T(8,128)(2,1)}, bf16[64,1536]{1,0:T(8,128)(2,1)}, bf16[32,1536]{1,0:T(8,128)(2,1)S(1)}, bf16[128,1024]{1,0:T(8,128)(2,1)}, bf16[128,1024]{1,0:T(8,128)(2,1)}) custom-call(bf16[192,1536]{1,0:T(8,128)(2,1)} %get-tuple-element.184.refs_0_, bf16[96,1536]{1,0:T(8,128)(2,1)} %get-tuple-element.189.refs_1_, ...), custom_call_target="tpu_custom_call" | custom-call | tf_op jit(solution)/shard_map/pallas_call | solution.py:516
  75.4 2.1 %collective-permute-done.52.refs_13_ = bf16[64,1536]{1,0:T(8,128)(2,1)S(1)} collective-permute-done((bf16[64,1536]{1,0:T(8,128)(2,1)}, bf16[64,1536]{1,0:T(8,128)(2,1)S(1)}, u32[]{:S(2)}, u32[]{:S(2)}) %collective-permute-start.52) | collective-permute-done | bytes 196640 | tf_op jit(solution)/shard_map/ppermute | solution.py:472
  77.6 0.7 copy-done.21
  79.0 1.2 collective-permute-start.54
  80.2 2.9 %collective-permute-start.56 = (bf16[64,1536]{1,0:T(8,128)(2,1)}, bf16[64,1536]{1,0:T(8,128)(2,1)}, u32[]{:S(2)}, u32[]{:S(2)}) collective-permute-start(bf16[64,1536]{1,0:T(8,128)(2,1)} %get-tuple-element.208), channel_id=1, source_target_pairs={{0,8},{4,12},{8,0},{12,4},{1,9},{5,13},{9,1},{13,5},{2,10},{6,14},... | collective-permute-start | bytes 589832 | tf_op jit(solution)/shard_map/ppermute | solution.py:472
  83.9 7.9 %shard_map.144 = (f32[8,128]{1,0:T(8,128)}, bf16[480,1024]{1,0:T(8,128)(2,1)}, bf16[480,1024]{1,0:T(8,128)(2,1)}, bf16[288,256]{1,0:T(8,128)(2,1)}, bf16[288,1536]{1,0:T(8,128)(2,1)}) custom-call(s32[4]{0:T(128)} %shadow.11, f32[8,128]{1,0:T(8,128)} %get-tuple-element.202.load_in, bf16[272,1024]{1,0:T(8,128)(2,1)} %copy-done.6, bf16[272,1024]{1,0:T(8,128)(2,1)} %copy-done.9, ...), custom_call_target="tpu_custom_call" | custom-call | tf_op jit(solution)/shard_map/pallas_call | solution.py:485
  91.8 2.2 %collective-permute-done.48.refs_2_ = bf16[192,1536]{1,0:T(8,128)(2,1)S(1)} collective-permute-done((bf16[192,1536]{1,0:T(8,128)(2,1)S(1)}, bf16[192,1536]{1,0:T(8,128)(2,1)S(1)}, u32[]{:S(2)}, u32[]{:S(2)}) %collective-permute-start.48) | collective-permute-done | bytes 589856 | tf_op jit(solution)/shard_map/ppermute | solution.py:627
  95.2 5.9 %shard_map.145 = (bf16[192,1536]{1,0:T(8,128)(2,1)}, bf16[64,1536]{1,0:T(8,128)(2,1)}, bf16[32,1536]{1,0:T(8,128)(2,1)S(1)}, bf16[128,1024]{1,0:T(8,128)(2,1)}, bf16[128,1024]{1,0:T(8,128)(2,1)}) custom-call(bf16[192,1536]{1,0:T(8,128)(2,1)} %get-tuple-element.196.refs_0_, bf16[96,1536]{1,0:T(8,128)(2,1)} %get-tuple-element.201.refs_1_, ...), custom_call_target="tpu_custom_call" | custom-call | tf_op jit(solution)/shard_map/pallas_call | solution.py:516
  101.2 1.0 add_convert_fusion.3
  102.2 1.2 collective-permute-start.47
  103.5 1.0 add_convert_fusion.2
  104.5 3.0 %collective-permute-start.58 = (bf16[128,1024]{1,0:T(8,128)(2,1)S(1)}, bf16[128,1024]{1,0:T(8,128)(2,1)S(1)}, u32[]{:S(2)}, u32[]{:S(2)}) collective-permute-start(bf16[128,1024]{1,0:T(8,128)(2,1)S(1)} %add_convert_fusion.2), channel_id=1, source_target_pairs={{0,8},{4,12},{8,0},{12,4},{1,9},{5,13},{9,1},{13,5},{2,10},{6,14},... | collective-permute-start | bytes 786440 | tf_op jit(solution)/shard_map/ppermute | solution.py:472
  107.5 0.6 collective-permute-start.61
  108.1 1.5 collective-permute-start.60
  109.6 2.1 %collective-permute-done.60.other = f32[8,128]{1,0:T(8,128)S(1)} collective-permute-done((f32[8,128]{1,0:T(8,128)S(1)}, f32[8,128]{1,0:T(8,128)S(1)}, u32[]{:S(2)}, u32[]{:S(2)}) %collective-permute-start.60) | collective-permute-done | bytes 4128 | tf_op jit(solution)/shard_map/ppermute | solution.py:643
  111.7 0.6 copy-done.25
  112.3 1.9 %shard_map.146.which = s32[1]{0:T(128)} custom-call(s32[1]{0:T(128)} %get-tuple-element.213.which, f32[8,128]{1,0:T(8,128)} %get-tuple-element.214.load, f32[8,128]{1,0:T(8,128)} %copy-done.25), custom_call_target="tpu_custom_call" | custom-call | tf_op jit(solution)/shard_map/pallas_call | solution.py:637
  114.2 6.6 %collective-permute-done.61.refs_17_ = bf16[64,1536]{1,0:T(8,128)(2,1)S(1)} collective-permute-done((bf16[64,1536]{1,0:T(8,128)(2,1)}, bf16[64,1536]{1,0:T(8,128)(2,1)S(1)}, u32[]{:S(2)}, u32[]{:S(2)}) %collective-permute-start.61) | collective-permute-done | bytes 196640 | tf_op jit(solution)/shard_map/ppermute | solution.py:472
  120.9 0.9 copy-done
  121.8 6.1 %shard_map.147 = (bf16[192,1536]{1,0:T(8,128)(2,1)}, bf16[64,1536]{1,0:T(8,128)(2,1)}, bf16[32,1536]{1,0:T(8,128)(2,1)S(1)}, bf16[128,1024]{1,0:T(8,128)(2,1)}, bf16[128,1024]{1,0:T(8,128)(2,1)}) custom-call(bf16[288,1536]{1,0:T(8,128)(2,1)} %get-tuple-element.207.refs_0_, bf16[288,1536]{1,0:T(8,128)(2,1)} %copy-done, ...), custom_call_target="tpu_custom_call" | custom-call | tf_op jit(solution)/shard_map/pallas_call | solution.py:516
  128.6 0.9 constant_dynamic-update-slice_fusion.24
  129.6 14.6 %conditional.1 = (bf16[128,1536]{1,0:T(8,128)(2,1)}, bf16[128,1536]{1,0:T(8,128)(2,1)}, bf16[128,1536]{1,0:T(8,128)(2,1)}, bf16[128,1536]{1,0:T(8,128)(2,1)}) conditional(s32[]{:T(128)} %bitcast.2, bf16[128,1536]{1,0:T(8,128)(2,1)S(1)} %constant_dynamic-update-slice_fusion.24, ...), branch_computations={%region_0.0_spmd, %region_1.0_spmd, %region_2.0_spmd, %region_3.0_... | conditional | bytes 7078080 | solution.py:662
  129.6 6.3 %collective-permute-start.11 = (bf16[128,1536]{1,0:T(8,128)(2,1)S(1)}, bf16[128,1536]{1,0:T(8,128)(2,1)}, u32[]{:S(2)}, u32[]{:S(2)}) collective-permute-start(bf16[128,1536]{1,0:T(8,128)(2,1)S(1)} %param.5), channel_id=1, source_target_pairs={{0,12},{8,4},{1,13},{9,5},{2,14},{10,6},{3,15},{11,7},{16,28},{24,... | collective-permute-start | bytes 1179656 | tf_op jit(solution)/shard_map/cond/branch_5_fun/ppermute | solution.py:656
  135.9 1.4 collective-permute-start.10
  137.3 6.9 %collective-permute-done.11 = bf16[128,1536]{1,0:T(8,128)(2,1)} collective-permute-done((bf16[128,1536]{1,0:T(8,128)(2,1)S(1)}, bf16[128,1536]{1,0:T(8,128)(2,1)}, u32[]{:S(2)}, u32[]{:S(2)}) %collective-permute-start.11) | collective-permute-done | bytes 393248 | tf_op jit(solution)/shard_map/cond/branch_5_fun/ppermute | solution.py:656
  144.3 12.9 %collective-permute-start.63 = (bf16[128,1024]{1,0:T(8,128)(2,1)S(1)}, bf16[128,1024]{1,0:T(8,128)(2,1)S(1)}, u32[]{:S(2)}, u32[]{:S(2)}) collective-permute-start(bf16[128,1024]{1,0:T(8,128)(2,1)S(1)} %add_convert_fusion.1), channel_id=1, source_target_pairs={{0,12},{4,8},{8,4},{12,0},{1,13},{5,9},{9,5},{13,1},{2,14},{6,10},... | collective-permute-start | bytes 786440 | tf_op jit(solution)/shard_map/ppermute | solution.py:472
  157.2 8.6 %shard_map.148 = (bf16[2,1024,512]{2,1,0:T(8,128)(2,1)}, bf16[2,1024,512]{2,1,0:T(8,128)(2,1)}, bf16[2,512,1024]{2,1,0:T(8,128)(2,1)}) custom-call(s32[4]{0:T(128)} %shadow.11, s32[1]{0:T(128)} %shard_map.146.which, bf16[480,1024]{1,0:T(8,128)(2,1)} %get-tuple-element.219.refs_0_, bf16[480,1024]{1,0:T(8,128)(2,1)} %get-tuple-element.220.refs_1_, ...), custom_call_target="tpu_custom_call" | custom-call | tf_op jit(solution)/shard_map/pallas_call | solution.py:558
  165.8 0.9 add_convert_fusion
  (86 shorter events, 4.6 us)
Async XLA Ops:
  2.5 3.2 %collective-permute-start.36 = (bf16[272,1024]{1,0:T(8,128)(2,1)}, bf16[272,1024]{1,0:T(8,128)(2,1)S(1)}, u32[]{:S(2)}, u32[]{:S(2)}) collective-permute-start(bf16[272,1024]{1,0:T(8,128)(2,1)} %get-tuple-element.191.own), channel_id=1, source_target_pairs={{0,1},{1,0},{2,3},{3,2},{4,5},{5,4},{6,7},{7,6},{8,9},{9,8},{10,11... | collective-permute-start | bytes 1671176 | tf_op jit(solution)/shard_map/ppermute | solution.py:475
  3.1 16.1 %collective-permute-start.38 = (bf16[272,1024]{1,0:T(8,128)(2,1)}, bf16[272,1024]{1,0:T(8,128)(2,1)S(1)}, u32[]{:S(2)}, u32[]{:S(2)}) collective-permute-start(bf16[272,1024]{1,0:T(8,128)(2,1)} %get-tuple-element.191.own), channel_id=1, source_target_pairs={{0,4},{4,0},{8,12},{12,8},{1,5},{5,1},{9,13},{13,9},{2,6},{6,2},{1... | collective-permute-start | bytes 1671176 | tf_op jit(solution)/shard_map/ppermute | solution.py:472
  6.5 18.1 %copy-start.7 = (bf16[272,1024]{1,0:T(8,128)(2,1)S(1)}, bf16[272,1024]{1,0:T(8,128)(2,1)}, u32[]{:S(2)}) copy-start(bf16[272,1024]{1,0:T(8,128)(2,1)} %get-tuple-element.191.own) | copy-start | bytes 1671172
  14.5 10.1 %collective-permute-start.39 = (bf16[96,1536]{1,0:T(8,128)(2,1)}, bf16[96,1536]{1,0:T(8,128)(2,1)S(1)}, u32[]{:S(2)}, u32[]{:S(2)}) collective-permute-start(bf16[96,1536]{1,0:T(8,128)(2,1)} %get-tuple-element.179.refs_1_), channel_id=1, source_target_pairs={{0,2},{2,0},{1,3},{3,1},{4,6},{6,4},{5,7},{7,5},{8,10},{10,8},{9,1... | collective-permute-start | bytes 884744 | tf_op jit(solution)/shard_map/ppermute | solution.py:611
  16.6 20.2 %collective-permute-start.37 = (bf16[192,1536]{1,0:T(8,128)(2,1)}, bf16[192,1536]{1,0:T(8,128)(2,1)S(1)}, u32[]{:S(2)}, u32[]{:S(2)}) collective-permute-start(bf16[192,1536]{1,0:T(8,128)(2,1)} %get-tuple-element.178.refs_0_), channel_id=1, source_target_pairs={{0,2},{2,0},{1,3},{3,1},{4,6},{6,4},{5,7},{7,5},{8,10},{10,8},{9,1... | collective-permute-start | bytes 1769480 | tf_op jit(solution)/shard_map/ppermute | solution.py:612
  19.1 8.7 %copy-start.8 = (bf16[272,1024]{1,0:T(8,128)(2,1)}, bf16[272,1024]{1,0:T(8,128)(2,1)S(1)}, u32[]{:S(2)}) copy-start(bf16[272,1024]{1,0:T(8,128)(2,1)S(1)} %collective-permute-done.38.own) | copy-start | bytes 1671172
  24.6 14.2 %copy-start.15 = (bf16[96,1536]{1,0:T(8,128)(2,1)}, bf16[96,1536]{1,0:T(8,128)(2,1)S(1)}, u32[]{:S(2)}) copy-start(bf16[96,1536]{1,0:T(8,128)(2,1)S(1)} %collective-permute-done.39.refs_3_) | copy-start | bytes 884740
  24.6 3.2 %collective-permute-start.40 = (bf16[272,1024]{1,0:T(8,128)(2,1)S(1)}, bf16[272,1024]{1,0:T(8,128)(2,1)S(1)}, u32[]{:S(2)}, u32[]{:S(2)}) collective-permute-start(bf16[272,1024]{1,0:T(8,128)(2,1)S(1)} %collective-permute-done.38.own), channel_id=1, source_target_pairs={{0,1},{1,0},{2,3},{3,2},{4,5},{5,4},{6,7},{7,6},{8,9},{9,8},{10,11... | collective-permute-start | bytes 1671176 | tf_op jit(solution)/shard_map/ppermute | solution.py:475
  24.6 28.4 %collective-permute-start.43 = (bf16[272,1024]{1,0:T(8,128)(2,1)S(1)}, bf16[272,1024]{1,0:T(8,128)(2,1)S(1)}, u32[]{:S(2)}, u32[]{:S(2)}) collective-permute-start(bf16[272,1024]{1,0:T(8,128)(2,1)S(1)} %copy-done.7), channel_id=1, source_target_pairs={{0,8},{4,12},{8,0},{12,4},{1,9},{5,13},{9,1},{13,5},{2,10},{6,14},... | collective-permute-start | bytes 1671176 | tf_op jit(solution)/shard_map/ppermute | solution.py:472
  36.7 2.0 %copy-start.4 = (bf16[192,1536]{1,0:T(8,128)(2,1)}, bf16[192,1536]{1,0:T(8,128)(2,1)S(1)}, u32[]{:S(2)}) copy-start(bf16[192,1536]{1,0:T(8,128)(2,1)S(1)} %collective-permute-done.37.refs_2_) | copy-start | bytes 1769476
  36.7 16.2 %collective-permute-start.44 = (bf16[96,1536]{1,0:T(8,128)(2,1)}, bf16[96,1536]{1,0:T(8,128)(2,1)S(1)}, u32[]{:S(2)}, u32[]{:S(2)}) collective-permute-start(bf16[96,1536]{1,0:T(8,128)(2,1)} %get-tuple-element.189.refs_1_), channel_id=1, source_target_pairs={{0,2},{2,0},{1,3},{3,1},{4,6},{6,4},{5,7},{7,5},{8,10},{10,8},{9,1... | collective-permute-start | bytes 884744 | tf_op jit(solution)/shard_map/ppermute | solution.py:617
  38.5 25.3 %collective-permute-start.42 = (bf16[192,1536]{1,0:T(8,128)(2,1)}, bf16[192,1536]{1,0:T(8,128)(2,1)S(1)}, u32[]{:S(2)}, u32[]{:S(2)}) collective-permute-start(bf16[192,1536]{1,0:T(8,128)(2,1)} %get-tuple-element.184.refs_0_), channel_id=1, source_target_pairs={{0,2},{2,0},{1,3},{3,1},{4,6},{6,4},{5,7},{7,5},{8,10},{10,8},{9,1... | collective-permute-start | bytes 1769480 | tf_op jit(solution)/shard_map/ppermute | solution.py:618
  53.0 2.0 %copy-start.5 = (bf16[272,1024]{1,0:T(8,128)(2,1)}, bf16[272,1024]{1,0:T(8,128)(2,1)S(1)}, u32[]{:S(2)}) copy-start(bf16[272,1024]{1,0:T(8,128)(2,1)S(1)} %collective-permute-done.43.own) | copy-start | bytes 1671172
  53.0 16.5 %copy-start.14 = (bf16[96,1536]{1,0:T(8,128)(2,1)}, bf16[96,1536]{1,0:T(8,128)(2,1)S(1)}, u32[]{:S(2)}) copy-start(bf16[96,1536]{1,0:T(8,128)(2,1)S(1)} %collective-permute-done.44.refs_3_) | copy-start | bytes 884740
  53.0 2.0 %collective-permute-start.45 = (bf16[272,1024]{1,0:T(8,128)(2,1)S(1)}, bf16[272,1024]{1,0:T(8,128)(2,1)S(1)}, u32[]{:S(2)}, u32[]{:S(2)}) collective-permute-start(bf16[272,1024]{1,0:T(8,128)(2,1)S(1)} %collective-permute-done.43.own), channel_id=1, source_target_pairs={{0,1},{1,0},{2,3},{3,2},{4,5},{5,4},{6,7},{7,6},{8,9},{9,8},{10,11... | collective-permute-start | bytes 1671176 | tf_op jit(solution)/shard_map/ppermute | solution.py:475
  53.1 24.5 %collective-permute-start.49 = (bf16[272,1024]{1,0:T(8,128)(2,1)S(1)}, bf16[272,1024]{1,0:T(8,128)(2,1)S(1)}, u32[]{:S(2)}, u32[]{:S(2)}) collective-permute-start(bf16[272,1024]{1,0:T(8,128)(2,1)S(1)} %collective-permute-done.43.own), channel_id=1, source_target_pairs={{0,4},{4,0},{8,12},{12,8},{1,5},{5,1},{9,13},{13,9},{2,6},{6,2},{1... | collective-permute-start | bytes 1671176 | tf_op jit(solution)/shard_map/ppermute | solution.py:472
  63.8 5.7 %copy-start.2 = (bf16[192,1536]{1,0:T(8,128)(2,1)}, bf16[192,1536]{1,0:T(8,128)(2,1)S(1)}, u32[]{:S(2)}) copy-start(bf16[192,1536]{1,0:T(8,128)(2,1)S(1)} %collective-permute-done.42.refs_2_) | copy-start | bytes 1769476
  63.8 13.8 %collective-permute-start.50 = (bf16[96,1536]{1,0:T(8,128)(2,1)}, bf16[96,1536]{1,0:T(8,128)(2,1)S(1)}, u32[]{:S(2)}, u32[]{:S(2)}) collective-permute-start(bf16[96,1536]{1,0:T(8,128)(2,1)} %get-tuple-element.201.refs_1_), channel_id=1, source_target_pairs={{0,2},{2,0},{1,3},{3,1},{4,6},{6,4},{5,7},{7,5},{8,10},{10,8},{9,1... | collective-permute-start | bytes 884744 | tf_op jit(solution)/shard_map/ppermute | solution.py:626
  65.4 12.1 %collective-permute-start.52 = (bf16[64,1536]{1,0:T(8,128)(2,1)}, bf16[64,1536]{1,0:T(8,128)(2,1)S(1)}, u32[]{:S(2)}, u32[]{:S(2)}) collective-permute-start(bf16[64,1536]{1,0:T(8,128)(2,1)} %get-tuple-element.204), channel_id=1, source_target_pairs={{0,8},{4,12},{8,0},{12,4},{1,9},{5,13},{9,1},{13,5},{2,10},{6,14},... | collective-permute-start | bytes 589832 | tf_op jit(solution)/shard_map/ppermute | solution.py:472
  67.6 9.9 %collective-permute-start.51 = (bf16[64,1536]{1,0:T(8,128)(2,1)}, bf16[64,1536]{1,0:T(8,128)(2,1)S(1)}, u32[]{:S(2)}, u32[]{:S(2)}) collective-permute-start(bf16[64,1536]{1,0:T(8,128)(2,1)} %get-tuple-element.204), channel_id=1, source_target_pairs={{0,4},{4,0},{8,12},{12,8},{1,5},{5,1},{9,13},{13,9},{2,6},{6,2},{1... | collective-permute-start | bytes 589832 | tf_op jit(solution)/shard_map/ppermute | solution.py:472
  69.5 8.8 %copy-start.1 = (bf16[192,1536]{1,0:T(8,128)(2,1)S(1)}, bf16[192,1536]{1,0:T(8,128)(2,1)}, u32[]{:S(2)}) copy-start(bf16[192,1536]{1,0:T(8,128)(2,1)} %get-tuple-element.196.refs_0_) | copy-start | bytes 1769476
  77.5 23.6 %copy-start.20 = (bf16[64,1536]{1,0:T(8,128)(2,1)}, bf16[64,1536]{1,0:T(8,128)(2,1)S(1)}, u32[]{:S(2)}) copy-start(bf16[64,1536]{1,0:T(8,128)(2,1)S(1)} %collective-permute-done.52.refs_13_) | copy-start | bytes 589828
  77.6 5.8 %copy-start.6 = (bf16[272,1024]{1,0:T(8,128)(2,1)}, bf16[272,1024]{1,0:T(8,128)(2,1)S(1)}, u32[]{:S(2)}) copy-start(bf16[272,1024]{1,0:T(8,128)(2,1)S(1)} %collective-permute-done.49.own) | copy-start | bytes 1671172
  77.6 17.6 %copy-start.13 = (bf16[96,1536]{1,0:T(8,128)(2,1)}, bf16[96,1536]{1,0:T(8,128)(2,1)S(1)}, u32[]{:S(2)}) copy-start(bf16[96,1536]{1,0:T(8,128)(2,1)S(1)} %collective-permute-done.50.refs_3_) | copy-start | bytes 884740
  78.3 4.8 %collective-permute-start.53 = (bf16[272,1024]{1,0:T(8,128)(2,1)S(1)}, bf16[272,1024]{1,0:T(8,128)(2,1)S(1)}, u32[]{:S(2)}, u32[]{:S(2)}) collective-permute-start(bf16[272,1024]{1,0:T(8,128)(2,1)S(1)} %collective-permute-done.49.own), channel_id=1, source_target_pairs={{0,1},{1,0},{2,3},{3,2},{4,5},{5,4},{6,7},{7,6},{8,9},{9,8},{10,11... | collective-permute-start | bytes 1671176 | tf_op jit(solution)/shard_map/ppermute | solution.py:475
  78.3 15.7 %collective-permute-start.48 = (bf16[192,1536]{1,0:T(8,128)(2,1)S(1)}, bf16[192,1536]{1,0:T(8,128)(2,1)S(1)}, u32[]{:S(2)}, u32[]{:S(2)}) collective-permute-start(bf16[192,1536]{1,0:T(8,128)(2,1)S(1)} %copy-done.1), channel_id=1, source_target_pairs={{0,2},{2,0},{1,3},{3,1},{4,6},{6,4},{5,7},{7,5},{8,10},{10,8},{9,1... | collective-permute-start | bytes 1769480 | tf_op jit(solution)/shard_map/ppermute | solution.py:627
  78.8 22.4 %collective-permute-start.46 = (bf16[128,1024]{1,0:T(8,128)(2,1)}, bf16[128,1024]{1,0:T(8,128)(2,1)}, u32[]{:S(2)}, u32[]{:S(2)}) collective-permute-start(bf16[128,1024]{1,0:T(8,128)(2,1)} %get-tuple-element.200), channel_id=1, source_target_pairs={{0,1},{1,0},{2,3},{3,2},{4,5},{5,4},{6,7},{7,6},{8,9},{9,8},{10,11... | collective-permute-start | bytes 786440 | tf_op jit(solution)/shard_map/ppermute | solution.py:475
  79.0 15.5 %collective-permute-start.54 = (bf16[64,1536]{1,0:T(8,128)(2,1)S(1)}, bf16[64,1536]{1,0:T(8,128)(2,1)S(1)}, u32[]{:S(2)}, u32[]{:S(2)}) collective-permute-start(bf16[64,1536]{1,0:T(8,128)(2,1)S(1)} %collective-permute-done.52.refs_13_), channel_id=1, source_target_pairs={{0,4},{4,0},{8,12},{12,8},{1,5},{5,1},{9,13},{13,9},{2,6},{6,2},{1... | collective-permute-start | bytes 589832 | tf_op jit(solution)/shard_map/ppermute | solution.py:472
  80.2 14.4 %collective-permute-start.56 = (bf16[64,1536]{1,0:T(8,128)(2,1)}, bf16[64,1536]{1,0:T(8,128)(2,1)}, u32[]{:S(2)}, u32[]{:S(2)}) collective-permute-start(bf16[64,1536]{1,0:T(8,128)(2,1)} %get-tuple-element.208), channel_id=1, source_target_pairs={{0,8},{4,12},{8,0},{12,4},{1,9},{5,13},{9,1},{13,5},{2,10},{6,14},... | collective-permute-start | bytes 589832 | tf_op jit(solution)/shard_map/ppermute | solution.py:472
  83.1 11.6 %collective-permute-start.55 = (bf16[64,1536]{1,0:T(8,128)(2,1)}, bf16[64,1536]{1,0:T(8,128)(2,1)}, u32[]{:S(2)}, u32[]{:S(2)}) collective-permute-start(bf16[64,1536]{1,0:T(8,128)(2,1)} %get-tuple-element.208), channel_id=1, source_target_pairs={{0,4},{4,0},{8,12},{12,8},{1,5},{5,1},{9,13},{13,9},{2,6},{6,2},{1... | collective-permute-start | bytes 589832 | tf_op jit(solution)/shard_map/ppermute | solution.py:472
  94.0 26.8 %collective-permute-start.59 = (bf16[288,1536]{1,0:T(8,128)(2,1)}, bf16[288,1536]{1,0:T(8,128)(2,1)S(1)}, u32[]{:S(2)}, u32[]{:S(2)}) collective-permute-start(bf16[288,1536]{1,0:T(8,128)(2,1)} %get-tuple-element.207.refs_0_), channel_id=1, source_target_pairs={{0,2},{2,0},{1,3},{3,1},{4,6},{6,4},{5,7},{7,5},{8,10},{10,8},{9,1... | collective-permute-start | bytes 2654216 | tf_op jit(solution)/shard_map/ppermute | solution.py:636
  95.2 6.0 %copy-start.17 = (bf16[128,1024]{1,0:T(8,128)(2,1)S(1)}, bf16[128,1024]{1,0:T(8,128)(2,1)}, u32[]{:S(2)}) copy-start(bf16[128,1024]{1,0:T(8,128)(2,1)} %get-tuple-element.199) | copy-start | bytes 786436
  95.2 12.9 %copy-start.24 = (f32[8,128]{1,0:T(8,128)S(1)}, f32[8,128]{1,0:T(8,128)}, u32[]{:S(2)}) copy-start(f32[8,128]{1,0:T(8,128)} %get-tuple-element.214.load) | copy-start | bytes 12292
  101.1 2.4 %collective-permute-start.57 = (bf16[128,1024]{1,0:T(8,128)(2,1)}, bf16[128,1024]{1,0:T(8,128)(2,1)S(1)}, u32[]{:S(2)}, u32[]{:S(2)}) collective-permute-start(bf16[128,1024]{1,0:T(8,128)(2,1)} %get-tuple-element.212), channel_id=1, source_target_pairs={{0,1},{1,0},{2,3},{3,2},{4,5},{5,4},{6,7},{7,6},{8,9},{9,8},{10,11... | collective-permute-start | bytes 786440 | tf_op jit(solution)/shard_map/ppermute | solution.py:475
  102.2 18.6 %collective-permute-start.47 = (bf16[128,1024]{1,0:T(8,128)(2,1)S(1)}, bf16[128,1024]{1,0:T(8,128)(2,1)S(1)}, u32[]{:S(2)}, u32[]{:S(2)}) collective-permute-start(bf16[128,1024]{1,0:T(8,128)(2,1)S(1)} %add_convert_fusion.3), channel_id=1, source_target_pairs={{0,4},{4,0},{8,12},{12,8},{1,5},{5,1},{9,13},{13,9},{2,6},{6,2},{1... | collective-permute-start | bytes 786440 | tf_op jit(solution)/shard_map/ppermute | solution.py:472
  104.5 16.3 %collective-permute-start.58 = (bf16[128,1024]{1,0:T(8,128)(2,1)S(1)}, bf16[128,1024]{1,0:T(8,128)(2,1)S(1)}, u32[]{:S(2)}, u32[]{:S(2)}) collective-permute-start(bf16[128,1024]{1,0:T(8,128)(2,1)S(1)} %add_convert_fusion.2), channel_id=1, source_target_pairs={{0,8},{4,12},{8,0},{12,4},{1,9},{5,13},{9,1},{13,5},{2,10},{6,14},... | collective-permute-start | bytes 786440 | tf_op jit(solution)/shard_map/ppermute | solution.py:472
  107.5 13.4 %collective-permute-start.61 = (bf16[64,1536]{1,0:T(8,128)(2,1)}, bf16[64,1536]{1,0:T(8,128)(2,1)S(1)}, u32[]{:S(2)}, u32[]{:S(2)}) collective-permute-start(bf16[64,1536]{1,0:T(8,128)(2,1)} %collective-permute-done.56.refs_16_), channel_id=1, source_target_pairs={{0,4},{4,0},{8,12},{12,8},{1,5},{5,1},{9,13},{13,9},{2,6},{6,2},{1... | collective-permute-start | bytes 589832 | tf_op jit(solution)/shard_map/ppermute | solution.py:472
  108.1 3.6 %collective-permute-start.60 = (f32[8,128]{1,0:T(8,128)S(1)}, f32[8,128]{1,0:T(8,128)S(1)}, u32[]{:S(2)}, u32[]{:S(2)}) collective-permute-start(f32[8,128]{1,0:T(8,128)S(1)} %copy-done.24), channel_id=1, source_target_pairs={{0,16},{16,0},{1,17},{17,1},{2,18},{18,2},{3,19},{19,3},{4,20},{20... | collective-permute-start | bytes 12296 | tf_op jit(solution)/shard_map/ppermute | solution.py:643
  120.8 8.7 %copy-start.23 = (bf16[64,1536]{1,0:T(8,128)(2,1)}, bf16[64,1536]{1,0:T(8,128)(2,1)S(1)}, u32[]{:S(2)}) copy-start(bf16[64,1536]{1,0:T(8,128)(2,1)S(1)} %collective-permute-done.61.refs_17_) | copy-start | bytes 589828
  121.8 6.2 %copy-start.19 = (bf16[64,1536]{1,0:T(8,128)(2,1)S(1)}, bf16[64,1536]{1,0:T(8,128)(2,1)}, u32[]{:S(2)}) copy-start(bf16[64,1536]{1,0:T(8,128)(2,1)} %get-tuple-element.229) | copy-start | bytes 589828
  127.9 16.3 %collective-permute-start.62 = (bf16[128,1024]{1,0:T(8,128)(2,1)}, bf16[128,1024]{1,0:T(8,128)(2,1)S(1)}, u32[]{:S(2)}, u32[]{:S(2)}) collective-permute-start(bf16[128,1024]{1,0:T(8,128)(2,1)} %get-tuple-element.218), channel_id=1, source_target_pairs={{0,1},{1,0},{2,3},{3,2},{4,5},{5,4},{6,7},{7,6},{8,9},{9,8},{10,11... | collective-permute-start | bytes 786440 | tf_op jit(solution)/shard_map/ppermute | solution.py:475
  129.5 14.7 %copy-start.26 = (bf16[128,1024]{1,0:T(8,128)(2,1)S(1)}, bf16[128,1024]{1,0:T(8,128)(2,1)}, u32[]{:S(2)}) copy-start(bf16[128,1024]{1,0:T(8,128)(2,1)} %get-tuple-element.188) | copy-start | bytes 786436
  129.5 14.7 %copy-start.16 = (bf16[128,1024]{1,0:T(8,128)(2,1)S(1)}, bf16[128,1024]{1,0:T(8,128)(2,1)}, u32[]{:S(2)}) copy-start(bf16[128,1024]{1,0:T(8,128)(2,1)} %get-tuple-element.217) | copy-start | bytes 786436
  129.6 14.6 %collective-permute-start.11 = (bf16[128,1536]{1,0:T(8,128)(2,1)S(1)}, bf16[128,1536]{1,0:T(8,128)(2,1)}, u32[]{:S(2)}, u32[]{:S(2)}) collective-permute-start(bf16[128,1536]{1,0:T(8,128)(2,1)S(1)} %param.5), channel_id=1, source_target_pairs={{0,12},{8,4},{1,13},{9,5},{2,14},{10,6},{3,15},{11,7},{16,28},{24,... | collective-permute-start | bytes 1179656 | tf_op jit(solution)/shard_map/cond/branch_5_fun/ppermute | solution.py:656
  135.9 8.3 %collective-permute-start.10 = (bf16[128,1536]{1,0:T(8,128)(2,1)S(1)}, bf16[128,1536]{1,0:T(8,128)(2,1)}, u32[]{:S(2)}, u32[]{:S(2)}) collective-permute-start(bf16[128,1536]{1,0:T(8,128)(2,1)S(1)} %param.5), channel_id=1, source_target_pairs={{4,12},{12,4},{5,13},{13,5},{6,14},{14,6},{7,15},{15,7},{20,28},{2... | collective-permute-start | bytes 1179656 | tf_op jit(solution)/shard_map/cond/branch_5_fun/ppermute | solution.py:656
  144.2 21.6 %collective-permute-start.41 = (bf16[128,1024]{1,0:T(8,128)(2,1)S(1)}, bf16[128,1024]{1,0:T(8,128)(2,1)S(1)}, u32[]{:S(2)}, u32[]{:S(2)}) collective-permute-start(bf16[128,1024]{1,0:T(8,128)(2,1)S(1)} %copy-done.26), channel_id=1, source_target_pairs={{0,1},{1,0},{2,3},{3,2},{4,5},{5,4},{6,7},{7,6},{8,9},{9,8},{10,11... | collective-permute-start | bytes 786440 | tf_op jit(solution)/shard_map/ppermute | solution.py:475
  144.3 21.5 %collective-permute-start.63 = (bf16[128,1024]{1,0:T(8,128)(2,1)S(1)}, bf16[128,1024]{1,0:T(8,128)(2,1)S(1)}, u32[]{:S(2)}, u32[]{:S(2)}) collective-permute-start(bf16[128,1024]{1,0:T(8,128)(2,1)S(1)} %add_convert_fusion.1), channel_id=1, source_target_pairs={{0,12},{4,8},{8,4},{12,0},{1,13},{5,9},{9,5},{13,1},{2,14},{6,10},... | collective-permute-start | bytes 786440 | tf_op jit(solution)/shard_map/ppermute | solution.py:472
  157.2 8.6 %copy-start.18 = (bf16[128,1024]{1,0:T(8,128)(2,1)S(1)}, bf16[128,1024]{1,0:T(8,128)(2,1)}, u32[]{:S(2)}) copy-start(bf16[128,1024]{1,0:T(8,128)(2,1)} %get-tuple-element.187) | copy-start | bytes 786436
  (9 other events, 7.4 us)

commit v4 on v3

--- a/solution.py
+++ b/solution.py
@@ -17,7 +17,7 @@
         in_specs=in_specs,
         out_specs=out_specs,
         scratch_shapes=scratch,
-        compiler_params=pltpu.CompilerParams(vmem_limit_bytes=60 * 1024 * 1024),
+        compiler_params=pltpu.CompilerParams(vmem_limit_bytes=57 * 1024 * 1024),
         **kw,
     )
 

time: 167 us -> 166 us (level)
  the two profiles are of different devices: /device:TPU:0 before, /device:TPU:9 now
where the time goes in v4:
time: 166 us; the launch traced here: 167 us
  Pallas kernels  69.6 us (42%)
  waiting for transfers between devices  53.7 us (32%)
  starting transfers between devices  34.7 us (21%)
  local copies, waits for them, and re-layouts  5.3 us (3%)
  other arithmetic  2.07 us (1%)
    pallas_call x4, Pallas kernels, forward(): call(functools.partial(forward_kernel, count, cap, light, split), outs, [...  31.6 us
    pallas_call x4, Pallas kernels, backward(): call(functools.partial(backward_kernel, parts, split, cap, light), outs,...  23.9 us
    ppermute x2, waiting for transfers between devices, light_branch(): return [[lax.ppermute(x, 'expert', p), u] for p, u in zip(perms, unused)]  22.2 us
    ppermute x12, waiting for transfers between devices, to_index(): return lax.ppermute(x, 'expert', [(i, i ^ k) for i in range(count)])  20.3 us
    ppermute x12, starting transfers between devices, to_index(): return lax.ppermute(x, 'expert', [(i, i ^ k) for i in range(count)])  16.1 us
    pallas_call x1, Pallas kernels, weight_grads(): call(functools.partial(weights_kernel, count, cap, light, layout, heavy_f...  10.2 us
    ppermute x8, starting transfers between devices, swapped(): return lax.ppermute(x, 'inner', swap)  7.6 us
    ppermute x2, starting transfers between devices, light_branch(): return [[lax.ppermute(x, 'expert', p), u] for p, u in zip(perms, unused)]  4.91 us
  transfers between devices with their start and end apart: 30, of which 13 were waited for; matrix products, arithmetic and copies ran while one was open for 2% of the time, Pallas kernels for 37%

profile of v4, /device:TPU:9, one launch (start us, length us, event | category | flops | bytes accessed | tf_op | source)
XLA Modules:
  0.0 166.9 jit_solution(7337978861079894959)
XLA Ops:
  0.6 1.9 %shard_map.138 = (bf16[272,1024]{1,0:T(8,128)(2,1)}, s32[1]{0:T(128)}) custom-call(s32[4]{0:T(128)} %shadow.11, bf16[128,1024]{1,0:T(8,128)(2,1)} %tok_ref.1, bf16[128,1024]{1,0:T(8,128)(2,1)} %grad_ref.1, s32[2,128]{1,0:T(2,128)} %bitcast.3, f32[2,128]{1,0:T(2,128)} %bitcast.4), custom_call_target="tpu_custom_call" | custom-call | tf_op jit(solution)/shard_map/pallas_call | solution.py:573
  2.5 0.7 collective-permute-start.36
  3.3 1.8 %collective-permute-done.36.sib = bf16[272,1024]{1,0:T(8,128)(2,1)S(1)} collective-permute-done((bf16[272,1024]{1,0:T(8,128)(2,1)}, bf16[272,1024]{1,0:T(8,128)(2,1)S(1)}, u32[]{:S(2)}, u32[]{:S(2)}) %collective-permute-start.36) | collective-permute-done | bytes 557088 | tf_op jit(solution)/shard_map/ppermute | solution.py:475
  5.9 8.0 %shard_map.139 = (f32[8,128]{1,0:T(8,128)}, bf16[480,1024]{1,0:T(8,128)(2,1)}, bf16[480,1024]{1,0:T(8,128)(2,1)}, bf16[288,256]{1,0:T(8,128)(2,1)}, bf16[192,1536]{1,0:T(8,128)(2,1)}, /*index=5*/bf16[96,1536]{1,0:T(8,128)(2,1)}) custom-call(s32[4]{0:T(128)} %shadow.11, f32[8,128]{1,0:T(8,128)} %broadcast_in_dim.3.load_in, ...), custom_call_target="tpu_custom_call" | custom-call | tf_op jit(solution)/shard_map/pallas_call | solution.py:485
  13.9 1.3 collective-permute-start.39
  15.4 2.3 %collective-permute-done.38.own = bf16[272,1024]{1,0:T(8,128)(2,1)S(1)} collective-permute-done((bf16[272,1024]{1,0:T(8,128)(2,1)}, bf16[272,1024]{1,0:T(8,128)(2,1)S(1)}, u32[]{:S(2)}, u32[]{:S(2)}) %collective-permute-start.38) | collective-permute-done | bytes 557088 | tf_op jit(solution)/shard_map/ppermute | solution.py:472
  17.7 4.6 %collective-permute-done.39.refs_3_ = bf16[96,1536]{1,0:T(8,128)(2,1)S(1)} collective-permute-done((bf16[96,1536]{1,0:T(8,128)(2,1)}, bf16[96,1536]{1,0:T(8,128)(2,1)S(1)}, u32[]{:S(2)}, u32[]{:S(2)}) %collective-permute-start.39) | collective-permute-done | bytes 294944 | tf_op jit(solution)/shard_map/ppermute | solution.py:611
  22.4 2.0 %collective-permute-start.40 = (bf16[272,1024]{1,0:T(8,128)(2,1)S(1)}, bf16[272,1024]{1,0:T(8,128)(2,1)S(1)}, u32[]{:S(2)}, u32[]{:S(2)}) collective-permute-start(bf16[272,1024]{1,0:T(8,128)(2,1)S(1)} %collective-permute-done.38.own), channel_id=1, source_target_pairs={{0,1},{1,0},{2,3},{3,2},{4,5},{5,4},{6,7},{7,6},{8,9},{9,8},{10,11... | collective-permute-start | bytes 1671176 | tf_op jit(solution)/shard_map/ppermute | solution.py:475
  24.4 2.3 %collective-permute-start.43 = (bf16[272,1024]{1,0:T(8,128)(2,1)S(1)}, bf16[272,1024]{1,0:T(8,128)(2,1)S(1)}, u32[]{:S(2)}, u32[]{:S(2)}) collective-permute-start(bf16[272,1024]{1,0:T(8,128)(2,1)S(1)} %copy-done.7), channel_id=1, source_target_pairs={{0,8},{4,12},{8,0},{12,4},{1,9},{5,13},{9,1},{13,5},{2,10},{6,14},... | collective-permute-start | bytes 1671176 | tf_op jit(solution)/shard_map/ppermute | solution.py:472
  26.7 0.8 copy-done.11
  27.5 7.8 %shard_map.140 = (f32[8,128]{1,0:T(8,128)}, bf16[480,1024]{1,0:T(8,128)(2,1)}, bf16[480,1024]{1,0:T(8,128)(2,1)}, bf16[288,256]{1,0:T(8,128)(2,1)}, bf16[192,1536]{1,0:T(8,128)(2,1)}, /*index=5*/bf16[96,1536]{1,0:T(8,128)(2,1)}) custom-call(s32[4]{0:T(128)} %shadow.11, f32[8,128]{1,0:T(8,128)} %get-tuple-element.180.load_in, bf16[272,1024]{1,0:T(8,128)(2,1)} %copy-done.8, ...), custom_call_target="tpu_custom_call" | custom-call | tf_op jit(solution)/shard_map/pallas_call | solution.py:485
  35.4 1.3 collective-permute-start.44
  36.9 6.0 %shard_map.141 = (bf16[192,1536]{1,0:T(8,128)(2,1)}, bf16[64,1536]{1,0:T(8,128)(2,1)}, bf16[32,1536]{1,0:T(8,128)(2,1)S(1)}, bf16[128,1024]{1,0:T(8,128)(2,1)}, bf16[128,1024]{1,0:T(8,128)(2,1)}) custom-call(bf16[192,1536]{1,0:T(8,128)(2,1)} %get-tuple-element.178.refs_0_, bf16[96,1536]{1,0:T(8,128)(2,1)} %get-tuple-element.179.refs_1_, ...), custom_call_target="tpu_custom_call" | custom-call | tf_op jit(solution)/shard_map/pallas_call | solution.py:516
  42.9 8.0 %collective-permute-done.43.own = bf16[272,1024]{1,0:T(8,128)(2,1)S(1)} collective-permute-done((bf16[272,1024]{1,0:T(8,128)(2,1)S(1)}, bf16[272,1024]{1,0:T(8,128)(2,1)S(1)}, u32[]{:S(2)}, u32[]{:S(2)}) %collective-permute-start.43) | collective-permute-done | bytes 557088 | tf_op jit(solution)/shard_map/ppermute | solution.py:472
  51.4 1.1 collective-permute-start.49
  53.0 0.8 copy-done.12
  53.7 7.9 %shard_map.142 = (f32[8,128]{1,0:T(8,128)}, bf16[480,1024]{1,0:T(8,128)(2,1)}, bf16[480,1024]{1,0:T(8,128)(2,1)}, bf16[288,256]{1,0:T(8,128)(2,1)}, bf16[192,1536]{1,0:T(8,128)(2,1)}, /*index=5*/bf16[96,1536]{1,0:T(8,128)(2,1)}) custom-call(s32[4]{0:T(128)} %shadow.11, f32[8,128]{1,0:T(8,128)} %get-tuple-element.190.load_in, bf16[272,1024]{1,0:T(8,128)(2,1)} %copy-done.5, ...), custom_call_target="tpu_custom_call" | custom-call | tf_op jit(solution)/shard_map/pallas_call | solution.py:485
  61.7 1.3 collective-permute-start.50
  63.0 3.1 %collective-permute-start.52 = (bf16[64,1536]{1,0:T(8,128)(2,1)S(1)}, bf16[64,1536]{1,0:T(8,128)(2,1)S(1)}, u32[]{:S(2)}, u32[]{:S(2)}) collective-permute-start(bf16[64,1536]{1,0:T(8,128)(2,1)S(1)} %copy-done.29), channel_id=1, source_target_pairs={{0,8},{4,12},{8,0},{12,4},{1,9},{5,13},{9,1},{13,5},{2,10},{6,14},... | collective-permute-start | bytes 589832 | tf_op jit(solution)/shard_map/ppermute | solution.py:472
  66.2 5.9 %shard_map.143 = (bf16[192,1536]{1,0:T(8,128)(2,1)}, bf16[64,1536]{1,0:T(8,128)(2,1)}, bf16[32,1536]{1,0:T(8,128)(2,1)S(1)}, bf16[128,1024]{1,0:T(8,128)(2,1)}, bf16[128,1024]{1,0:T(8,128)(2,1)}) custom-call(bf16[192,1536]{1,0:T(8,128)(2,1)} %get-tuple-element.184.refs_0_, bf16[96,1536]{1,0:T(8,128)(2,1)} %get-tuple-element.189.refs_1_, ...), custom_call_target="tpu_custom_call" | custom-call | tf_op jit(solution)/shard_map/pallas_call | solution.py:516
  72.1 2.5 %collective-permute-done.52.refs_13_ = bf16[64,1536]{1,0:T(8,128)(2,1)S(1)} collective-permute-done((bf16[64,1536]{1,0:T(8,128)(2,1)S(1)}, bf16[64,1536]{1,0:T(8,128)(2,1)S(1)}, u32[]{:S(2)}, u32[]{:S(2)}) %collective-permute-start.52) | collective-permute-done | bytes 196640 | tf_op jit(solution)/shard_map/ppermute | solution.py:472
  74.7 1.6 collective-permute-start.53
  76.9 0.8 collective-permute-start.54
  77.6 2.1 %collective-permute-start.56 = (bf16[64,1536]{1,0:T(8,128)(2,1)}, bf16[64,1536]{1,0:T(8,128)(2,1)S(1)}, u32[]{:S(2)}, u32[]{:S(2)}) collective-permute-start(bf16[64,1536]{1,0:T(8,128)(2,1)} %get-tuple-element.208), channel_id=1, source_target_pairs={{0,8},{4,12},{8,0},{12,4},{1,9},{5,13},{9,1},{13,5},{2,10},{6,14},... | collective-permute-start | bytes 589832 | tf_op jit(solution)/shard_map/ppermute | solution.py:472
  79.7 1.4 collective-permute-start.55
  81.2 7.8 %shard_map.144 = (f32[8,128]{1,0:T(8,128)}, bf16[480,1024]{1,0:T(8,128)(2,1)}, bf16[480,1024]{1,0:T(8,128)(2,1)}, bf16[288,256]{1,0:T(8,128)(2,1)}, bf16[288,1536]{1,0:T(8,128)(2,1)}) custom-call(s32[4]{0:T(128)} %shadow.11, f32[8,128]{1,0:T(8,128)} %get-tuple-element.202.load_in, bf16[272,1024]{1,0:T(8,128)(2,1)} %copy-done.6, bf16[272,1024]{1,0:T(8,128)(2,1)} %copy-done.9, ...), custom_call_target="tpu_custom_call" | custom-call | tf_op jit(solution)/shard_map/pallas_call | solution.py:485
  89.0 2.2 %collective-permute-done.48.refs_2_ = bf16[192,1536]{1,0:T(8,128)(2,1)S(1)} collective-permute-done((bf16[192,1536]{1,0:T(8,128)(2,1)S(1)}, bf16[192,1536]{1,0:T(8,128)(2,1)S(1)}, u32[]{:S(2)}, u32[]{:S(2)}) %collective-permute-start.48) | collective-permute-done | bytes 589856 | tf_op jit(solution)/shard_map/ppermute | solution.py:627
  92.0 5.9 %shard_map.145 = (bf16[192,1536]{1,0:T(8,128)(2,1)}, bf16[64,1536]{1,0:T(8,128)(2,1)}, bf16[32,1536]{1,0:T(8,128)(2,1)S(1)}, bf16[128,1024]{1,0:T(8,128)(2,1)}, bf16[128,1024]{1,0:T(8,128)(2,1)}) custom-call(bf16[192,1536]{1,0:T(8,128)(2,1)} %get-tuple-element.196.refs_0_, bf16[96,1536]{1,0:T(8,128)(2,1)} %get-tuple-element.201.refs_1_, ...), custom_call_target="tpu_custom_call" | custom-call | tf_op jit(solution)/shard_map/pallas_call | solution.py:516
  97.9 0.9 collective-permute-start.57
  98.9 0.7 collective-permute-start.47
  100.2 1.0 add_convert_fusion.2
  101.2 2.8 %collective-permute-start.58 = (bf16[128,1024]{1,0:T(8,128)(2,1)S(1)}, bf16[128,1024]{1,0:T(8,128)(2,1)S(1)}, u32[]{:S(2)}, u32[]{:S(2)}) collective-permute-start(bf16[128,1024]{1,0:T(8,128)(2,1)S(1)} %add_convert_fusion.2), channel_id=1, source_target_pairs={{0,8},{4,12},{8,0},{12,4},{1,9},{5,13},{9,1},{13,5},{2,10},{6,14},... | collective-permute-start | bytes 786440 | tf_op jit(solution)/shard_map/ppermute | solution.py:472
  104.3 1.2 collective-permute-start.60
  105.5 1.5 collective-permute-done.60.other
  107.6 2.0 %shard_map.146.which = s32[1]{0:T(128)} custom-call(s32[1]{0:T(128)} %get-tuple-element.213.which, f32[8,128]{1,0:T(8,128)} %get-tuple-element.214.load, f32[8,128]{1,0:T(8,128)} %copy-done.27), custom_call_target="tpu_custom_call" | custom-call | tf_op jit(solution)/shard_map/pallas_call | solution.py:637
  109.6 7.1 %collective-permute-done.61.refs_17_ = bf16[64,1536]{1,0:T(8,128)(2,1)S(1)} collective-permute-done((bf16[64,1536]{1,0:T(8,128)(2,1)S(1)}, bf16[64,1536]{1,0:T(8,128)(2,1)S(1)}, u32[]{:S(2)}, u32[]{:S(2)}) %collective-permute-start.61) | collective-permute-done | bytes 196640 | tf_op jit(solution)/shard_map/ppermute | solution.py:472
  116.8 0.9 copy-done
  117.7 6.1 %shard_map.147 = (bf16[192,1536]{1,0:T(8,128)(2,1)}, bf16[64,1536]{1,0:T(8,128)(2,1)}, bf16[32,1536]{1,0:T(8,128)(2,1)S(1)}, bf16[128,1024]{1,0:T(8,128)(2,1)}, bf16[128,1024]{1,0:T(8,128)(2,1)}) custom-call(bf16[288,1536]{1,0:T(8,128)(2,1)} %get-tuple-element.207.refs_0_, bf16[288,1536]{1,0:T(8,128)(2,1)} %copy-done, ...), custom_call_target="tpu_custom_call" | custom-call | tf_op jit(solution)/shard_map/pallas_call | solution.py:516
  123.8 0.9 collective-permute-start.62
  125.3 0.9 constant_dynamic-update-slice_fusion.24
  126.3 27.2 %conditional.1 = (bf16[128,1536]{1,0:T(8,128)(2,1)}, bf16[128,1536]{1,0:T(8,128)(2,1)}, bf16[128,1536]{1,0:T(8,128)(2,1)}, bf16[128,1536]{1,0:T(8,128)(2,1)}) conditional(s32[]{:T(128)} %bitcast.2, bf16[128,1536]{1,0:T(8,128)(2,1)S(1)} %constant_dynamic-update-slice_fusion.24, ...), branch_computations={%region_0.0_spmd, %region_1.0_spmd, %region_2.0_spmd, %region_3.0_... | conditional | bytes 7078080 | solution.py:662
  126.3 3.6 %collective-permute-start.9 = (bf16[128,1536]{1,0:T(8,128)(2,1)S(1)}, bf16[128,1536]{1,0:T(8,128)(2,1)}, u32[]{:S(2)}, u32[]{:S(2)}) collective-permute-start(bf16[128,1536]{1,0:T(8,128)(2,1)S(1)} %param.4), channel_id=1, source_target_pairs={{4,8},{8,4},{5,9},{9,5},{6,10},{10,6},{7,11},{11,7},{20,24},{24,20... | collective-permute-start | bytes 1179656 | tf_op jit(solution)/shard_map/cond/branch_4_fun/ppermute | solution.py:656
  130.0 1.3 collective-permute-start.8
  131.3 22.2 %collective-permute-done.9 = bf16[128,1536]{1,0:T(8,128)(2,1)} collective-permute-done((bf16[128,1536]{1,0:T(8,128)(2,1)S(1)}, bf16[128,1536]{1,0:T(8,128)(2,1)}, u32[]{:S(2)}, u32[]{:S(2)}) %collective-permute-start.9) | collective-permute-done | bytes 393248 | tf_op jit(solution)/shard_map/cond/branch_4_fun/ppermute | solution.py:656
  153.5 0.7 collective-permute-start.41
  154.3 1.5 collective-permute-start.63
  155.8 10.2 %shard_map.148 = (bf16[2,1024,512]{2,1,0:T(8,128)(2,1)}, bf16[2,1024,512]{2,1,0:T(8,128)(2,1)}, bf16[2,512,1024]{2,1,0:T(8,128)(2,1)}) custom-call(s32[4]{0:T(128)} %shadow.11, s32[1]{0:T(128)} %shard_map.146.which, bf16[480,1024]{1,0:T(8,128)(2,1)} %get-tuple-element.219.refs_0_, bf16[480,1024]{1,0:T(8,128)(2,1)} %get-tuple-element.220.refs_1_, ...), custom_call_target="tpu_custom_call" | custom-call | tf_op jit(solution)/shard_map/pallas_call | solution.py:558
  166.0 0.9 add_convert_fusion
  (92 shorter events, 5.4 us)
Async XLA Ops:
  2.5 2.5 %collective-permute-start.36 = (bf16[272,1024]{1,0:T(8,128)(2,1)}, bf16[272,1024]{1,0:T(8,128)(2,1)S(1)}, u32[]{:S(2)}, u32[]{:S(2)}) collective-permute-start(bf16[272,1024]{1,0:T(8,128)(2,1)} %get-tuple-element.191.own), channel_id=1, source_target_pairs={{0,1},{1,0},{2,3},{3,2},{4,5},{5,4},{6,7},{7,6},{8,9},{9,8},{10,11... | collective-permute-start | bytes 1671176 | tf_op jit(solution)/shard_map/ppermute | solution.py:475
  3.3 14.4 %collective-permute-start.38 = (bf16[272,1024]{1,0:T(8,128)(2,1)}, bf16[272,1024]{1,0:T(8,128)(2,1)S(1)}, u32[]{:S(2)}, u32[]{:S(2)}) collective-permute-start(bf16[272,1024]{1,0:T(8,128)(2,1)} %get-tuple-element.191.own), channel_id=1, source_target_pairs={{0,4},{4,0},{8,12},{12,8},{1,5},{5,1},{9,13},{13,9},{2,6},{6,2},{1... | collective-permute-start | bytes 1671176 | tf_op jit(solution)/shard_map/ppermute | solution.py:472
  5.9 18.5 %copy-start.7 = (bf16[272,1024]{1,0:T(8,128)(2,1)S(1)}, bf16[272,1024]{1,0:T(8,128)(2,1)}, u32[]{:S(2)}) copy-start(bf16[272,1024]{1,0:T(8,128)(2,1)} %get-tuple-element.191.own) | copy-start | bytes 1671172
  13.9 8.5 %collective-permute-start.39 = (bf16[96,1536]{1,0:T(8,128)(2,1)}, bf16[96,1536]{1,0:T(8,128)(2,1)S(1)}, u32[]{:S(2)}, u32[]{:S(2)}) collective-permute-start(bf16[96,1536]{1,0:T(8,128)(2,1)} %get-tuple-element.179.refs_1_), channel_id=1, source_target_pairs={{0,2},{2,0},{1,3},{3,1},{4,6},{6,4},{5,7},{7,5},{8,10},{10,8},{9,1... | collective-permute-start | bytes 884744 | tf_op jit(solution)/shard_map/ppermute | solution.py:611
  15.1 20.2 %collective-permute-start.37 = (bf16[192,1536]{1,0:T(8,128)(2,1)}, bf16[192,1536]{1,0:T(8,128)(2,1)S(1)}, u32[]{:S(2)}, u32[]{:S(2)}) collective-permute-start(bf16[192,1536]{1,0:T(8,128)(2,1)} %get-tuple-element.178.refs_0_), channel_id=1, source_target_pairs={{0,2},{2,0},{1,3},{3,1},{4,6},{6,4},{5,7},{7,5},{8,10},{10,8},{9,1... | collective-permute-start | bytes 1769480 | tf_op jit(solution)/shard_map/ppermute | solution.py:612
  17.7 9.0 %copy-start.8 = (bf16[272,1024]{1,0:T(8,128)(2,1)}, bf16[272,1024]{1,0:T(8,128)(2,1)S(1)}, u32[]{:S(2)}) copy-start(bf16[272,1024]{1,0:T(8,128)(2,1)S(1)} %collective-permute-done.38.own) | copy-start | bytes 1671172
  22.3 14.5 %copy-start.15 = (bf16[96,1536]{1,0:T(8,128)(2,1)}, bf16[96,1536]{1,0:T(8,128)(2,1)S(1)}, u32[]{:S(2)}) copy-start(bf16[96,1536]{1,0:T(8,128)(2,1)S(1)} %collective-permute-done.39.refs_3_) | copy-start | bytes 884740
  22.4 4.3 %collective-permute-start.40 = (bf16[272,1024]{1,0:T(8,128)(2,1)S(1)}, bf16[272,1024]{1,0:T(8,128)(2,1)S(1)}, u32[]{:S(2)}, u32[]{:S(2)}) collective-permute-start(bf16[272,1024]{1,0:T(8,128)(2,1)S(1)} %collective-permute-done.38.own), channel_id=1, source_target_pairs={{0,1},{1,0},{2,3},{3,2},{4,5},{5,4},{6,7},{7,6},{8,9},{9,8},{10,11... | collective-permute-start | bytes 1671176 | tf_op jit(solution)/shard_map/ppermute | solution.py:475
  24.4 26.5 %collective-permute-start.43 = (bf16[272,1024]{1,0:T(8,128)(2,1)S(1)}, bf16[272,1024]{1,0:T(8,128)(2,1)S(1)}, u32[]{:S(2)}, u32[]{:S(2)}) collective-permute-start(bf16[272,1024]{1,0:T(8,128)(2,1)S(1)} %copy-done.7), channel_id=1, source_target_pairs={{0,8},{4,12},{8,0},{12,4},{1,9},{5,13},{9,1},{13,5},{2,10},{6,14},... | collective-permute-start | bytes 1671176 | tf_op jit(solution)/shard_map/ppermute | solution.py:472
  35.4 15.5 %collective-permute-start.44 = (bf16[96,1536]{1,0:T(8,128)(2,1)}, bf16[96,1536]{1,0:T(8,128)(2,1)S(1)}, u32[]{:S(2)}, u32[]{:S(2)}) collective-permute-start(bf16[96,1536]{1,0:T(8,128)(2,1)} %get-tuple-element.189.refs_1_), channel_id=1, source_target_pairs={{0,2},{2,0},{1,3},{3,1},{4,6},{6,4},{5,7},{7,5},{8,10},{10,8},{9,1... | collective-permute-start | bytes 884744 | tf_op jit(solution)/shard_map/ppermute | solution.py:617
  36.7 25.0 %collective-permute-start.42 = (bf16[192,1536]{1,0:T(8,128)(2,1)}, bf16[192,1536]{1,0:T(8,128)(2,1)S(1)}, u32[]{:S(2)}, u32[]{:S(2)}) collective-permute-start(bf16[192,1536]{1,0:T(8,128)(2,1)} %get-tuple-element.184.refs_0_), channel_id=1, source_target_pairs={{0,2},{2,0},{1,3},{3,1},{4,6},{6,4},{5,7},{7,5},{8,10},{10,8},{9,1... | collective-permute-start | bytes 1769480 | tf_op jit(solution)/shard_map/ppermute | solution.py:618
  50.9 15.3 %copy-start.14 = (bf16[96,1536]{1,0:T(8,128)(2,1)}, bf16[96,1536]{1,0:T(8,128)(2,1)S(1)}, u32[]{:S(2)}) copy-start(bf16[96,1536]{1,0:T(8,128)(2,1)S(1)} %collective-permute-done.44.refs_3_) | copy-start | bytes 884740
  50.9 2.0 %collective-permute-start.45 = (bf16[272,1024]{1,0:T(8,128)(2,1)S(1)}, bf16[272,1024]{1,0:T(8,128)(2,1)S(1)}, u32[]{:S(2)}, u32[]{:S(2)}) collective-permute-start(bf16[272,1024]{1,0:T(8,128)(2,1)S(1)} %collective-permute-done.43.own), channel_id=1, source_target_pairs={{0,1},{1,0},{2,3},{3,2},{4,5},{5,4},{6,7},{7,6},{8,9},{9,8},{10,11... | collective-permute-start | bytes 1671176 | tf_op jit(solution)/shard_map/ppermute | solution.py:475
  51.4 23.3 %collective-permute-start.49 = (bf16[272,1024]{1,0:T(8,128)(2,1)S(1)}, bf16[272,1024]{1,0:T(8,128)(2,1)S(1)}, u32[]{:S(2)}, u32[]{:S(2)}) collective-permute-start(bf16[272,1024]{1,0:T(8,128)(2,1)S(1)} %collective-permute-done.43.own), channel_id=1, source_target_pairs={{0,4},{4,0},{8,12},{12,8},{1,5},{5,1},{9,13},{13,9},{2,6},{6,2},{1... | collective-permute-start | bytes 1671176 | tf_op jit(solution)/shard_map/ppermute | solution.py:472
  53.7 9.3 %copy-start.29 = (bf16[64,1536]{1,0:T(8,128)(2,1)S(1)}, bf16[64,1536]{1,0:T(8,128)(2,1)}, u32[]{:S(2)}) copy-start(bf16[64,1536]{1,0:T(8,128)(2,1)} %get-tuple-element.204) | copy-start | bytes 589828
  61.7 13.0 %collective-permute-start.50 = (bf16[96,1536]{1,0:T(8,128)(2,1)}, bf16[96,1536]{1,0:T(8,128)(2,1)S(1)}, u32[]{:S(2)}, u32[]{:S(2)}) collective-permute-start(bf16[96,1536]{1,0:T(8,128)(2,1)} %get-tuple-element.201.refs_1_), channel_id=1, source_target_pairs={{0,2},{2,0},{1,3},{3,1},{4,6},{6,4},{5,7},{7,5},{8,10},{10,8},{9,1... | collective-permute-start | bytes 884744 | tf_op jit(solution)/shard_map/ppermute | solution.py:626
  63.0 11.6 %collective-permute-start.52 = (bf16[64,1536]{1,0:T(8,128)(2,1)S(1)}, bf16[64,1536]{1,0:T(8,128)(2,1)S(1)}, u32[]{:S(2)}, u32[]{:S(2)}) collective-permute-start(bf16[64,1536]{1,0:T(8,128)(2,1)S(1)} %copy-done.29), channel_id=1, source_target_pairs={{0,8},{4,12},{8,0},{12,4},{1,9},{5,13},{9,1},{13,5},{2,10},{6,14},... | collective-permute-start | bytes 589832 | tf_op jit(solution)/shard_map/ppermute | solution.py:472
  66.2 8.5 %collective-permute-start.51 = (bf16[64,1536]{1,0:T(8,128)(2,1)S(1)}, bf16[64,1536]{1,0:T(8,128)(2,1)S(1)}, u32[]{:S(2)}, u32[]{:S(2)}) collective-permute-start(bf16[64,1536]{1,0:T(8,128)(2,1)S(1)} %copy-done.29), channel_id=1, source_target_pairs={{0,4},{4,0},{8,12},{12,8},{1,5},{5,1},{9,13},{13,9},{2,6},{6,2},{1... | collective-permute-start | bytes 589832 | tf_op jit(solution)/shard_map/ppermute | solution.py:472
  66.2 10.1 %copy-start.1 = (bf16[192,1536]{1,0:T(8,128)(2,1)S(1)}, bf16[192,1536]{1,0:T(8,128)(2,1)}, u32[]{:S(2)}) copy-start(bf16[192,1536]{1,0:T(8,128)(2,1)} %get-tuple-element.196.refs_0_) | copy-start | bytes 1769476
  74.6 23.2 %copy-start.20 = (bf16[64,1536]{1,0:T(8,128)(2,1)}, bf16[64,1536]{1,0:T(8,128)(2,1)S(1)}, u32[]{:S(2)}) copy-start(bf16[64,1536]{1,0:T(8,128)(2,1)S(1)} %collective-permute-done.52.refs_13_) | copy-start | bytes 589828
  74.7 23.2 %copy-start.21 = (bf16[64,1536]{1,0:T(8,128)(2,1)}, bf16[64,1536]{1,0:T(8,128)(2,1)S(1)}, u32[]{:S(2)}) copy-start(bf16[64,1536]{1,0:T(8,128)(2,1)S(1)} %collective-permute-done.51.refs_12_) | copy-start | bytes 589828
  74.7 17.0 %copy-start.13 = (bf16[96,1536]{1,0:T(8,128)(2,1)}, bf16[96,1536]{1,0:T(8,128)(2,1)S(1)}, u32[]{:S(2)}) copy-start(bf16[96,1536]{1,0:T(8,128)(2,1)S(1)} %collective-permute-done.50.refs_3_) | copy-start | bytes 884740
  74.7 5.0 %collective-permute-start.53 = (bf16[272,1024]{1,0:T(8,128)(2,1)S(1)}, bf16[272,1024]{1,0:T(8,128)(2,1)S(1)}, u32[]{:S(2)}, u32[]{:S(2)}) collective-permute-start(bf16[272,1024]{1,0:T(8,128)(2,1)S(1)} %collective-permute-done.49.own), channel_id=1, source_target_pairs={{0,1},{1,0},{2,3},{3,2},{4,5},{5,4},{6,7},{7,6},{8,9},{9,8},{10,11... | collective-permute-start | bytes 1671176 | tf_op jit(solution)/shard_map/ppermute | solution.py:475
  76.3 14.9 %collective-permute-start.48 = (bf16[192,1536]{1,0:T(8,128)(2,1)S(1)}, bf16[192,1536]{1,0:T(8,128)(2,1)S(1)}, u32[]{:S(2)}, u32[]{:S(2)}) collective-permute-start(bf16[192,1536]{1,0:T(8,128)(2,1)S(1)} %copy-done.1), channel_id=1, source_target_pairs={{0,2},{2,0},{1,3},{3,1},{4,6},{6,4},{5,7},{7,5},{8,10},{10,8},{9,1... | collective-permute-start | bytes 1769480 | tf_op jit(solution)/shard_map/ppermute | solution.py:627
  76.5 22.3 %collective-permute-start.46 = (bf16[128,1024]{1,0:T(8,128)(2,1)}, bf16[128,1024]{1,0:T(8,128)(2,1)S(1)}, u32[]{:S(2)}, u32[]{:S(2)}) collective-permute-start(bf16[128,1024]{1,0:T(8,128)(2,1)} %get-tuple-element.200), channel_id=1, source_target_pairs={{0,1},{1,0},{2,3},{3,2},{4,5},{5,4},{6,7},{7,6},{8,9},{9,8},{10,11... | collective-permute-start | bytes 786440 | tf_op jit(solution)/shard_map/ppermute | solution.py:475
  76.9 14.5 %collective-permute-start.54 = (bf16[64,1536]{1,0:T(8,128)(2,1)S(1)}, bf16[64,1536]{1,0:T(8,128)(2,1)S(1)}, u32[]{:S(2)}, u32[]{:S(2)}) collective-permute-start(bf16[64,1536]{1,0:T(8,128)(2,1)S(1)} %collective-permute-done.52.refs_13_), channel_id=1, source_target_pairs={{0,4},{4,0},{8,12},{12,8},{1,5},{5,1},{9,13},{13,9},{2,6},{6,2},{1... | collective-permute-start | bytes 589832 | tf_op jit(solution)/shard_map/ppermute | solution.py:472
  77.6 13.8 %collective-permute-start.56 = (bf16[64,1536]{1,0:T(8,128)(2,1)}, bf16[64,1536]{1,0:T(8,128)(2,1)S(1)}, u32[]{:S(2)}, u32[]{:S(2)}) collective-permute-start(bf16[64,1536]{1,0:T(8,128)(2,1)} %get-tuple-element.208), channel_id=1, source_target_pairs={{0,8},{4,12},{8,0},{12,4},{1,9},{5,13},{9,1},{13,5},{2,10},{6,14},... | collective-permute-start | bytes 589832 | tf_op jit(solution)/shard_map/ppermute | solution.py:472
  79.7 12.0 %collective-permute-start.55 = (bf16[64,1536]{1,0:T(8,128)(2,1)}, bf16[64,1536]{1,0:T(8,128)(2,1)S(1)}, u32[]{:S(2)}, u32[]{:S(2)}) collective-permute-start(bf16[64,1536]{1,0:T(8,128)(2,1)} %get-tuple-element.208), channel_id=1, source_target_pairs={{0,4},{4,0},{8,12},{12,8},{1,5},{5,1},{9,13},{13,9},{2,6},{6,2},{1... | collective-permute-start | bytes 589832 | tf_op jit(solution)/shard_map/ppermute | solution.py:472
  91.2 25.6 %collective-permute-start.59 = (bf16[288,1536]{1,0:T(8,128)(2,1)}, bf16[288,1536]{1,0:T(8,128)(2,1)S(1)}, u32[]{:S(2)}, u32[]{:S(2)}) collective-permute-start(bf16[288,1536]{1,0:T(8,128)(2,1)} %get-tuple-element.207.refs_0_), channel_id=1, source_target_pairs={{0,2},{2,0},{1,3},{3,1},{4,6},{6,4},{5,7},{7,5},{8,10},{10,8},{9,1... | collective-permute-start | bytes 2654216 | tf_op jit(solution)/shard_map/ppermute | solution.py:636
  91.4 6.5 %copy-start.22 = (bf16[64,1536]{1,0:T(8,128)(2,1)}, bf16[64,1536]{1,0:T(8,128)(2,1)S(1)}, u32[]{:S(2)}) copy-start(bf16[64,1536]{1,0:T(8,128)(2,1)S(1)} %collective-permute-done.54.refs_14_) | copy-start | bytes 589828
  91.4 12.6 %copy-start.23 = (bf16[64,1536]{1,0:T(8,128)(2,1)}, bf16[64,1536]{1,0:T(8,128)(2,1)S(1)}, u32[]{:S(2)}) copy-start(bf16[64,1536]{1,0:T(8,128)(2,1)S(1)} %collective-permute-done.56.refs_16_) | copy-start | bytes 589828
  92.0 6.8 %copy-start.17 = (bf16[128,1024]{1,0:T(8,128)(2,1)S(1)}, bf16[128,1024]{1,0:T(8,128)(2,1)}, u32[]{:S(2)}) copy-start(bf16[128,1024]{1,0:T(8,128)(2,1)} %get-tuple-element.199) | copy-start | bytes 786436
  92.0 12.3 %copy-start.26 = (f32[8,128]{1,0:T(8,128)S(1)}, f32[8,128]{1,0:T(8,128)}, u32[]{:S(2)}) copy-start(f32[8,128]{1,0:T(8,128)} %get-tuple-element.214.load) | copy-start | bytes 12292
  97.9 2.3 %collective-permute-start.57 = (bf16[128,1024]{1,0:T(8,128)(2,1)}, bf16[128,1024]{1,0:T(8,128)(2,1)S(1)}, u32[]{:S(2)}, u32[]{:S(2)}) collective-permute-start(bf16[128,1024]{1,0:T(8,128)(2,1)} %get-tuple-element.212), channel_id=1, source_target_pairs={{0,1},{1,0},{2,3},{3,2},{4,5},{5,4},{6,7},{7,6},{8,9},{9,8},{10,11... | collective-permute-start | bytes 786440 | tf_op jit(solution)/shard_map/ppermute | solution.py:475
  98.9 17.9 %collective-permute-start.47 = (bf16[128,1024]{1,0:T(8,128)(2,1)S(1)}, bf16[128,1024]{1,0:T(8,128)(2,1)S(1)}, u32[]{:S(2)}, u32[]{:S(2)}) collective-permute-start(bf16[128,1024]{1,0:T(8,128)(2,1)S(1)} %add_convert_fusion.3), channel_id=1, source_target_pairs={{0,4},{4,0},{8,12},{12,8},{1,5},{5,1},{9,13},{13,9},{2,6},{6,2},{1... | collective-permute-start | bytes 786440 | tf_op jit(solution)/shard_map/ppermute | solution.py:472
  101.2 15.5 %collective-permute-start.58 = (bf16[128,1024]{1,0:T(8,128)(2,1)S(1)}, bf16[128,1024]{1,0:T(8,128)(2,1)S(1)}, u32[]{:S(2)}, u32[]{:S(2)}) collective-permute-start(bf16[128,1024]{1,0:T(8,128)(2,1)S(1)} %add_convert_fusion.2), channel_id=1, source_target_pairs={{0,8},{4,12},{8,0},{12,4},{1,9},{5,13},{9,1},{13,5},{2,10},{6,14},... | collective-permute-start | bytes 786440 | tf_op jit(solution)/shard_map/ppermute | solution.py:472
  104.0 12.7 %collective-permute-start.61 = (bf16[64,1536]{1,0:T(8,128)(2,1)S(1)}, bf16[64,1536]{1,0:T(8,128)(2,1)S(1)}, u32[]{:S(2)}, u32[]{:S(2)}) collective-permute-start(bf16[64,1536]{1,0:T(8,128)(2,1)S(1)} %collective-permute-done.56.refs_16_), channel_id=1, source_target_pairs={{0,4},{4,0},{8,12},{12,8},{1,5},{5,1},{9,13},{13,9},{2,6},{6,2},{1... | collective-permute-start | bytes 589832 | tf_op jit(solution)/shard_map/ppermute | solution.py:472
  104.3 2.8 %collective-permute-start.60 = (f32[8,128]{1,0:T(8,128)S(1)}, f32[8,128]{1,0:T(8,128)S(1)}, u32[]{:S(2)}, u32[]{:S(2)}) collective-permute-start(f32[8,128]{1,0:T(8,128)S(1)} %copy-done.26), channel_id=1, source_target_pairs={{0,16},{16,0},{1,17},{17,1},{2,18},{18,2},{3,19},{19,3},{4,20},{20... | collective-permute-start | bytes 12296 | tf_op jit(solution)/shard_map/ppermute | solution.py:643
  116.8 9.5 %copy-start.25 = (bf16[64,1536]{1,0:T(8,128)(2,1)}, bf16[64,1536]{1,0:T(8,128)(2,1)S(1)}, u32[]{:S(2)}) copy-start(bf16[64,1536]{1,0:T(8,128)(2,1)S(1)} %collective-permute-done.61.refs_17_) | copy-start | bytes 589828
  117.7 7.0 %copy-start.19 = (bf16[64,1536]{1,0:T(8,128)(2,1)S(1)}, bf16[64,1536]{1,0:T(8,128)(2,1)}, u32[]{:S(2)}) copy-start(bf16[64,1536]{1,0:T(8,128)(2,1)} %get-tuple-element.229) | copy-start | bytes 589828
  123.8 30.3 %collective-permute-start.62 = (bf16[128,1024]{1,0:T(8,128)(2,1)}, bf16[128,1024]{1,0:T(8,128)(2,1)S(1)}, u32[]{:S(2)}, u32[]{:S(2)}) collective-permute-start(bf16[128,1024]{1,0:T(8,128)(2,1)} %get-tuple-element.218), channel_id=1, source_target_pairs={{0,1},{1,0},{2,3},{3,2},{4,5},{5,4},{6,7},{7,6},{8,9},{9,8},{10,11... | collective-permute-start | bytes 786440 | tf_op jit(solution)/shard_map/ppermute | solution.py:475
  126.3 27.2 %copy-start.28 = (bf16[128,1024]{1,0:T(8,128)(2,1)S(1)}, bf16[128,1024]{1,0:T(8,128)(2,1)}, u32[]{:S(2)}) copy-start(bf16[128,1024]{1,0:T(8,128)(2,1)} %get-tuple-element.188) | copy-start | bytes 786436
  126.3 27.9 %copy-start.16 = (bf16[128,1024]{1,0:T(8,128)(2,1)S(1)}, bf16[128,1024]{1,0:T(8,128)(2,1)}, u32[]{:S(2)}) copy-start(bf16[128,1024]{1,0:T(8,128)(2,1)} %get-tuple-element.217) | copy-start | bytes 786436
  126.3 27.2 %collective-permute-start.9 = (bf16[128,1536]{1,0:T(8,128)(2,1)S(1)}, bf16[128,1536]{1,0:T(8,128)(2,1)}, u32[]{:S(2)}, u32[]{:S(2)}) collective-permute-start(bf16[128,1536]{1,0:T(8,128)(2,1)S(1)} %param.4), channel_id=1, source_target_pairs={{4,8},{8,4},{5,9},{9,5},{6,10},{10,6},{7,11},{11,7},{20,24},{24,20... | collective-permute-start | bytes 1179656 | tf_op jit(solution)/shard_map/cond/branch_4_fun/ppermute | solution.py:656
  130.0 23.5 %collective-permute-start.8 = (bf16[128,1536]{1,0:T(8,128)(2,1)S(1)}, bf16[128,1536]{1,0:T(8,128)(2,1)}, u32[]{:S(2)}, u32[]{:S(2)}) collective-permute-start(bf16[128,1536]{1,0:T(8,128)(2,1)S(1)} %param.4), channel_id=1, source_target_pairs={{0,8},{12,4},{1,9},{13,5},{2,10},{14,6},{3,11},{15,7},{16,24},{28,... | collective-permute-start | bytes 1179656 | tf_op jit(solution)/shard_map/cond/branch_4_fun/ppermute | solution.py:656
  153.5 12.5 %collective-permute-start.41 = (bf16[128,1024]{1,0:T(8,128)(2,1)S(1)}, bf16[128,1024]{1,0:T(8,128)(2,1)S(1)}, u32[]{:S(2)}, u32[]{:S(2)}) collective-permute-start(bf16[128,1024]{1,0:T(8,128)(2,1)S(1)} %copy-done.28), channel_id=1, source_target_pairs={{0,1},{1,0},{2,3},{3,2},{4,5},{5,4},{6,7},{7,6},{8,9},{9,8},{10,11... | collective-permute-start | bytes 786440 | tf_op jit(solution)/shard_map/ppermute | solution.py:475
  154.3 11.7 %collective-permute-start.63 = (bf16[128,1024]{1,0:T(8,128)(2,1)S(1)}, bf16[128,1024]{1,0:T(8,128)(2,1)S(1)}, u32[]{:S(2)}, u32[]{:S(2)}) collective-permute-start(bf16[128,1024]{1,0:T(8,128)(2,1)S(1)} %add_convert_fusion.1), channel_id=1, source_target_pairs={{0,12},{4,8},{8,4},{12,0},{1,13},{5,9},{9,5},{13,1},{2,14},{6,10},... | collective-permute-start | bytes 786440 | tf_op jit(solution)/shard_map/ppermute | solution.py:472
  155.8 10.2 %copy-start.18 = (bf16[128,1024]{1,0:T(8,128)(2,1)S(1)}, bf16[128,1024]{1,0:T(8,128)(2,1)}, u32[]{:S(2)}) copy-start(bf16[128,1024]{1,0:T(8,128)(2,1)} %get-tuple-element.187) | copy-start | bytes 786436
  (12 other events, 27.0 us)
